TPU v7x, 32 devices: a whole 2x2x4 slice. The times are simulated.
32 devices in a mesh: groups: 2 (over y), replica: 16 (over z, x, core).
Axes of the slice: x: 2, y: 2, z: 4, core: 2. Of those that a mesh axis runs over, the one named last changes fastest.
Arguments:
- first_activations: bfloat16 [4096, 4096], P(('groups', 'replica')), parts along dimension 0, may hold values from -6 to 6
- second_activations: bfloat16 [4096, 4096], P(('groups', 'replica')), parts along dimension 0, may hold values from -6 to 6
- first_adapter_ids: int32 [4096], P(('groups', 'replica')), parts along dimension 0, may hold values from 0 to 63, as said below
- second_adapter_ids: int32 [4096], P(('groups', 'replica')), parts along dimension 0, may hold values from 0 to 63, as said below
- valid_row_counts: int32 [2, 32], P(None, ('groups', 'replica')), parts along dimension 1, may hold values from 64 to 128, as said below
- popular_adapters: int32 [16], P('groups'), parts along dimension 0, may hold values from 0 to 63, as said below
- replica_hosting: int32 [32], P(('groups', 'replica')), parts along dimension 0, may hold values from 0 to 7
- value_weight_base: bfloat16 [4096, 512], replicated, may hold values from -0.09375 to 0.09375
- adapter_down_factors: bfloat16 [64, 4096, 64], P('replica'), may hold values from -0.09375 to 0.09375
- adapter_up_factors: bfloat16 [64, 64, 512], P('replica'), may hold values from -0.75 to 0.75
Outputs:
- first_output: bfloat16 [4096, 512], P(('groups', 'replica')), parts along dimension 0
- second_output: bfloat16 [4096, 512], P(('groups', 'replica')), parts along dimension 0
- resident_down: bfloat16 [32, 4096, 64], P(('groups', 'replica')), parts along dimension 0
- resident_up: bfloat16 [32, 64, 512], P(('groups', 'replica')), parts along dimension 0
There are 2 independent parts, one for each index of `groups`. A program takes and returns all parts, laid end to end along the dimension named above; an argument that names none is the same for every part. Nothing has to cross between parts.
Inputs may be any that keep to these rules, and one draw needn't show every extreme that they name: `first_adapter_ids`: adapter a is homed on replica a // 4. Among the 128 rows of one replica at most 12 name adapters homed on one replica, and in every draw some replica receives exactly 12 from every replica. `second_adapter_ids`: same law as first_adapter_ids, drawn afresh. `valid_row_counts`: in each micro-batch some replica has all 128 rows valid. `popular_adapters`: 8 distinct adapters, homed on distinct replicas.
All inputs are finite; a program needn't handle non-finite values.
Results may differ from a plain program's by a relative error of at most 0.0052.
Values may be sent and summed in bfloat16 or wider, within the bound.
No kernel may reach another device: no remote copies, remote signals or barrier semaphores. Data moves between devices by JAX's collectives and lax.ppermute only.
A program may use at most 64 MiB of HBM per device.

v0:
```python
import jax
import jax.numpy as jnp
from jax import lax
from jax.sharding import PartitionSpec as P


def from_root(block, axis, owner):
    block = jnp.where(lax.axis_index(axis) == owner, block, jnp.zeros_like(block))
    return lax.psum(block, axis)


def masked_term(block_rows, slot_ids, down_joined, up_joined, factor_rank):
    projected = jnp.dot(block_rows, down_joined, preferred_element_type=jnp.float32)
    column_slot = lax.broadcasted_iota(jnp.int32, (1, down_joined.shape[1]), 1) // factor_rank
    keeping = column_slot == slot_ids[:, None]
    projected = jnp.where(keeping, projected, 0.0).astype(jnp.bfloat16)
    return jnp.dot(projected, up_joined, preferred_element_type=jnp.float32).astype(jnp.bfloat16)


def local(
    first_activations,
    second_activations,
    first_adapter_ids,
    second_adapter_ids,
    valid_row_counts,
    popular_adapters,
    replica_hosting,
    value_weight_base,
    adapter_down_factors,
    adapter_up_factors,
):
    tok_rows = first_activations.shape[0]
    peers = lax.axis_size("replica")
    home_assigned = adapter_down_factors.shape[0]
    model_width = adapter_down_factors.shape[1]
    factor_rank = adapter_down_factors.shape[2]
    feature_width = adapter_up_factors.shape[2]
    hot_count = popular_adapters.shape[0]
    capacity = max(2, 3 * tok_rows // (2 * peers))
    down_joined = jnp.transpose(adapter_down_factors, (1, 0, 2)).reshape(
        model_width, home_assigned * factor_rank
    )
    up_joined = adapter_up_factors.reshape(home_assigned * factor_rank, feature_width)

    def routed_term(block_rows, selected, sending):
        target = selected // home_assigned
        onehot = (target[:, None] == lax.broadcasted_iota(jnp.int32, (1, peers), 1)) & sending[
            :, None
        ]
        as_ints = onehot.astype(jnp.int32)
        earlier = jnp.cumsum(as_ints, axis=0) - as_ints
        position = jnp.sum(jnp.where(onehot, earlier, 0), axis=1)
        slot_index = jnp.where(sending, target * capacity + position, peers * capacity)
        buffer_rows = (
            jnp.zeros((peers * capacity, model_width), jnp.bfloat16)
            .at[slot_index]
            .set(block_rows, mode="drop")
        )
        buffer_slots = (
            jnp.full((peers * capacity,), -1, jnp.int32)
            .at[slot_index]
            .set(selected % home_assigned, mode="drop")
        )
        got_rows = lax.all_to_all(
            buffer_rows.reshape(peers, capacity, model_width),
            "replica",
            split_axis=0,
            concat_axis=0,
            tiled=True,
        )
        got_slots = lax.all_to_all(
            buffer_slots.reshape(peers, capacity),
            "replica",
            split_axis=0,
            concat_axis=0,
            tiled=True,
        )
        senders, items = got_slots.shape
        result = masked_term(
            got_rows.reshape(senders * items, model_width),
            got_slots.reshape(senders * items),
            down_joined,
            up_joined,
            factor_rank,
        )
        computed = result.reshape(senders, items, feature_width)
        returned = lax.all_to_all(computed, "replica", split_axis=0, concat_axis=0, tiled=True)
        flat_back = returned.reshape(peers * capacity, feature_width)
        safe_index = jnp.minimum(slot_index, peers * capacity - 1)
        return jnp.where(sending[:, None], flat_back[safe_index], jnp.zeros((), jnp.bfloat16))

    def finish(block_rows, lowrank_update, valid):
        base = jnp.dot(block_rows, value_weight_base, preferred_element_type=jnp.float32)
        summed = (base + lowrank_update.astype(jnp.float32)).astype(jnp.bfloat16)
        return jnp.where(valid[:, None], summed, jnp.zeros((), jnp.bfloat16))

    positions = lax.iota(jnp.int32, tok_rows)
    valid_first = positions < valid_row_counts[0, 0]
    first_output = finish(
        first_activations,
        routed_term(first_activations, first_adapter_ids, valid_first),
        valid_first,
    )

    def fetch(hot_index, stacks):
        target = popular_adapters[hot_index]
        source = target // home_assigned
        inside_limit = target % home_assigned
        down_portion = lax.dynamic_index_in_dim(
            adapter_down_factors, inside_limit, 0, keepdims=False
        )
        up_portion = lax.dynamic_index_in_dim(adapter_up_factors, inside_limit, 0, keepdims=False)
        got_down, got_up = (
            from_root(down_portion, "replica", source),
            from_root(up_portion, "replica", source),
        )
        return (stacks[0].at[hot_index].set(got_down), stacks[1].at[hot_index].set(got_up))

    start = (
        jnp.zeros((hot_count, model_width, factor_rank), jnp.bfloat16),
        jnp.zeros((hot_count, factor_rank, feature_width), jnp.bfloat16),
    )
    got_down, got_up = lax.fori_loop(0, hot_count, fetch, start)
    valid_second = positions < valid_row_counts[1, 0]
    delta_second = routed_term(second_activations, second_adapter_ids, valid_second)
    second_output = finish(second_activations, delta_second, valid_second)
    hosted_adapters = replica_hosting[0]
    resident_down = lax.dynamic_slice_in_dim(got_down, hosted_adapters, 1, 0)
    resident_up = lax.dynamic_slice_in_dim(got_up, hosted_adapters, 1, 0)
    return (first_output, second_output, resident_down, resident_up)


def solution(mesh):
    return jax.shard_map(
        local,
        mesh=mesh,
        in_specs=(
            P(("groups", "replica"), None),
            P(("groups", "replica"), None),
            P(("groups", "replica")),
            P(("groups", "replica")),
            P(None, ("groups", "replica")),
            P("groups"),
            P(("groups", "replica")),
            P(),
            P("replica", None, None),
            P("replica", None, None),
        ),
        out_specs=(
            P(("groups", "replica"), None),
            P(("groups", "replica"), None),
            P(("groups", "replica"), None, None),
            P(("groups", "replica"), None, None),
        ),
        check_vma=False,
    )
```

profile of v0, /device:TPU:0, one launch (start us, length us, event | category | flops | bytes accessed | tf_op | source)
XLA Modules:
  0.0 992.8 jit_solution(6599949073675891544)
XLA Ops:
  8.5 1.3 fusion.28
  12.0 1.3 compare_select_fusion
  15.0 7.4 all-to-all-start
  24.1 4.6 all-to-all-done
  28.7 3.5 all-to-all-start.3
  32.2 3.2 scatter_custom_fusion.3
  35.4 1.6 reshape.229
  37.0 1.5 all-to-all-done.3
  38.5 4.4 all-to-all-start.4
  43.6 4.0 scatter_custom_fusion.1
  47.6 3.4 reshape.223
  51.1 33.0 %all-to-all-done.4 = bf16[16,12,4096]{2,1,0:T(8,128)(2,1)S(1)} async-done(((bf16[16,12,4096]{2,1,0:T(8,128)(2,1)}), bf16[16,12,4096]{2,1,0:T(8,128)(2,1)S(1)}, u32[]{:S(2)}, u32[]{:S(2)}) %all-to-all-start.4) | async-done | bytes 1572896 | tf_op jit(solution)/shard_map/all_to_all | solution.py:64
  84.1 11.3 %all-to-all-start.1 = ((bf16[16,12,4096]{2,1,0:T(8,128)(2,1)}), bf16[16,12,4096]{2,1,0:T(8,128)(2,1)}, u32[]{:S(2)}, u32[]{:S(2)}) async-start(bf16[16,12,4096]{2,1,0:T(8,128)(2,1)} %reshape.223), calls=%async_computation.1 | async-start | bytes 4194304 | tf_op jit(solution)/shard_map/all_to_all | solution.py:64
  95.4 2.4 broadcast_in_dim.83.clone
  97.9 844.5 %while.19 = (s32[]{:T(128)}, bf16[8,4096,64]{1,2,0:T(8,128)(2,1)}, bf16[8,64,512]{2,1,0:T(8,128)(2,1)S(1)}, s32[8]{0:T(128)S(1)}, bf16[4,4096,64]{1,2,0:T(8,128)...) while((s32[]{:T(128)}, bf16[8,4096,64]{1,2,0:T(8,128)(2,1)}, ...), condition=%wide.region_12.13_spmd, body=%wide.region_8.12_spmd.sunk | while | flops 884780 | bytes 14091272 | solution.py:123
  104.4 1.1 constant_dynamic-slice_fusion.7
  106.7 108.8 %all-reduce.5.cloned.1.call-done = (bf16[1,4096,64]{2,1,0:T(8,128)(2,1)}, bf16[1,64,512]{2,1,0:T(8,128)(2,1)}) async-done(((bf16[1,4096,64]{2,1,0:T(8,128)(2,1)}, bf16[1,64,512]{2,1,0:T(8,128)(2,1)}), (bf16[1,4096,64]{2,1,0:T(8,128)(2,1)}, bf16[1,64,512]{2,1,0:T(8,128)(2,1)})) %all-reduce.5.cloned.1.call-update) | async-done | bytes 589840 | tf_op jit(solution)/shard_map/while/body/eval_jaxpr/psum | solution.py:9
  215.6 2.0 broadcast_select_fusion.5
  226.0 1.1 constant_dynamic-slice_fusion.7
  228.2 90.6 %all-reduce.5.cloned.1.call-done = (bf16[1,4096,64]{2,1,0:T(8,128)(2,1)}, bf16[1,64,512]{2,1,0:T(8,128)(2,1)}) async-done(((bf16[1,4096,64]{2,1,0:T(8,128)(2,1)}, bf16[1,64,512]{2,1,0:T(8,128)(2,1)}), (bf16[1,4096,64]{2,1,0:T(8,128)(2,1)}, bf16[1,64,512]{2,1,0:T(8,128)(2,1)})) %all-reduce.5.cloned.1.call-update) | async-done | bytes 589840 | tf_op jit(solution)/shard_map/while/body/eval_jaxpr/psum | solution.py:9
  318.8 2.0 broadcast_select_fusion.5
  329.2 1.1 constant_dynamic-slice_fusion.7
  331.5 90.6 %all-reduce.5.cloned.1.call-done = (bf16[1,4096,64]{2,1,0:T(8,128)(2,1)}, bf16[1,64,512]{2,1,0:T(8,128)(2,1)}) async-done(((bf16[1,4096,64]{2,1,0:T(8,128)(2,1)}, bf16[1,64,512]{2,1,0:T(8,128)(2,1)}), (bf16[1,4096,64]{2,1,0:T(8,128)(2,1)}, bf16[1,64,512]{2,1,0:T(8,128)(2,1)})) %all-reduce.5.cloned.1.call-update) | async-done | bytes 589840 | tf_op jit(solution)/shard_map/while/body/eval_jaxpr/psum | solution.py:9
  422.1 2.0 broadcast_select_fusion.5
  432.5 1.1 constant_dynamic-slice_fusion.7
  434.8 90.6 %all-reduce.5.cloned.1.call-done = (bf16[1,4096,64]{2,1,0:T(8,128)(2,1)}, bf16[1,64,512]{2,1,0:T(8,128)(2,1)}) async-done(((bf16[1,4096,64]{2,1,0:T(8,128)(2,1)}, bf16[1,64,512]{2,1,0:T(8,128)(2,1)}), (bf16[1,4096,64]{2,1,0:T(8,128)(2,1)}, bf16[1,64,512]{2,1,0:T(8,128)(2,1)})) %all-reduce.5.cloned.1.call-update) | async-done | bytes 589840 | tf_op jit(solution)/shard_map/while/body/eval_jaxpr/psum | solution.py:9
  525.4 2.0 broadcast_select_fusion.5
  535.8 1.1 constant_dynamic-slice_fusion.7
  538.1 90.6 %all-reduce.5.cloned.1.call-done = (bf16[1,4096,64]{2,1,0:T(8,128)(2,1)}, bf16[1,64,512]{2,1,0:T(8,128)(2,1)}) async-done(((bf16[1,4096,64]{2,1,0:T(8,128)(2,1)}, bf16[1,64,512]{2,1,0:T(8,128)(2,1)}), (bf16[1,4096,64]{2,1,0:T(8,128)(2,1)}, bf16[1,64,512]{2,1,0:T(8,128)(2,1)})) %all-reduce.5.cloned.1.call-update) | async-done | bytes 589840 | tf_op jit(solution)/shard_map/while/body/eval_jaxpr/psum | solution.py:9
  628.7 2.0 broadcast_select_fusion.5
  639.1 1.1 constant_dynamic-slice_fusion.7
  641.4 90.6 %all-reduce.5.cloned.1.call-done = (bf16[1,4096,64]{2,1,0:T(8,128)(2,1)}, bf16[1,64,512]{2,1,0:T(8,128)(2,1)}) async-done(((bf16[1,4096,64]{2,1,0:T(8,128)(2,1)}, bf16[1,64,512]{2,1,0:T(8,128)(2,1)}), (bf16[1,4096,64]{2,1,0:T(8,128)(2,1)}, bf16[1,64,512]{2,1,0:T(8,128)(2,1)})) %all-reduce.5.cloned.1.call-update) | async-done | bytes 589840 | tf_op jit(solution)/shard_map/while/body/eval_jaxpr/psum | solution.py:9
  732.0 2.0 broadcast_select_fusion.5
  744.7 90.6 %all-reduce.5.cloned.1.call-done = (bf16[1,4096,64]{2,1,0:T(8,128)(2,1)}, bf16[1,64,512]{2,1,0:T(8,128)(2,1)}) async-done(((bf16[1,4096,64]{2,1,0:T(8,128)(2,1)}, bf16[1,64,512]{2,1,0:T(8,128)(2,1)}), (bf16[1,4096,64]{2,1,0:T(8,128)(2,1)}, bf16[1,64,512]{2,1,0:T(8,128)(2,1)})) %all-reduce.5.cloned.1.call-update) | async-done | bytes 589840 | tf_op jit(solution)/shard_map/while/body/eval_jaxpr/psum | solution.py:9
  835.2 2.0 broadcast_select_fusion.5
  847.9 90.6 %all-reduce.5.cloned.1.call-done = (bf16[1,4096,64]{2,1,0:T(8,128)(2,1)}, bf16[1,64,512]{2,1,0:T(8,128)(2,1)}) async-done(((bf16[1,4096,64]{2,1,0:T(8,128)(2,1)}, bf16[1,64,512]{2,1,0:T(8,128)(2,1)}), (bf16[1,4096,64]{2,1,0:T(8,128)(2,1)}, bf16[1,64,512]{2,1,0:T(8,128)(2,1)})) %all-reduce.5.cloned.1.call-update) | async-done | bytes 589840 | tf_op jit(solution)/shard_map/while/body/eval_jaxpr/psum | solution.py:9
  938.5 2.0 broadcast_select_fusion.5
  943.0 1.9 constant_dynamic-slice_fusion.3
  946.3 3.6 reshape.230
  949.9 2.5 convolution_convert_fusion
  953.1 4.7 all-to-all-start.5
  958.6 3.6 reshape.224
  962.2 2.5 convolution_convert_fusion.1
  965.5 2.4 all-to-all-done.5
  967.9 3.6 all-to-all-start.2
  972.4 3.7 fusion.4
  976.1 5.5 all-to-all-done.2
  982.4 3.6 fusion.5
  (161 shorter events, 70.6 us)
Async XLA Ops:
  15.0 13.7 %all-to-all-start = ((s32[16,1,12]{2,1,0:T(1,128)}), s32[16,1,12]{2,1,0:T(1,128)S(1)}, u32[]{:S(2)}, u32[]{:S(2)}) async-start(s32[16,1,12]{2,1,0:T(1,128)} %bitcast.3), calls=%async_computation | async-start | bytes 16384 | tf_op jit(solution)/shard_map/all_to_all | solution.py:71
  28.7 9.8 all-to-all-start.3
  38.5 45.6 %all-to-all-start.4 = ((bf16[16,12,4096]{2,1,0:T(8,128)(2,1)}), bf16[16,12,4096]{2,1,0:T(8,128)(2,1)S(1)}, u32[]{:S(2)}, u32[]{:S(2)}) async-start(bf16[16,12,4096]{2,1,0:T(8,128)(2,1)} %reshape.229), calls=%async_computation.4 | async-start | bytes 4194304 | tf_op jit(solution)/shard_map/all_to_all | solution.py:64
  84.1 11.3 %copy-start.1 = (bf16[16,12,4096]{2,1,0:T(8,128)(2,1)}, bf16[16,12,4096]{2,1,0:T(8,128)(2,1)S(1)}, u32[]{:S(2)}) copy-start(bf16[16,12,4096]{2,1,0:T(8,128)(2,1)S(1)} %all-to-all-done.4) | copy-start | bytes 4718596
  84.1 869.0 %all-to-all-start.1 = ((bf16[16,12,4096]{2,1,0:T(8,128)(2,1)}), bf16[16,12,4096]{2,1,0:T(8,128)(2,1)}, u32[]{:S(2)}, u32[]{:S(2)}) async-start(bf16[16,12,4096]{2,1,0:T(8,128)(2,1)} %reshape.223), calls=%async_computation.1 | async-start | bytes 4194304 | tf_op jit(solution)/shard_map/all_to_all | solution.py:64
  95.4 2.5 copy-start.2
  95.4 2.5 copy-start.6
  95.4 2.5 copy-start.7
  97.9 117.7 %all-reduce.5.cloned.1.call-start = ((), (), s32[]{:S(2)}) async-start(), calls=%async_computation.6 | async-start | bytes 2228224 | tf_op jit(solution)/shard_map/while/body/eval_jaxpr/psum | solution.py:9
  217.6 1.2 copy-start.3
  219.4 99.4 %all-reduce.5.cloned.1.call-start = ((), (), s32[]{:S(2)}) async-start(), calls=%async_computation.6 | async-start | bytes 2228224 | tf_op jit(solution)/shard_map/while/body/eval_jaxpr/psum | solution.py:9
  320.8 1.2 copy-start.3
  322.7 99.4 %all-reduce.5.cloned.1.call-start = ((), (), s32[]{:S(2)}) async-start(), calls=%async_computation.6 | async-start | bytes 2228224 | tf_op jit(solution)/shard_map/while/body/eval_jaxpr/psum | solution.py:9
  424.1 1.2 copy-start.3
  426.0 99.4 %all-reduce.5.cloned.1.call-start = ((), (), s32[]{:S(2)}) async-start(), calls=%async_computation.6 | async-start | bytes 2228224 | tf_op jit(solution)/shard_map/while/body/eval_jaxpr/psum | solution.py:9
  527.4 1.2 copy-start.3
  529.3 99.4 %all-reduce.5.cloned.1.call-start = ((), (), s32[]{:S(2)}) async-start(), calls=%async_computation.6 | async-start | bytes 2228224 | tf_op jit(solution)/shard_map/while/body/eval_jaxpr/psum | solution.py:9
  630.7 1.2 copy-start.3
  632.5 99.4 %all-reduce.5.cloned.1.call-start = ((), (), s32[]{:S(2)}) async-start(), calls=%async_computation.6 | async-start | bytes 2228224 | tf_op jit(solution)/shard_map/while/body/eval_jaxpr/psum | solution.py:9
  733.9 1.2 copy-start.3
  735.8 99.4 %all-reduce.5.cloned.1.call-start = ((), (), s32[]{:S(2)}) async-start(), calls=%async_computation.6 | async-start | bytes 2228224 | tf_op jit(solution)/shard_map/while/body/eval_jaxpr/psum | solution.py:9
  837.2 1.2 copy-start.3
  839.1 99.4 %all-reduce.5.cloned.1.call-start = ((), (), s32[]{:S(2)}) async-start(), calls=%async_computation.6 | async-start | bytes 2228224 | tf_op jit(solution)/shard_map/while/body/eval_jaxpr/psum | solution.py:9
  940.5 1.2 copy-start.3
  944.9 5.0 copy-start
  953.1 14.8 %all-to-all-start.5 = ((bf16[16,12,512]{2,1,0:T(8,128)(2,1)}), bf16[16,12,512]{2,1,0:T(8,128)(2,1)S(1)}, u32[]{:S(2)}, u32[]{:S(2)}) async-start(bf16[16,12,512]{2,1,0:T(8,128)(2,1)} %reshape.231), calls=%async_computation.5 | async-start | bytes 524288 | tf_op jit(solution)/shard_map/all_to_all | solution.py:87
  964.7 7.7 copy-start.4
  967.9 13.6 %all-to-all-start.2 = ((bf16[16,12,512]{2,1,0:T(8,128)(2,1)}), bf16[16,12,512]{2,1,0:T(8,128)(2,1)S(1)}, u32[]{:S(2)}, u32[]{:S(2)}) async-start(bf16[16,12,512]{2,1,0:T(8,128)(2,1)} %reshape.227), calls=%async_computation.2 | async-start | bytes 524288 | tf_op jit(solution)/shard_map/all_to_all | solution.py:87
  972.4 10.0 %copy-start.5 = (bf16[128,4096]{1,0:T(8,128)(2,1)S(1)}, bf16[128,4096]{1,0:T(8,128)(2,1)}, u32[]{:S(2)}) copy-start(bf16[128,4096]{1,0:T(8,128)(2,1)} %param.16) | copy-start | bytes 3145732
Sparse Core Ops, SparseCore 0:
  104.6 110.9 all-reduce.4
  226.1 92.6 all-reduce.4
  329.4 92.6 all-reduce.4
  432.7 92.6 all-reduce.4
  535.9 92.6 all-reduce.4
  639.2 92.6 all-reduce.4
  742.5 92.6 all-reduce.4
  845.8 92.6 all-reduce.4
where the time goes:
time: 995 us; the launch traced here: 993 us
  waiting for transfers between devices  790 us (79%)
  local copies, waits for them, and re-layouts  72.1 us (7%)
  other arithmetic  46.7 us (5%)
  starting transfers between devices  35.2 us (4%)
  loops' own time  21.7 us (2%)
  between operations  14.9 us (1%)
  matrix products  12.2 us (1%)
    psum x8, waiting for transfers between devices, from_root(): return lax.psum(block, axis)  743 us
    all_to_all x2, waiting for transfers between devices, routed_term(): lax.all_to_all(buffer_rows.reshape(peers, capacity, model_width), 'replic...  33 us
    another operation x1, loops' own time, local(): got_down, got_up = lax.fori_loop(0, hot_count, fetch, start)  21.7 us
    another operation x16, other arithmetic  21.6 us
  transfers between devices with their start and end apart: 14, of which 13 were waited for; matrix products, arithmetic and copies ran while one was open for 12% of the time, Pallas kernels for 0%

commit v1 on v0

v1 whole, which is shorter than its diff:
```python
import functools
import math

import jax
import jax.numpy as jnp
from jax import lax
from jax.experimental import pallas as pl
from jax.experimental.pallas import tpu as pltpu
from jax.sharding import PartitionSpec as P

LANES = 128
ROWS = 16
CHUNK = 256
F32 = jnp.float32
BF16 = jnp.bfloat16


class Plan:
    def __init__(self, peers, tok, width, rank, feature, homed):
        self.peers, self.tok, self.width, self.rank = peers, tok, width, rank
        self.feature, self.homed = feature, homed
        self.cap = max(2, 3 * tok // (2 * peers))
        g = math.gcd(self.cap, ROWS)
        self.keep = self.cap // g
        self.pieces = ROWS // g
        self.extra = self.pieces - self.keep
        self.piece = width // self.pieces
        self.back = 2 * feature // self.pieces
        self.packed = peers * ROWS
        self.chunk = min(CHUNK, self.packed)
        self.row_groups = rank // ROWS
        self.col_tiles = (width + feature) // LANES
        self.tiles = self.row_groups * self.col_tiles
        self.share = -(-self.tiles // peers)
        self.tok_cols = self.keep * self.piece
        self.spread_cols = self.share * LANES
        self.back_cols = self.keep * self.back
        self.out_cols = 2 * self.tok_cols + self.spread_cols + LANES
        self.ret_cols = self.spread_cols + self.back_cols

    def chunks(self, body):
        count = self.packed // self.chunk
        if count == 1:
            body(0)
        else:

            @pl.loop(0, count)
            def _(i):
                body(pl.multiple_of(i * self.chunk, self.chunk))

    def extra_place(self, position, q):
        index = position * self.extra + (q - self.keep)
        row = index // self.keep
        return self.cap + row, index - row * self.keep


def route(ids_row, homed):
    n = ids_row.shape[1]
    ids = jnp.broadcast_to(ids_row, (n, n))
    peer_row = ids // homed
    peer_col = jnp.transpose(ids.astype(F32)).astype(jnp.int32) // homed
    same = peer_row == peer_col
    above = lax.broadcasted_iota(jnp.int32, (n, n), 0)
    along = lax.broadcasted_iota(jnp.int32, (n, n), 1)
    pos_row = jnp.sum(jnp.where(same & (above < along), 1, 0), axis=0, keepdims=True)
    pos_col = jnp.sum(jnp.where(same & (along < above), 1, 0), axis=1, keepdims=True)
    return peer_row[0:1, :], pos_row, peer_col[:, 0:1], pos_col


def pack_kernel(plan, ids1, ids2, popular, hosting, x1, x2, down, up, out):
    me = lax.axis_index("replica")
    slot = jnp.int32(0)
    for i in range(popular.shape[0]):
        adapter = popular[i]
        slot = jnp.where(adapter // plan.homed == me, adapter % plan.homed, slot)
    wanted = popular[hosting[0]] // plan.homed
    base = 2 * plan.tok_cols
    for t in range(plan.share * plan.peers):
        d, j = divmod(t, plan.share)
        to = (pl.ds(d * ROWS, ROWS), pl.ds(base + j * LANES, LANES))
        if t < plan.tiles:
            group, col = divmod(t, plan.col_tiles)
            rows = pl.ds(group * ROWS, ROWS)
            col *= LANES
            if col < plan.width:
                out[to] = down[slot, rows, pl.ds(col, LANES)]
            else:
                out[to] = up[slot, rows, pl.ds(col - plan.width, LANES)]
        else:
            out[to] = jnp.zeros((ROWS, LANES), BF16)
    routes = []
    for ids in (ids1, ids2):
        peer, pos, _, _ = route(ids[...], plan.homed)
        routes.append((peer, pos, (ids[...] % plan.homed).astype(F32)))

    def body(start):
        index = lax.broadcasted_iota(jnp.int32, (plan.chunk, plan.tok), 0) + start
        meta = jnp.zeros((plan.chunk, LANES), F32)
        lane = lax.broadcasted_iota(jnp.int32, (plan.chunk, LANES), 1)
        rows = pl.ds(start, plan.chunk)
        for b, x in enumerate((x1, x2)):
            peer, pos, slots = routes[b]
            direct = index == peer * ROWS + pos
            slot_col = jnp.sum(jnp.where(direct, slots, 0.0), axis=1, keepdims=True)
            meta = jnp.where(lane == b, slot_col, meta)
            ends = [plan.extra_place(pos, q) for q in range(plan.keep, plan.pieces)]
            for k in range(plan.keep):
                hots = [direct] + [(index == peer * ROWS + r) & (blk == k) for r, blk in ends]
                parts = [x[:, k * plan.piece : (k + 1) * plan.piece]]
                parts += [
                    x[:, q * plan.piece : (q + 1) * plan.piece]
                    for q in range(plan.keep, plan.pieces)
                ]
                hot = jnp.concatenate(
                    [jnp.where(h, 1.0, 0.0).astype(BF16) for h in hots], axis=1
                )
                got = jnp.dot(hot, jnp.concatenate(parts, axis=0), preferred_element_type=F32)
                col = b * plan.tok_cols + k * plan.piece
                out[rows, col : col + plan.piece] = got.astype(BF16)
        meta = jnp.where(lane == 2, wanted.astype(F32), meta)
        out[rows, base + plan.spread_cols :] = meta.astype(BF16)

    plan.chunks(body)


def home_kernel(plan, got, down, up, out):
    base = 2 * plan.tok_cols
    joined = plan.homed * plan.rank

    def unpack(start, first, size, q, into):
        n = plan.chunk
        row = lax.broadcasted_iota(jnp.int32, (n, n), 0)
        col = lax.broadcasted_iota(jnp.int32, (n, n), 1)
        p = row % ROWS
        place, blk = plan.extra_place(p, q)
        target = row - p + place
        rows = pl.ds(start, n)
        total = None
        hots = [
            jnp.where((col == target) & (blk == k) & (p < plan.cap), 1.0, 0.0).astype(BF16)
            for k in range(plan.keep)
        ]
        parts = [got[rows, first + k * size : first + (k + 1) * size] for k in range(plan.keep)]
        return jnp.dot(
            jnp.concatenate(hots, axis=1),
            jnp.concatenate(parts, axis=0),
            preferred_element_type=F32,
        ).astype(BF16)

    def body(start):
        n = plan.chunk
        rows = pl.ds(start, n)
        meta = got[rows, base + plan.spread_cols : base + plan.spread_cols + LANES].astype(F32)
        meta = meta.astype(jnp.int32)
        deltas = []
        nt = (((1,), (1,)), ((), ()))
        for b in range(2):
            first = b * plan.tok_cols
            total = lax.dot_general(
                got[rows, first : first + plan.tok_cols],
                down[:, : plan.tok_cols],
                nt,
                preferred_element_type=F32,
            )
            for q in range(plan.keep, plan.pieces):
                total += lax.dot_general(
                    unpack(start, first, plan.piece, q, None),
                    down[:, q * plan.piece : (q + 1) * plan.piece],
                    nt,
                    preferred_element_type=F32,
                )
            column = lax.broadcasted_iota(jnp.int32, (n, joined), 1) // plan.rank
            kept = jnp.where(column == meta[:, b : b + 1], total, 0.0).astype(BF16)
            deltas.append(
                jnp.dot(kept, up[...], preferred_element_type=F32).astype(BF16)
            )
        both = jnp.concatenate(deltas, axis=1)
        row = lax.broadcasted_iota(jnp.int32, (n, n), 0)
        col = lax.broadcasted_iota(jnp.int32, (n, n), 1)
        p = col % ROWS
        straight = (row == col) & (p < plan.cap)
        ends = [plan.extra_place(p, q) for q in range(plan.keep, plan.pieces)]
        for k in range(plan.keep):
            hots = [straight] + [
                (row == col - p + r) & (blk == k) & (p < plan.cap) for r, blk in ends
            ]
            parts = [both[:, k * plan.back : (k + 1) * plan.back]] + [
                both[:, q * plan.back : (q + 1) * plan.back]
                for q in range(plan.keep, plan.pieces)
            ]
            hot = jnp.concatenate([jnp.where(h, 1.0, 0.0).astype(BF16) for h in hots], axis=1)
            sent = jnp.dot(hot, jnp.concatenate(parts, axis=0), preferred_element_type=F32)
            at = plan.spread_cols + k * plan.back
            out[rows, at : at + plan.back] = sent.astype(BF16)
        wide = lax.broadcasted_iota(jnp.int32, (n, plan.packed), 1)
        inner = lax.broadcasted_iota(jnp.int32, (n, plan.packed), 0) % ROWS
        pick = jnp.where(wide == meta[:, 2:3] * ROWS + inner, 1.0, 0.0).astype(BF16)
        out[rows, : plan.spread_cols] = jnp.dot(
            pick, got[:, base : base + plan.spread_cols], preferred_element_type=F32
        ).astype(BF16)

    plan.chunks(body)


def final_kernel(plan, ids1, ids2, counts, back, base1, base2, out1, out2, down, up):
    for t in range(plan.tiles):
        d, j = divmod(t, plan.share)
        group, col = divmod(t, plan.col_tiles)
        tile = back[d * ROWS : (d + 1) * ROWS, j * LANES : (j + 1) * LANES]
        rows = slice(group * ROWS, (group + 1) * ROWS)
        col *= LANES
        if col < plan.width:
            down[0, rows, col : col + LANES] = tile
        else:
            up[0, rows, col - plan.width : col - plan.width + LANES] = tile
    index = lax.broadcasted_iota(jnp.int32, (plan.tok, plan.packed), 1)
    half = plan.pieces // 2
    for b, (ids, base, out) in enumerate(((ids1, base1, out1), (ids2, base2, out2))):
        _, _, peer, pos = route(ids[...], plan.homed)
        valid = lax.broadcasted_iota(jnp.int32, (plan.tok, plan.back), 0) < counts[b, 0]
        for i in range(half):
            q = b * half + i
            if q < plan.keep:
                hots = [index == peer * ROWS + pos]
                blocks = [q]
            else:
                r, blk = plan.extra_place(pos, q)
                hots = [(index == peer * ROWS + r) & (blk == k) for k in range(plan.keep)]
                blocks = range(plan.keep)
            delta = None
            for h, k in zip(hots, blocks):
                at = plan.spread_cols + k * plan.back
                term = jnp.dot(
                    jnp.where(h, 1.0, 0.0).astype(BF16),
                    back[:, at : at + plan.back],
                    preferred_element_type=F32,
                )
                delta = term if delta is None else delta + term
            cols = slice(i * plan.back, (i + 1) * plan.back)
            out[:, cols] = jnp.where(valid, base[:, cols] + delta, 0.0).astype(BF16)


def local(
    first_activations,
    second_activations,
    first_adapter_ids,
    second_adapter_ids,
    valid_row_counts,
    popular_adapters,
    replica_hosting,
    value_weight_base,
    adapter_down_factors,
    adapter_up_factors,
):
    tok, width = first_activations.shape
    homed, _, rank = adapter_down_factors.shape
    feature = adapter_up_factors.shape[2]
    plan = Plan(lax.axis_size("replica"), tok, width, rank, feature, homed)
    down = jnp.swapaxes(adapter_down_factors, 1, 2)
    ids1 = first_adapter_ids.reshape(1, tok)
    ids2 = second_adapter_ids.reshape(1, tok)
    vmem = pl.BlockSpec(memory_space=pltpu.VMEM)
    smem = pl.BlockSpec(memory_space=pltpu.SMEM)
    params = pltpu.CompilerParams(vmem_limit_bytes=48 * 1024 * 1024)

    sent = pl.pallas_call(
        functools.partial(pack_kernel, plan),
        out_shape=jax.ShapeDtypeStruct((plan.packed, plan.out_cols), BF16),
        in_specs=[vmem, vmem, smem, smem, vmem, vmem, vmem, vmem],
        out_specs=vmem,
        compiler_params=params,
        name="pack",
    )(
        ids1,
        ids2,
        popular_adapters,
        replica_hosting,
        first_activations,
        second_activations,
        down,
        adapter_up_factors,
    )
    exchange = functools.partial(
        lax.all_to_all, axis_name="replica", split_axis=0, concat_axis=0, tiled=True
    )
    got = exchange(sent.reshape(plan.peers, ROWS, plan.out_cols))
    base1 = jnp.dot(first_activations, value_weight_base, preferred_element_type=F32)
    base2 = jnp.dot(second_activations, value_weight_base, preferred_element_type=F32)
    reply = pl.pallas_call(
        functools.partial(home_kernel, plan),
        out_shape=jax.ShapeDtypeStruct((plan.packed, plan.ret_cols), BF16),
        in_specs=[vmem, vmem, vmem],
        out_specs=vmem,
        compiler_params=params,
        name="home",
    )(
        got.reshape(plan.packed, plan.out_cols),
        down.reshape(homed * rank, width),
        adapter_up_factors.reshape(homed * rank, feature),
    )
    back = exchange(reply.reshape(plan.peers, ROWS, plan.ret_cols))
    out1, out2, resident_down, resident_up = pl.pallas_call(
        functools.partial(final_kernel, plan),
        out_shape=[
            jax.ShapeDtypeStruct((tok, feature), BF16),
            jax.ShapeDtypeStruct((tok, feature), BF16),
            jax.ShapeDtypeStruct((1, rank, width), BF16),
            jax.ShapeDtypeStruct((1, rank, feature), BF16),
        ],
        in_specs=[vmem, vmem, smem, vmem, vmem, vmem],
        out_specs=[vmem] * 4,
        compiler_params=params,
        name="finish",
    )(
        ids1,
        ids2,
        valid_row_counts,
        back.reshape(plan.packed, plan.ret_cols),
        base1,
        base2,
    )
    return out1, out2, jnp.swapaxes(resident_down, 1, 2), resident_up


def solution(mesh):
    return jax.shard_map(
        local,
        mesh=mesh,
        in_specs=(
            P(("groups", "replica"), None),
            P(("groups", "replica"), None),
            P(("groups", "replica")),
            P(("groups", "replica")),
            P(None, ("groups", "replica")),
            P("groups"),
            P(("groups", "replica")),
            P(),
            P("replica", None, None),
            P("replica", None, None),
        ),
        out_specs=(
            P(("groups", "replica"), None),
            P(("groups", "replica"), None),
            P(("groups", "replica"), None, None),
            P(("groups", "replica"), None, None),
        ),
        check_vma=False,
    )
```

time: 995 us -> 142 us (0.14)
  waiting for transfers between devices: 790 us -> 17.5 us
  blocking collectives: 0 us -> 93.3 us
  local copies, waits for them, and re-layouts: 72.1 us -> 7.43 us
  other arithmetic: 46.7 us -> 0 us
  starting transfers between devices: 35.2 us -> 3.77 us
  loops' own time: 21.7 us -> 0 us
  between operations: 14.9 us -> 1.34 us
  Pallas kernels: 0 us -> 13.4 us
    psum x8 -> x0, waiting for transfers between devices: 743 us -> none  [from_root(): return lax.psum(block, axis)]
    all_to_all x0 -> x1, blocking collectives: none -> 93.3 us  [local(): got = exchange(sent.reshape(plan.peers, ROWS, plan.out_cols))]
    all_to_all x6 -> x1, starting transfers between devices: 34.8 us -> 3.77 us  [local(): back = exchange(reply.reshape(plan.peers, ROWS, plan.ret_cols))]
    all_to_all x6 -> x1, waiting for transfers between devices: 47.1 us -> 17.5 us  [local(): back = exchange(reply.reshape(plan.peers, ROWS, plan.ret_cols))]
    another operation x18 -> x0, other arithmetic: 21.9 us -> none
    another operation x1 -> x0, loops' own time: 21.7 us -> none  [local(): got_down, got_up = lax.fori_loop(0, hot_count, fetch, start)]
    dynamic_slice x26 -> x0, local copies, waits for them, and re-layouts: 19.7 us -> none  [the longest x16 12.5 us: fetch(): lax.dynamic_index_in_dim(adapter_down_factors, inside_limit, 0, keepdims=...]
    scatter x20 -> x0, local copies, waits for them, and re-layouts: 18.6 us -> none  [the longest x16 9.39 us: fetch(): stacks[0].at[hot_index].set(got_down)]
  transfers between devices with their start and end apart: 14 -> 1, of which waited for: 13 -> 1; matrix products, arithmetic and copies ran while one was open for 12% -> 3% of each run, Pallas kernels for 0% -> 0%
where the time goes in v1:
time: 142 us; the launch traced here: 141 us
  blocking collectives  93.3 us (66%)
  waiting for transfers between devices  17.5 us (12%)
  Pallas kernels  13.4 us (9%)
  local copies, waits for them, and re-layouts  7.43 us (5%)
  matrix products  3.83 us (3%)
  starting transfers between devices  3.77 us (3%)
    all_to_all x1, blocking collectives, local(): got = exchange(sent.reshape(plan.peers, ROWS, plan.out_cols))  93.3 us
    all_to_all x1, waiting for transfers between devices, local(): back = exchange(reply.reshape(plan.peers, ROWS, plan.ret_cols))  17.5 us
    pallas_call x1, Pallas kernels, local(): pl.pallas_call(functools.partial(home_kernel, plan), out_shape=jax.ShapeD...  7.88 us
    unnamed x29, local copies, waits for them, and re-layouts  7.43 us
    all_to_all x1, starting transfers between devices, local(): back = exchange(reply.reshape(plan.peers, ROWS, plan.ret_cols))  3.77 us
    pallas_call x1, Pallas kernels, local(): pl.pallas_call(functools.partial(pack_kernel, plan), out_shape=jax.ShapeD...  3.58 us
    dot_general x1, matrix products, local(): jnp.dot(first_activations, value_weight_base, preferred_element_type=F32)  3.06 us
  transfers between devices with their start and end apart: 1, of which 1 were waited for; matrix products, arithmetic and copies ran while one was open for 3% of the time, Pallas kernels for 0%

profile of v1, /device:TPU:0, one launch (start us, length us, event | category | flops | bytes accessed | tf_op | source)
XLA Modules:
  0.0 140.5 jit_solution(17548813066031057346)
XLA Ops:
  1.3 0.0 copy-start
  1.3 1.6 %copy-done = bf16[4,4096,64]{1,2,0:T(8,128)(2,1)S(1)} copy-done((bf16[4,4096,64]{1,2,0:T(8,128)(2,1)S(1)}, bf16[4,4096,64]{1,2,0:T(8,128)(2,1)}, u32[]{:S(2)}) %copy-start) | copy-done | bytes 2097176
  2.9 0.0 copy-start.2
  2.9 1.2 copy-done.2
  4.1 0.0 copy-start.4
  4.1 1.2 copy-done.4
  5.3 0.0 copy-start.6
  5.3 0.9 copy-done.6
  6.3 0.0 copy-start.7
  6.3 0.7 copy-done.7
  6.9 0.0 copy-start.9
  6.9 0.7 copy-done.9
  7.6 0.0 copy-start.11
  7.6 0.7 copy-done.11
  8.2 3.6 %pack.1 = bf16[256,7424]{1,0:T(8,128)(2,1)} custom-call(s32[1,128]{1,0:T(1,128)S(1)} %bitcast.19, s32[1,128]{1,0:T(1,128)S(1)} %bitcast.21, s32[8]{0:T(128)S(1)} %copy-done.11, s32[1]{0:T(128)S(6)} %copy.15.hosting, bf16[128,4096]{1,0:T(8,128)(2,1)S(1)} %copy-done.2, bf16[128,4096]{1,0:T(8,128)(2,1)S(1)} %copy-done.4, bf16[4,64,4096]{2,1,0:T(8,128)(2,1)S(1)} %bitcast.15, ...), custom_call_target="tpu_custom_call" | custom-call | tf_op jit(solution)/shard_map/pack/pallas_call | solution.py:266
  11.8 0.0 copy-start.1
  11.8 93.3 %all_to_all.10 = bf16[16,16,7424]{2,1,0:T(8,128)(2,1)} all-to-all(bf16[16,16,7424]{2,1,0:T(8,128)(2,1)} %bitcast.23), channel_id=1, replica_groups=mesh['groups'=2,'replica'=16] {'replica'}, dimensions={0} | all-to-all | bytes 7602176 | tf_op jit(solution)/shard_map/all_to_all | solution.py:286
  105.1 0.0 copy-done.1
  105.1 0.0 copy-start.13
  105.1 0.0 copy-start.3
  105.1 7.9 %home.1 = bf16[256,1920]{1,0:T(8,128)(2,1)} custom-call(bf16[256,7424]{1,0:T(8,128)(2,1)} %bitcast.24, bf16[256,4096]{1,0:T(8,128)(2,1)S(1)} %bitcast.16, bf16[256,512]{1,0:T(8,128)(2,1)S(1)} %bitcast.18), custom_call_target="tpu_custom_call" | custom-call | tf_op jit(solution)/shard_map/home/pallas_call | solution.py:289
  113.0 0.0 copy-start.5
  113.0 3.8 %all-to-all-start.1 = ((bf16[16,16,1920]{2,1,0:T(8,128)(2,1)}), bf16[16,16,1920]{2,1,0:T(8,128)(2,1)S(1)}, u32[]{:S(2)}, u32[]{:S(2)}) async-start(bf16[16,16,1920]{2,1,0:T(8,128)(2,1)} %bitcast.7), calls=%async_computation.1 | async-start | bytes 1966080 | tf_op jit(solution)/shard_map/all_to_all | solution.py:301
  116.7 0.0 copy-done.13
  116.8 0.1 copy.14.counts
  116.8 0.0 copy-done.3
  116.9 0.0 copy-start.12
  116.9 0.0 copy-start.8
  116.9 0.0 copy-start.10
  116.9 3.1 %fusion.base1 = f32[128,512]{1,0:T(8,128)S(1)} fusion(bf16[128,4096]{1,0:T(8,128)(2,1)S(1)} %copy-done.3, bf16[4096,512]{1,0:T(8,128)(2,1)} %param.17), kind=kOutput, calls=%fused_computation | convolution fusion | flops 536870912 | bytes 5505024 | tf_op jit(solution)/shard_map/dot_general | solution.py:287
  119.9 0.0 copy-done.5
  119.9 0.4 copy-done.12
  120.3 0.8 fusion.1.base2
  121.1 17.5 %all-to-all-done.1 = bf16[16,16,1920]{2,1,0:T(8,128)(2,1)S(1)} async-done(((bf16[16,16,1920]{2,1,0:T(8,128)(2,1)}), bf16[16,16,1920]{2,1,0:T(8,128)(2,1)S(1)}, u32[]{:S(2)}, u32[]{:S(2)}) %all-to-all-start.1) | async-done | bytes 983072 | tf_op jit(solution)/shard_map/all_to_all | solution.py:301
  138.6 0.0 copy-done.8
  138.6 0.0 copy-done.10
  138.6 2.0 %finish.1 = (bf16[128,512]{1,0:T(8,128)(2,1)}, bf16[128,512]{1,0:T(8,128)(2,1)}, bf16[1,64,4096]{2,1,0:T(8,128)(2,1)}, bf16[1,64,512]{2,1,0:T(8,128)(2,1)}) custom-call(s32[1,128]{1,0:T(1,128)S(1)} %bitcast.20, s32[1,128]{1,0:T(1,128)S(1)} %bitcast.22, s32[2,1]{1,0:T(2,128)S(1)} %copy.14.counts, bf16[256,1920]{1,0:T(8,128)(2,1)S(1)} %bitcast.17, ...), custom_call_target="tpu_custom_call" | custom-call | tf_op jit(solution)/shard_map/finish/pallas_call | solution.py:302
Async XLA Ops:
  1.3 1.6 %copy-start = (bf16[4,4096,64]{1,2,0:T(8,128)(2,1)S(1)}, bf16[4,4096,64]{1,2,0:T(8,128)(2,1)}, u32[]{:S(2)}) copy-start(bf16[4,4096,64]{1,2,0:T(8,128)(2,1)} %param.18) | copy-start | bytes 6291460
  2.9 1.2 copy-start.2
  4.1 1.2 copy-start.4
  5.3 0.9 copy-start.6
  6.3 0.7 copy-start.7
  6.9 0.7 copy-start.9
  7.6 0.7 copy-start.11
  11.8 93.3 %copy-start.1 = (bf16[4,4096,64]{1,2,0:T(8,128)(2,1)S(1)}, bf16[4,4096,64]{1,2,0:T(8,128)(2,1)}, u32[]{:S(2)}) copy-start(bf16[4,4096,64]{1,2,0:T(8,128)(2,1)} %param.18) | copy-start | bytes 6291460
  105.1 11.7 %copy-start.13 = (s32[2,1]{0,1:T(1,128)S(1)}, s32[2,1]{0,1:T(1,128)}, u32[]{:S(2)}) copy-start(s32[2,1]{0,1:T(1,128)} %param.14) | copy-start | bytes 28
  105.1 11.8 %copy-start.3 = (bf16[128,4096]{1,0:T(8,128)(2,1)S(1)}, bf16[128,4096]{1,0:T(8,128)(2,1)}, u32[]{:S(2)}) copy-start(bf16[128,4096]{1,0:T(8,128)(2,1)} %x1.1) | copy-start | bytes 3145732
  113.0 7.0 %copy-start.5 = (bf16[128,4096]{1,0:T(8,128)(2,1)S(1)}, bf16[128,4096]{1,0:T(8,128)(2,1)}, u32[]{:S(2)}) copy-start(bf16[128,4096]{1,0:T(8,128)(2,1)} %x2.1) | copy-start | bytes 3145732
  113.0 25.6 %all-to-all-start.1 = ((bf16[16,16,1920]{2,1,0:T(8,128)(2,1)}), bf16[16,16,1920]{2,1,0:T(8,128)(2,1)S(1)}, u32[]{:S(2)}, u32[]{:S(2)}) async-start(bf16[16,16,1920]{2,1,0:T(8,128)(2,1)} %bitcast.7), calls=%async_computation.1 | async-start | bytes 1966080 | tf_op jit(solution)/shard_map/all_to_all | solution.py:301
  116.9 3.5 %copy-start.12 = (bf16[4096,512]{1,0:T(8,128)(2,1)S(1)}, bf16[4096,512]{1,0:T(8,128)(2,1)}, u32[]{:S(2)}) copy-start(bf16[4096,512]{1,0:T(8,128)(2,1)} %param.17) | copy-start | bytes 12582916
  116.9 21.7 %copy-start.8 = (s32[128]{0:T(128)S(1)}, s32[128]{0:T(128)}, u32[]{:S(2)}) copy-start(s32[128]{0:T(128)} %param.12) | copy-start | bytes 1540
  116.9 21.7 %copy-start.10 = (s32[128]{0:T(128)S(1)}, s32[128]{0:T(128)}, u32[]{:S(2)}) copy-start(s32[128]{0:T(128)} %param.13) | copy-start | bytes 1540

commit v2 on v0

v2 whole, which is shorter than its diff:
```python
import functools

import jax
import jax.numpy as jnp
from jax import lax
from jax.experimental import pallas as pl
from jax.experimental.pallas import tpu as pltpu
from jax.sharding import PartitionSpec as P

LANES = 128
ROWS = 16
CHUNK = 256
F32 = jnp.float32
BF16 = jnp.bfloat16
NT = (((1,), (1,)), ((), ()))


class Plan:
    def __init__(self, peers, tok, width, rank, feature, homed):
        self.peers, self.tok, self.width, self.rank = peers, tok, width, rank
        self.feature, self.homed = feature, homed
        self.cap = max(2, 3 * tok // (2 * peers))
        combined = 2 * self.cap
        self.full = combined // ROWS
        left = combined - self.full * ROWS
        if left > 8:
            self.full, left = self.full + 1, 0
        self.rest = left > 0
        self.sections = self.full + self.rest
        self.packed = peers * ROWS
        self.joined = homed * rank
        self.tok_cols = self.full * width + self.rest * (width // 2)
        self.back_cols = self.full * feature + self.rest * (feature // 2)
        self.col_tiles = (width + feature) // LANES
        tiles = (rank // ROWS) * self.col_tiles
        share = -(-tiles // peers)
        while self.col_tiles % share:
            share += 1
        self.per_group = self.col_tiles // share
        self.holders = tiles // share
        self.spread = share * LANES
        self.meta_at = self.tok_cols + self.spread
        self.cols = self.meta_at + LANES
        self.ret_cols = self.spread + self.back_cols
        self.half = peers // 2
        self.split = False and peers & (peers - 1) == 0 and self.half % self.per_group == 0

    def pieces(self, part, me):
        if part == "all":
            return 0, [(0, self.peers)]
        mine = (me // self.half) * self.half
        if part == "near":
            return mine, [(mine, self.half)]
        far = self.half - mine
        partner = me - mine
        return far, [(far + xor(partner, m, self.half), 1) for m in range(self.half)]

    def row_chunks(self, count):
        size = min(CHUNK, count * ROWS)
        return [(i, size) for i in range(0, count * ROWS, size)]


def xor(a, b, bound):
    out, bit = 0, 1
    while bit < bound:
        digit = (a // bit) % 2
        out = out + (1 - digit if b & bit else digit) * bit
        bit *= 2
    return out


def route(ids, homed):
    n = ids.shape[1]
    ids = jnp.broadcast_to(ids, (n, n))
    peer_row = ids // homed
    peer_col = jnp.transpose(ids.astype(F32)).astype(jnp.int32) // homed
    same = peer_row == peer_col
    above = lax.broadcasted_iota(jnp.int32, (n, n), 0)
    along = lax.broadcasted_iota(jnp.int32, (n, n), 1)
    pos_row = jnp.sum(jnp.where(same & (above < along), 1, 0), axis=0, keepdims=True)
    pos_col = jnp.sum(jnp.where(same & (along < above), 1, 0), axis=1, keepdims=True)
    return peer_row[0:1, :], pos_row, peer_col[:, 0:1], pos_col


def as_hot(mask):
    return jnp.where(mask, 1.0, 0.0).astype(BF16)


def pack_kernel(plan, part, ids1, ids2, popular, hosting, x1, x2, down, up, *refs):
    me = lax.axis_index("replica")
    first, arrays = plan.pieces(part, me)
    if part == "near":
        refs = refs[1:]
    outs, (ids, hot_ids, host_id, x, hot, packed, sems, out_sems) = (
        refs[: len(arrays)],
        refs[len(arrays) :],
    )
    count = sum(c for _, c in arrays)
    quarter = plan.width // 4
    loads = [
        pltpu.make_async_copy(popular, hot_ids, sems.at[0]),
        pltpu.make_async_copy(hosting, host_id, sems.at[1]),
        pltpu.make_async_copy(ids1, ids.at[0], sems.at[2]),
        pltpu.make_async_copy(ids2, ids.at[1], sems.at[3]),
    ]
    for c in range(4):
        cols = pl.ds(c * quarter, quarter)
        for b, src in enumerate((x1, x2)):
            loads.append(
                pltpu.make_async_copy(
                    src.at[:, cols],
                    x.at[pl.ds(b * plan.tok, plan.tok), cols],
                    sems.at[4 + 2 * c + b],
                )
            )
    for load in loads:
        load.start()
    loads[0].wait()
    loads[1].wait()
    slot = jnp.int32(0)
    for i in range(hot_ids.shape[0]):
        adapter = hot_ids[i]
        slot = jnp.where(adapter // plan.homed == me, adapter % plan.homed, slot)
    wanted = hot_ids[host_id[0]] // plan.homed
    hots = [
        pltpu.make_async_copy(down.at[slot], hot.at[:, pl.ds(0, plan.width)], sems.at[12]),
        pltpu.make_async_copy(up.at[slot], hot.at[:, pl.ds(plan.width, plan.feature)], sems.at[13]),
    ]
    for load in hots:
        load.start()
    loads[2].wait()
    loads[3].wait()
    peers, cells, slots = [], [], []
    for b in range(2):
        peer, pos, _, _ = route(ids[b], plan.homed)
        peers.append(peer - first)
        cells.append(pos + b * plan.cap)
        slots.append((ids[b] % plan.homed).astype(F32))
    peer, cell = jnp.concatenate(peers, axis=1), jnp.concatenate(cells, axis=1)
    slots = jnp.concatenate(slots, axis=1)
    chunks = plan.row_chunks(count)
    stores = []

    def send(at, size):
        for out, (peer0, n) in zip(outs, arrays):
            stores.append(
                pltpu.make_async_copy(
                    packed.at[pl.ds(pl.multiple_of((peer0 - first) * ROWS, ROWS), n * ROWS),
                              pl.ds(at, size)],
                    out.at[:, pl.ds(at, size)],
                    out_sems.at[len(stores)],
                )
            )
            stores[-1].start()

    masks = []
    for start, size in chunks:
        index = lax.broadcasted_iota(jnp.int32, (size, 2 * plan.tok), 0) + start
        own = index // ROWS == peer
        inner = index % ROWS
        sets = [own & (inner + s * ROWS == cell) for s in range(plan.full)]
        marks = list(sets)
        if plan.rest:
            low = own & (inner + plan.full * ROWS == cell) & (inner < 8)
            high = own & (inner - 8 + plan.full * ROWS == cell) & (inner >= 8)
            sets += [low, high]
            marks.append(low | high)
        masks.append([as_hot(m) for m in sets])
        lane = lax.broadcasted_iota(jnp.int32, (size, LANES), 1)
        meta = jnp.where(lane == plan.sections, wanted.astype(F32), 0.0)
        for s, mark in enumerate(marks):
            value = jnp.sum(jnp.where(mark, slots, 0.0), axis=1, keepdims=True)
            meta = jnp.where(lane == s, value, meta)
        packed[start : start + size, plan.meta_at :] = meta.astype(BF16)

    for c in range(4):
        loads[4 + 2 * c].wait()
        loads[5 + 2 * c].wait()
        cols = slice(c * quarter, (c + 1) * quarter)
        for (start, size), hot_masks in zip(chunks, masks):
            for s in range(plan.full):
                value = jnp.dot(hot_masks[s], x[:, cols], preferred_element_type=F32)
                at = s * plan.width + c * quarter
                packed[start : start + size, at : at + quarter] = value.astype(BF16)
        for s in range(plan.full):
            send(s * plan.width + c * quarter, quarter)
    if plan.rest:
        at = plan.full * plan.width
        for c in range(2):
            for (start, size), hot_masks in zip(chunks, masks):
                both = jnp.concatenate(hot_masks[plan.full :], axis=1)
                source = jnp.concatenate(
                    [
                        x[:, c * quarter : (c + 1) * quarter],
                        x[:, (c + 2) * quarter : (c + 3) * quarter],
                    ],
                    axis=0,
                )
                value = jnp.dot(both, source, preferred_element_type=F32)
                packed[start : start + size, at + c * quarter : at + (c + 1) * quarter] = (
                    value.astype(BF16)
                )
            send(at + c * quarter, quarter)
    for load in hots:
        load.wait()
    for i in range(count):
        peer0, group0 = (i % plan.holders, 0) if part == "all" else (i, first // plan.per_group)
        group = group0 + peer0 // plan.per_group
        col = (peer0 % plan.per_group) * plan.spread
        packed[i * ROWS : (i + 1) * ROWS, plan.tok_cols : plan.meta_at] = hot[
            pl.ds(pl.multiple_of(group * ROWS, ROWS), ROWS), col : col + plan.spread
        ]
    send(plan.tok_cols, plan.spread + LANES)
    for store in stores:
        store.wait()


def home_kernel(plan, parts, down, up, *refs):
    me = lax.axis_index("replica")
    arrays = [a for part in parts for a in plan.pieces(part, me)[1]]
    gots, out, (got, reply, sems, out_sems) = (
        refs[: len(arrays)],
        refs[len(arrays)],
        refs[len(arrays) + 1 :],
    )
    bounds = [(plan.tok_cols, plan.spread + LANES)]
    bounds += [(c, plan.width // 2) for c in range(0, plan.tok_cols, plan.width // 2)]
    loads = []
    for at, size in bounds:
        group = []
        for ref, (peer0, n) in zip(gots, arrays):
            group.append(
                pltpu.make_async_copy(
                    ref.at[:, pl.ds(at, size)],
                    got.at[pl.ds(pl.multiple_of(peer0 * ROWS, ROWS), n * ROWS), pl.ds(at, size)],
                    sems.at[len(loads) * len(arrays) + len(group)],
                )
            )
            group[-1].start()
        loads.append(group)

    def ready(i):
        for load in loads[i]:
            load.wait()

    chunks = plan.row_chunks(plan.peers)
    ready(0)
    metas = []
    for start, n in chunks:
        rows = slice(start, start + n)
        meta = got[rows, plan.meta_at :].astype(F32).astype(jnp.int32)
        metas.append(meta)
        wide = lax.broadcasted_iota(jnp.int32, (n, plan.packed), 1)
        inner = lax.broadcasted_iota(jnp.int32, (n, plan.packed), 0) % ROWS
        pick = as_hot(wide == meta[:, plan.sections : plan.sections + 1] * ROWS + inner)
        reply[rows, : plan.spread] = jnp.dot(
            pick, got[:, plan.tok_cols : plan.meta_at], preferred_element_type=F32
        ).astype(BF16)
    relayed = pltpu.make_async_copy(
        reply.at[:, pl.ds(0, plan.spread)], out.at[:, pl.ds(0, plan.spread)], out_sems.at[0]
    )
    relayed.start()
    half = plan.width // 2
    group = plan.joined
    for s in range(plan.sections):
        at = s * plan.width
        split = s == plan.full
        ready(1 + 2 * s)
        for i, ((start, n), meta) in enumerate(zip(chunks, metas)):
            rows = slice(start, start + n)
            low = lax.dot_general(
                got[rows, at : at + half], down[:, :half], NT, preferred_element_type=F32
            )
            if not split:
                if i == 0:
                    ready(2 + 2 * s)
                low += lax.dot_general(
                    got[rows, at + half : at + plan.width],
                    down[:, half:],
                    NT,
                    preferred_element_type=F32,
                )
                slot = meta[:, s : s + 1]
            else:
                high = lax.dot_general(
                    got[rows, at : at + half], down[:, half:], NT, preferred_element_type=F32
                )
                low = low.reshape(n // ROWS, 2, 8, group)[:, 0]
                high = high.reshape(n // ROWS, 2, 8, group)[:, 1]
                low = (low + high).reshape(n // 2, group)
                slot = meta.reshape(n // ROWS, 2, 8, LANES)[:, 0].reshape(n // 2, LANES)
                slot = slot[:, s : s + 1]
            column = lax.broadcasted_iota(jnp.int32, low.shape, 1) // plan.rank
            kept = jnp.where(column == slot, low, 0.0).astype(BF16)
            delta = jnp.dot(kept, up[...], preferred_element_type=F32)
            to = plan.spread + s * plan.feature
            if split:
                delta = delta.reshape(n // ROWS, 8, plan.feature)
                middle = plan.feature // 2
                delta = jnp.concatenate([delta[..., :middle], delta[..., middle:]], axis=1)
                delta = delta.reshape(n, middle)
            reply[rows, to : to + delta.shape[1]] = delta.astype(BF16)
    answered = pltpu.make_async_copy(
        reply.at[:, pl.ds(plan.spread, plan.back_cols)],
        out.at[:, pl.ds(plan.spread, plan.back_cols)],
        out_sems.at[1],
    )
    answered.start()
    relayed.wait()
    answered.wait()


def final_kernel(plan, ids1, ids2, counts, back, base1, base2, out1, out2, down, up):
    for d in range(plan.holders):
        rows = slice((d // plan.per_group) * ROWS, (d // plan.per_group + 1) * ROWS)
        for j in range(0, plan.spread, LANES):
            col = (d % plan.per_group) * plan.spread + j
            tile = back[d * ROWS : (d + 1) * ROWS, j : j + LANES]
            if col < plan.width:
                down[0, rows, col : col + LANES] = tile
            else:
                up[0, rows, col - plan.width : col - plan.width + LANES] = tile
    index = lax.broadcasted_iota(jnp.int32, (plan.tok, plan.packed), 1)
    inner = index % ROWS
    middle = plan.feature // 2
    for b, (ids, base, out) in enumerate(((ids1, base1, out1), (ids2, base2, out2))):
        _, _, peer, pos = route(ids[...], plan.homed)
        cell = pos + b * plan.cap
        own = index // ROWS == peer
        total = base[...]
        for s in range(plan.full):
            if (b + 1) * plan.cap <= s * ROWS or b * plan.cap >= (s + 1) * ROWS:
                continue
            hot = as_hot(own & (inner + s * ROWS == cell))
            at = plan.spread + s * plan.feature
            total += jnp.dot(hot, back[:, at : at + plan.feature], preferred_element_type=F32)
        if plan.rest and (b + 1) * plan.cap > plan.full * ROWS:
            at = plan.spread + plan.full * plan.feature
            values = back[:, at : at + middle]
            low = as_hot(own & (inner + plan.full * ROWS == cell) & (inner < 8))
            high = as_hot(own & (inner - 8 + plan.full * ROWS == cell) & (inner >= 8))
            total += jnp.concatenate(
                [jnp.dot(hot, values, preferred_element_type=F32) for hot in (low, high)], axis=1
            )
        valid = lax.broadcasted_iota(jnp.int32, total.shape, 0) < counts[b, 0]
        out[...] = jnp.where(valid, total, 0.0).astype(BF16)


def local(
    first_activations,
    second_activations,
    first_adapter_ids,
    second_adapter_ids,
    valid_row_counts,
    popular_adapters,
    replica_hosting,
    value_weight_base,
    adapter_down_factors,
    adapter_up_factors,
):
    tok, width = first_activations.shape
    homed, _, rank = adapter_down_factors.shape
    feature = adapter_up_factors.shape[2]
    plan = Plan(lax.axis_size("replica"), tok, width, rank, feature, homed)
    peers, half = plan.peers, plan.half
    down = jnp.swapaxes(adapter_down_factors, 1, 2)
    ids1 = first_adapter_ids.reshape(1, tok)
    ids2 = second_adapter_ids.reshape(1, tok)
    anywhere = pl.BlockSpec(memory_space=pl.ANY)
    vmem = pl.BlockSpec(memory_space=pltpu.VMEM)
    smem = pl.BlockSpec(memory_space=pltpu.SMEM)
    params = pltpu.CompilerParams(vmem_limit_bytes=60 * 1024 * 1024)

    def pack(part, *after):
        sizes = {"all": [peers], "near": [half], "far": [1] * half}[part]
        return pl.pallas_call(
            functools.partial(pack_kernel, plan, part),
            out_shape=[jax.ShapeDtypeStruct((n * ROWS, plan.cols), BF16) for n in sizes],
            in_specs=[anywhere] * (8 + len(after)),
            out_specs=[anywhere] * len(sizes),
            scratch_shapes=[
                pltpu.VMEM((2, 1, tok), jnp.int32),
                pltpu.SMEM(popular_adapters.shape, jnp.int32),
                pltpu.SMEM(replica_hosting.shape, jnp.int32),
                pltpu.VMEM((2 * tok, width), BF16),
                pltpu.VMEM((rank, width + feature), BF16),
                pltpu.VMEM((sum(sizes) * ROWS, plan.cols), BF16),
                pltpu.SemaphoreType.DMA((14,)),
                pltpu.SemaphoreType.DMA((len(sizes) * (4 * plan.full + 2 * plan.rest + 1),)),
            ],
            compiler_params=params,
            name="pack_" + part,
        )(
            ids1,
            ids2,
            popular_adapters,
            replica_hosting,
            first_activations,
            second_activations,
            down,
            adapter_up_factors,
            *after,
        )

    def exchange(x, n, **kwargs):
        x = x.reshape(n, x.shape[0] // n, x.shape[1])
        x = lax.all_to_all(x, "replica", split_axis=0, concat_axis=0, tiled=True, **kwargs)
        return x.reshape(n * x.shape[1], x.shape[2])

    if plan.split:
        parts = ("far", "near")
        gots = []
        far = pack("far")
        for m, block in enumerate(far):
            pairs = [(i, i ^ (m + half)) for i in range(peers)]
            gots.append(lax.ppermute(block, "replica", pairs))
        halves = [list(range(half)), list(range(half, peers))]
        near, _ = lax.optimization_barrier((pack("near", far[0])[0], gots[0]))
        gots.append(exchange(near, half, axis_index_groups=halves))
    else:
        parts = ("all",)
        gots = [exchange(pack("all")[0], peers)]
    base1 = jnp.dot(first_activations, value_weight_base, preferred_element_type=F32)
    base2 = jnp.dot(second_activations, value_weight_base, preferred_element_type=F32)
    pieces = (1 + 2 * plan.full + plan.rest) * len(gots)
    reply = pl.pallas_call(
        functools.partial(home_kernel, plan, parts),
        out_shape=jax.ShapeDtypeStruct((plan.packed, plan.ret_cols), BF16),
        in_specs=[vmem, vmem] + [anywhere] * len(gots),
        out_specs=anywhere,
        scratch_shapes=[
            pltpu.VMEM((plan.packed, plan.cols), BF16),
            pltpu.VMEM((plan.packed, plan.ret_cols), BF16),
            pltpu.SemaphoreType.DMA((pieces,)),
            pltpu.SemaphoreType.DMA((2,)),
        ],
        compiler_params=params,
        name="home",
    )(
        down.reshape(plan.joined, width),
        adapter_up_factors.reshape(plan.joined, feature),
        *gots,
    )
    out1, out2, resident_down, resident_up = pl.pallas_call(
        functools.partial(final_kernel, plan),
        out_shape=[
            jax.ShapeDtypeStruct((tok, feature), BF16),
            jax.ShapeDtypeStruct((tok, feature), BF16),
            jax.ShapeDtypeStruct((1, rank, width), BF16),
            jax.ShapeDtypeStruct((1, rank, feature), BF16),
        ],
        in_specs=[vmem, vmem, smem, vmem, vmem, vmem],
        out_specs=[vmem] * 4,
        compiler_params=params,
        name="finish",
    )(ids1, ids2, valid_row_counts, exchange(reply, peers), base1, base2)
    return out1, out2, jnp.swapaxes(resident_down, 1, 2), resident_up


def solution(mesh):
    return jax.shard_map(
        local,
        mesh=mesh,
        in_specs=(
            P(("groups", "replica"), None),
            P(("groups", "replica"), None),
            P(("groups", "replica")),
            P(("groups", "replica")),
            P(None, ("groups", "replica")),
            P("groups"),
            P(("groups", "replica")),
            P(),
            P("replica", None, None),
            P("replica", None, None),
        ),
        out_specs=(
            P(("groups", "replica"), None),
            P(("groups", "replica"), None),
            P(("groups", "replica"), None, None),
            P(("groups", "replica"), None, None),
        ),
        check_vma=False,
    )
```

time: 995 us -> 136 us (0.14)
  waiting for transfers between devices: 790 us -> 15.9 us
  blocking collectives: 0 us -> 93.1 us
  local copies, waits for them, and re-layouts: 72.1 us -> 1.63 us
  other arithmetic: 46.7 us -> 0 us
  starting transfers between devices: 35.2 us -> 3.79 us
  loops' own time: 21.7 us -> 0 us
  Pallas kernels: 0 us -> 14 us
  between operations: 14.9 us -> 1.32 us
    psum x8 -> x0, waiting for transfers between devices: 743 us -> none  [from_root(): return lax.psum(block, axis)]
    all_to_all x0 -> x1, blocking collectives: none -> 93.1 us  [exchange(): lax.all_to_all(x, 'replica', split_axis=0, concat_axis=0, tiled=True, **k...]
    all_to_all x6 -> x1, waiting for transfers between devices: 47.1 us -> 15.9 us  [exchange(): lax.all_to_all(x, 'replica', split_axis=0, concat_axis=0, tiled=True, **k...]
    all_to_all x6 -> x1, starting transfers between devices: 34.8 us -> 3.79 us  [exchange(): lax.all_to_all(x, 'replica', split_axis=0, concat_axis=0, tiled=True, **k...]
    another operation x18 -> x0, other arithmetic: 21.9 us -> none
    another operation x1 -> x0, loops' own time: 21.7 us -> none  [local(): got_down, got_up = lax.fori_loop(0, hot_count, fetch, start)]
    dynamic_slice x26 -> x0, local copies, waits for them, and re-layouts: 19.7 us -> none  [the longest x16 12.5 us: fetch(): lax.dynamic_index_in_dim(adapter_down_factors, inside_limit, 0, keepdims=...]
    scatter x20 -> x0, local copies, waits for them, and re-layouts: 18.6 us -> none  [the longest x16 9.39 us: fetch(): stacks[0].at[hot_index].set(got_down)]
  transfers between devices with their start and end apart: 14 -> 1, of which waited for: 13 -> 1; matrix products, arithmetic and copies ran while one was open for 12% -> 4% of each run, Pallas kernels for 0% -> 0%
where the time goes in v2:
time: 136 us; the launch traced here: 135 us
  blocking collectives  93.1 us (68%)
  waiting for transfers between devices  15.9 us (12%)
  Pallas kernels  14 us (10%)
  matrix products  5.26 us (4%)
  starting transfers between devices  3.79 us (3%)
  local copies, waits for them, and re-layouts  1.63 us (1%)
    all_to_all x1, blocking collectives, exchange(): lax.all_to_all(x, 'replica', split_axis=0, concat_axis=0, tiled=True, **k...  93.1 us
    all_to_all x1, waiting for transfers between devices, exchange(): lax.all_to_all(x, 'replica', split_axis=0, concat_axis=0, tiled=True, **k...  15.9 us
    pallas_call x1, Pallas kernels, local(): pl.pallas_call(functools.partial(home_kernel, plan, parts), out_shape=jax...  7.11 us
    pallas_call x1, Pallas kernels, pack(): pl.pallas_call(functools.partial(pack_kernel, plan, part), out_shape=[jax...  4.12 us
    all_to_all x1, starting transfers between devices, exchange(): lax.all_to_all(x, 'replica', split_axis=0, concat_axis=0, tiled=True, **k...  3.79 us
    dot_general x1, matrix products, local(): jnp.dot(first_activations, value_weight_base, preferred_element_type=F32)  3.76 us
    pallas_call x1, Pallas kernels, local(): pl.pallas_call(functools.partial(final_kernel, plan), out_shape=[jax.Shap...  2.74 us
  transfers between devices with their start and end apart: 1, of which 1 were waited for; matrix products, arithmetic and copies ran while one was open for 4% of the time, Pallas kernels for 0%

profile of v2, /device:TPU:0, one launch (start us, length us, event | category | flops | bytes accessed | tf_op | source)
XLA Modules:
  0.0 135.0 jit_solution(15717147335921952090)
XLA Ops:
  1.3 4.1 %pack_all.1 = bf16[256,7424]{1,0:T(8,128)(2,1)} custom-call(s32[1,128]{1,0:T(1,128)} %bitcast.22, s32[1,128]{1,0:T(1,128)} %bitcast.24, s32[8]{0:T(128)} %popular.1, s32[1]{0:T(128)S(6)} %copy.15.hosting, bf16[128,4096]{1,0:T(8,128)(2,1)} %x1.1, bf16[128,4096]{1,0:T(8,128)(2,1)} %x2.1, bf16[4,64,4096]{2,1,0:T(8,128)(2,1)} %bitcast.17, bf16[4,64,512]{2,1,0:T(8,128)(2,1)} %up.1), custom_call_target="tpu_custom_call" | custom-call | tf_op jit(solution)/shard_map/pack_all/pallas_call | solution.py:376
  5.4 93.1 %all_to_all.10 = bf16[16,16,7424]{2,1,0:T(8,128)(2,1)} all-to-all(bf16[16,16,7424]{2,1,0:T(8,128)(2,1)} %bitcast.15), channel_id=1, replica_groups=mesh['groups'=2,'replica'=16] {'replica'}, dimensions={0} | all-to-all | bytes 7602176 | tf_op jit(solution)/shard_map/all_to_all | solution.py:407
  98.5 0.0 copy-start.4
  98.5 0.0 copy-start.1
  98.5 7.1 %home.1 = bf16[256,1920]{1,0:T(8,128)(2,1)} custom-call(bf16[256,4096]{1,0:T(8,128)(2,1)} %bitcast.18, bf16[256,512]{1,0:T(8,128)(2,1)} %bitcast.21, bf16[256,7424]{1,0:T(8,128)(2,1)} %bitcast.16), custom_call_target="tpu_custom_call" | custom-call | tf_op jit(solution)/shard_map/home/pallas_call | solution.py:426
  105.7 0.0 copy-start.2
  105.7 3.8 %all-to-all-start.1 = ((bf16[16,16,1920]{2,1,0:T(8,128)(2,1)}), bf16[16,16,1920]{2,1,0:T(8,128)(2,1)S(1)}, u32[]{:S(2)}, u32[]{:S(2)}) async-start(bf16[16,16,1920]{2,1,0:T(8,128)(2,1)} %bitcast.19), calls=%async_computation.1 | async-start | bytes 1966080 | tf_op jit(solution)/shard_map/all_to_all | solution.py:407
  109.5 0.0 copy-done.4
  109.5 0.7 copy.14.counts
  110.2 0.0 copy-done.1
  110.2 0.0 copy-start
  110.2 3.8 %fusion.base1 = f32[128,512]{1,0:T(8,128)} fusion(bf16[128,4096]{1,0:T(8,128)(2,1)S(1)} %copy-done.1, bf16[4096,512]{1,0:T(8,128)(2,1)} %param.17), kind=kOutput, calls=%fused_computation | convolution fusion | flops 536870912 | bytes 5505024 | tf_op jit(solution)/shard_map/dot_general | solution.py:423
  113.9 0.0 copy-done.2
  113.9 0.0 copy-done
  113.9 1.5 %fusion.1.base2 = f32[128,512]{1,0:T(8,128)} fusion(bf16[128,4096]{1,0:T(8,128)(2,1)S(1)} %copy-done.2, bf16[4096,512]{1,0:T(8,128)(2,1)S(1)} %copy-done), kind=kOutput, calls=%fused_computation.1 | convolution fusion | flops 536870912 | bytes 5505024 | tf_op jit(solution)/shard_map/dot_general | solution.py:424
  115.4 15.9 %all-to-all-done.1 = bf16[16,16,1920]{2,1,0:T(8,128)(2,1)S(1)} async-done(((bf16[16,16,1920]{2,1,0:T(8,128)(2,1)}), bf16[16,16,1920]{2,1,0:T(8,128)(2,1)S(1)}, u32[]{:S(2)}, u32[]{:S(2)}) %all-to-all-start.1) | async-done | bytes 983072 | tf_op jit(solution)/shard_map/all_to_all | solution.py:407
  131.3 0.0 copy-start.3
  131.3 0.9 copy-done.3
  132.2 2.7 %finish.1 = (bf16[128,512]{1,0:T(8,128)(2,1)}, bf16[128,512]{1,0:T(8,128)(2,1)}, bf16[1,64,4096]{2,1,0:T(8,128)(2,1)}, bf16[1,64,512]{2,1,0:T(8,128)(2,1)}) custom-call(s32[1,128]{1,0:T(1,128)} %bitcast.23, s32[1,128]{1,0:T(1,128)} %bitcast.25, s32[2,1]{1,0:T(2,128)} %copy.14.counts, bf16[256,1920]{1,0:T(8,128)(2,1)} %bitcast.20, f32[128,512]{1,0:T(8,128)} %fusion.base1, ...), custom_call_target="tpu_custom_call" | custom-call | tf_op jit(solution)/shard_map/finish/pallas_call | solution.py:444
Async XLA Ops:
  98.5 10.9 %copy-start.4 = (s32[2,1]{0,1:T(1,128)S(1)}, s32[2,1]{0,1:T(1,128)}, u32[]{:S(2)}) copy-start(s32[2,1]{0,1:T(1,128)} %param.14) | copy-start | bytes 28
  98.5 11.6 %copy-start.1 = (bf16[128,4096]{1,0:T(8,128)(2,1)S(1)}, bf16[128,4096]{1,0:T(8,128)(2,1)}, u32[]{:S(2)}) copy-start(bf16[128,4096]{1,0:T(8,128)(2,1)} %x1.1) | copy-start | bytes 3145732
  105.7 8.3 %copy-start.2 = (bf16[128,4096]{1,0:T(8,128)(2,1)S(1)}, bf16[128,4096]{1,0:T(8,128)(2,1)}, u32[]{:S(2)}) copy-start(bf16[128,4096]{1,0:T(8,128)(2,1)} %x2.1) | copy-start | bytes 3145732
  105.7 25.6 %all-to-all-start.1 = ((bf16[16,16,1920]{2,1,0:T(8,128)(2,1)}), bf16[16,16,1920]{2,1,0:T(8,128)(2,1)S(1)}, u32[]{:S(2)}, u32[]{:S(2)}) async-start(bf16[16,16,1920]{2,1,0:T(8,128)(2,1)} %bitcast.19), calls=%async_computation.1 | async-start | bytes 1966080 | tf_op jit(solution)/shard_map/all_to_all | solution.py:407
  110.2 3.8 %copy-start = (bf16[4096,512]{1,0:T(8,128)(2,1)S(1)}, bf16[4096,512]{1,0:T(8,128)(2,1)}, u32[]{:S(2)}) copy-start(bf16[4096,512]{1,0:T(8,128)(2,1)} %param.17) | copy-start | bytes 12582916
  131.3 0.9 copy-start.3

commit v3 on v2

--- a/solution.py
+++ b/solution.py
@@ -42,31 +42,10 @@
         self.meta_at = self.tok_cols + self.spread
         self.cols = self.meta_at + LANES
         self.ret_cols = self.spread + self.back_cols
-        self.half = peers // 2
-        self.split = False and peers & (peers - 1) == 0 and self.half % self.per_group == 0
-
-    def pieces(self, part, me):
-        if part == "all":
-            return 0, [(0, self.peers)]
-        mine = (me // self.half) * self.half
-        if part == "near":
-            return mine, [(mine, self.half)]
-        far = self.half - mine
-        partner = me - mine
-        return far, [(far + xor(partner, m, self.half), 1) for m in range(self.half)]
 
     def row_chunks(self, count):
         size = min(CHUNK, count * ROWS)
         return [(i, size) for i in range(0, count * ROWS, size)]
-
-
-def xor(a, b, bound):
-    out, bit = 0, 1
-    while bit < bound:
-        digit = (a // bit) % 2
-        out = out + (1 - digit if b & bit else digit) * bit
-        bit *= 2
-    return out
 
 
 def route(ids, homed):
@@ -86,16 +65,10 @@
     return jnp.where(mask, 1.0, 0.0).astype(BF16)
 
 
-def pack_kernel(plan, part, ids1, ids2, popular, hosting, x1, x2, down, up, *refs):
+def pack_kernel(plan, ids1, ids2, popular, hosting, x1, x2, down, up, out, *scratch):
+    ids, hot_ids, host_id, x, hot, packed, sems, out_sems = scratch
     me = lax.axis_index("replica")
-    first, arrays = plan.pieces(part, me)
-    if part == "near":
-        refs = refs[1:]
-    outs, (ids, hot_ids, host_id, x, hot, packed, sems, out_sems) = (
-        refs[: len(arrays)],
-        refs[len(arrays) :],
-    )
-    count = sum(c for _, c in arrays)
+    count = plan.peers
     quarter = plan.width // 4
     loads = [
         pltpu.make_async_copy(popular, hot_ids, sems.at[0]),
@@ -133,7 +106,7 @@
     peers, cells, slots = [], [], []
     for b in range(2):
         peer, pos, _, _ = route(ids[b], plan.homed)
-        peers.append(peer - first)
+        peers.append(peer)
         cells.append(pos + b * plan.cap)
         slots.append((ids[b] % plan.homed).astype(F32))
     peer, cell = jnp.concatenate(peers, axis=1), jnp.concatenate(cells, axis=1)
@@ -142,16 +115,11 @@
     stores = []
 
     def send(at, size):
-        for out, (peer0, n) in zip(outs, arrays):
-            stores.append(
-                pltpu.make_async_copy(
-                    packed.at[pl.ds(pl.multiple_of((peer0 - first) * ROWS, ROWS), n * ROWS),
-                              pl.ds(at, size)],
-                    out.at[:, pl.ds(at, size)],
-                    out_sems.at[len(stores)],
-                )
-            )
-            stores[-1].start()
+        cols = pl.ds(at, size)
+        stores.append(
+            pltpu.make_async_copy(packed.at[:, cols], out.at[:, cols], out_sems.at[len(stores)])
+        )
+        stores[-1].start()
 
     masks = []
     for start, size in chunks:
@@ -204,44 +172,29 @@
     for load in hots:
         load.wait()
     for i in range(count):
-        peer0, group0 = (i % plan.holders, 0) if part == "all" else (i, first // plan.per_group)
-        group = group0 + peer0 // plan.per_group
-        col = (peer0 % plan.per_group) * plan.spread
+        group, col = divmod(i % plan.holders, plan.per_group)
+        col *= plan.spread
         packed[i * ROWS : (i + 1) * ROWS, plan.tok_cols : plan.meta_at] = hot[
-            pl.ds(pl.multiple_of(group * ROWS, ROWS), ROWS), col : col + plan.spread
+            group * ROWS : (group + 1) * ROWS, col : col + plan.spread
         ]
     send(plan.tok_cols, plan.spread + LANES)
     for store in stores:
         store.wait()
 
 
-def home_kernel(plan, parts, down, up, *refs):
-    me = lax.axis_index("replica")
-    arrays = [a for part in parts for a in plan.pieces(part, me)[1]]
-    gots, out, (got, reply, sems, out_sems) = (
-        refs[: len(arrays)],
-        refs[len(arrays)],
-        refs[len(arrays) + 1 :],
-    )
+def home_kernel(plan, down, up, source, out, got, reply, sems, out_sems):
     bounds = [(plan.tok_cols, plan.spread + LANES)]
     bounds += [(c, plan.width // 2) for c in range(0, plan.tok_cols, plan.width // 2)]
     loads = []
     for at, size in bounds:
-        group = []
-        for ref, (peer0, n) in zip(gots, arrays):
-            group.append(
-                pltpu.make_async_copy(
-                    ref.at[:, pl.ds(at, size)],
-                    got.at[pl.ds(pl.multiple_of(peer0 * ROWS, ROWS), n * ROWS), pl.ds(at, size)],
-                    sems.at[len(loads) * len(arrays) + len(group)],
-                )
-            )
-            group[-1].start()
-        loads.append(group)
+        cols = pl.ds(at, size)
+        loads.append(
+            pltpu.make_async_copy(source.at[:, cols], got.at[:, cols], sems.at[len(loads)])
+        )
+        loads[-1].start()
 
     def ready(i):
-        for load in loads[i]:
-            load.wait()
+        loads[i].wait()
 
     chunks = plan.row_chunks(plan.peers)
     ready(0)
@@ -346,6 +299,368 @@
         out[...] = jnp.where(valid, total, 0.0).astype(BF16)
 
 
+class Wide:
+    def __init__(self, plan, groups):
+        self.peers, self.tok, self.width, self.rank = plan.peers, plan.tok, plan.width, plan.rank
+        self.feature, self.homed, self.groups = plan.feature, plan.homed, groups
+        self.half = self.peers // 2
+        self.per = 2 * plan.cap
+        self.sections = -(-2 * self.per // ROWS)
+        self.packed = self.half * ROWS
+        self.tok_cols = self.sections * self.width
+        self.factor = self.width + self.feature
+        col_tiles = self.factor // LANES
+        tiles = (self.rank // ROWS) * col_tiles
+        self.share = tiles // max(self.half, 1)
+        self.spread = self.share * LANES
+        self.meta_at = self.tok_cols + self.spread
+        self.cols = self.meta_at + LANES
+        self.back_cols = self.sections * self.feature
+        self.ret_cols = self.back_cols + self.spread
+        self.per_group = col_tiles // max(self.share, 1)
+        self.cut = self.rank // 2
+        self.fits = (
+            groups == 2
+            and self.half > 0
+            and self.peers & (self.peers - 1) == 0
+            and self.peers <= 16
+            and tiles % self.half == 0
+            and self.share > 0
+            and col_tiles % self.share == 0
+            and self.homed > 2
+            and self.cut % ROWS == 0
+        )
+
+    def chunks(self, group):
+        return [(a, group) for a in range(self.homed)] + [(self.homed - 1, 1 - group)]
+
+    def place(self, j):
+        group, col = divmod(j, self.per_group)
+        return group * ROWS, col * self.spread
+
+
+def cut_kernel(plan, popular, other, down, up, *refs):
+    outs, (hot_ids, hot_sems, sems) = refs[:-3], refs[-3:]
+    me, group = lax.axis_index("replica"), lax.axis_index("groups")
+    order = travel_order(plan, me, popular, other, hot_ids, hot_sems)
+    copies = []
+    for (place, part), out in zip(plan.chunks(group), outs):
+        rows = pl.ds(pl.multiple_of(part * plan.cut, ROWS), plan.cut)
+        for src, cols in (
+            (down, pl.ds(0, plan.width)),
+            (up, pl.ds(plan.width, plan.feature)),
+        ):
+            copies.append(
+                pltpu.make_async_copy(
+                    src.at[order[place], rows], out.at[:, cols], sems.at[len(copies)]
+                )
+            )
+    for copy in copies:
+        copy.start()
+    for copy in copies:
+        copy.wait()
+
+
+def travel_order(plan, home, popular, other, hot_ids, sems):
+    loads = [
+        pltpu.make_async_copy(src, hot_ids.at[i], sems.at[i])
+        for i, src in enumerate((popular, other))
+    ]
+    for load in loads:
+        load.start()
+    for load in loads:
+        load.wait()
+    cold = [jnp.int32(1)] * plan.homed
+    for g in range(2):
+        for i in range(hot_ids.shape[1]):
+            for a in range(plan.homed):
+                cold[a] = jnp.where(hot_ids[g, i] == home * plan.homed + a, 0, cold[a])
+    order = [jnp.int32(0)] * plan.homed
+    for a in range(plan.homed):
+        rank = jnp.int32(0)
+        for b in range(plan.homed):
+            if b != a:
+                ahead = cold[b] <= cold[a] if b < a else cold[b] < cold[a]
+                rank = rank + jnp.where(ahead, 1, 0)
+        for c in range(plan.homed):
+            order[c] = jnp.where(rank == c, a, order[c])
+    return order
+
+
+def mirror_of(plan, me):
+    return me + plan.half - 2 * plan.half * (me // plan.half)
+
+
+def hot_slot(popular, homed, home):
+    slot = jnp.int32(0)
+    for i in range(popular.shape[0]):
+        adapter = popular[i]
+        slot = jnp.where(adapter // homed == home, adapter % homed, slot)
+    return slot
+
+
+def near_pack_kernel(plan, ids1, ids2, popular, hosting, x1, x2, down, up, out, *scratch):
+    ids, hot_ids, host_id, x, packed, sems, out_sems, hot_sems = scratch
+    me = lax.axis_index("replica")
+    side = me // plan.half
+    quarter = plan.width // 4
+    loads = [
+        pltpu.make_async_copy(popular, hot_ids, sems.at[0]),
+        pltpu.make_async_copy(hosting, host_id, sems.at[1]),
+        pltpu.make_async_copy(ids1, ids.at[0], sems.at[2]),
+        pltpu.make_async_copy(ids2, ids.at[1], sems.at[3]),
+    ]
+    for c in range(4):
+        cols = pl.ds(c * quarter, quarter)
+        for b, src in enumerate((x1, x2)):
+            loads.append(
+                pltpu.make_async_copy(
+                    src.at[:, cols],
+                    x.at[pl.ds(b * plan.tok, plan.tok), cols],
+                    sems.at[4 + 2 * c + b],
+                )
+            )
+    for load in loads:
+        load.start()
+    for load in loads[:4]:
+        load.wait()
+    slot = hot_slot(hot_ids, plan.homed, me)
+    hots = []
+    for j in range(plan.half):
+        row, col = plan.place(j)
+        rows, to = pl.ds(row, ROWS), pl.ds(j * ROWS, ROWS)
+        inside = min(plan.spread, max(plan.width - col, 0))
+        if inside:
+            hots.append((down.at[slot, rows, pl.ds(col, inside)], to, 0, inside))
+        if inside < plan.spread:
+            from_up = pl.ds(col + inside - plan.width, plan.spread - inside)
+            hots.append((up.at[slot, rows, from_up], to, inside, plan.spread - inside))
+    stores = []
+    for i, (src, to, at, size) in enumerate(hots):
+        hots[i] = pltpu.make_async_copy(
+            src, packed.at[to, pl.ds(plan.tok_cols + at, size)], hot_sems.at[i]
+        )
+        hots[i].start()
+    wanted = hot_ids[host_id[0]] // plan.homed
+    wanted = wanted % plan.half + jnp.where(wanted // plan.half == side, 0, plan.half)
+    peers, cells, slots = [], [], []
+    for b in range(2):
+        home = ids[b] // plan.homed
+        peer, pos, _, _ = route(home % plan.half, 1)
+        peers.append(peer)
+        cells.append(pos + b * plan.per)
+        far = jnp.where(home // plan.half == side, 0, plan.homed)
+        slots.append((ids[b] % plan.homed + far).astype(F32))
+    peer, cell = jnp.concatenate(peers, axis=1), jnp.concatenate(cells, axis=1)
+    slots = jnp.concatenate(slots, axis=1)
+    index = lax.broadcasted_iota(jnp.int32, (plan.packed, 2 * plan.tok), 0)
+    own = index // ROWS == peer
+    inner = index % ROWS
+    lane = lax.broadcasted_iota(jnp.int32, (plan.packed, LANES), 1)
+    meta = jnp.where(lane == plan.sections, wanted.astype(F32), 0.0)
+    masks = []
+    for s in range(plan.sections):
+        mark = own & (inner + s * ROWS == cell)
+        masks.append(as_hot(mark))
+        value = jnp.sum(jnp.where(mark, slots, 0.0), axis=1, keepdims=True)
+        meta = jnp.where(lane == s, value, meta)
+    mask = jnp.concatenate(masks, axis=0)
+    packed[:, plan.meta_at :] = meta.astype(BF16)
+
+    def send(at, size):
+        stores.append(
+            pltpu.make_async_copy(
+                packed.at[:, pl.ds(at, size)],
+                out.at[:, pl.ds(at, size)],
+                out_sems.at[len(stores)],
+            )
+        )
+        stores[-1].start()
+
+    for c in range(4):
+        loads[4 + 2 * c].wait()
+        loads[5 + 2 * c].wait()
+        value = jnp.dot(
+            mask, x[:, c * quarter : (c + 1) * quarter], preferred_element_type=F32
+        ).astype(BF16)
+        for s in range(plan.sections):
+            at = s * plan.width + c * quarter
+            packed[:, at : at + quarter] = value[s * plan.packed : (s + 1) * plan.packed]
+            send(at, quarter)
+        if c == 0:
+            for load in hots:
+                load.wait()
+            send(plan.tok_cols, plan.spread + LANES)
+    for store in stores:
+        store.wait()
+
+
+def near_home_kernel(plan, got, popular, other, down, up, *refs):
+    count = plan.homed
+    arrays, out = refs[: 2 * count], refs[2 * count]
+    x, meta, weights, ups, hot_ids, sems, hot_sems = refs[2 * count + 1 :]
+    group = lax.axis_index("groups")
+    pieces, joined = 4, plan.homed * plan.rank
+    size = plan.width // pieces
+    used = []
+
+    def load(src, dst):
+        used.append(pltpu.make_async_copy(src, dst, sems.at[len(used)]))
+        used[-1].start()
+        return used[-1]
+
+    order = travel_order(
+        plan, mirror_of(plan, lax.axis_index("replica")), popular, other, hot_ids, hot_sems
+    )
+    first = [load(got.at[:, pl.ds(plan.meta_at, LANES)], meta)]
+    far = []
+    halves = plan.chunks(group) + plan.chunks(1 - group)[: count - 1]
+    for (place, part), array in zip(halves, arrays):
+        at = joined + order[place] * plan.rank + part * plan.cut
+        far.append((array, pl.ds(pl.multiple_of(at, ROWS), plan.cut)))
+    steps = []
+    for c in range(pieces):
+        cols = pl.ds(c * size, size)
+        step = []
+        for s in range(plan.sections):
+            step.append(
+                load(
+                    got.at[:, pl.ds(s * plan.width + c * size, size)],
+                    x.at[pl.ds(s * plan.packed, plan.packed), cols],
+                )
+            )
+        step.append(load(down.at[:, cols], weights.at[pl.ds(0, joined), cols]))
+        for array, rows in far:
+            step.append(load(array.at[:, cols], weights.at[rows, cols]))
+        steps.append(step)
+    first.append(load(up, ups.at[pl.ds(0, joined)]))
+    for array, rows in far:
+        first.append(load(array.at[:, pl.ds(plan.width, plan.feature)], ups.at[rows]))
+    total = None
+    for c, step in enumerate(steps):
+        for copy in step:
+            copy.wait()
+        cols = slice(c * size, (c + 1) * size)
+        term = lax.dot_general(x[:, cols], weights[:, cols], NT, preferred_element_type=F32)
+        total = term if total is None else total + term
+    for copy in first:
+        copy.wait()
+    slots = meta[...].astype(F32).astype(jnp.int32)
+    slots = jnp.concatenate([slots[:, s : s + 1] for s in range(plan.sections)], axis=0)
+    column = lax.broadcasted_iota(jnp.int32, total.shape, 1) // plan.rank
+    kept = jnp.where(column == slots, total, 0.0).astype(BF16)
+    delta = jnp.dot(kept, ups[...], preferred_element_type=F32).astype(BF16)
+    for s in range(plan.sections):
+        out[:, s * plan.feature : (s + 1) * plan.feature] = delta[
+            s * plan.packed : (s + 1) * plan.packed
+        ]
+
+
+def far_hot_kernel(plan, popular, other, *refs):
+    out, hot_ids, hot_sems, sems = refs[-4:]
+    count = 2
+    crossed, swapped = refs[:count], refs[count : 2 * count]
+    mirror = mirror_of(plan, lax.axis_index("replica"))
+    group = lax.axis_index("groups")
+    order = travel_order(plan, mirror, popular, other, hot_ids, hot_sems)
+    second = hot_slot(hot_ids.at[0], plan.homed, mirror) == order[1]
+    for place in range(2):
+        for g in range(2):
+
+            @pl.when((second if place else ~second) & (group == g))
+            def _():
+                copies = []
+                for j in range(plan.half):
+                    row, col = plan.place(j)
+                    part, row = divmod(row, plan.cut)
+                    src = (crossed if part == g else swapped)[place]
+                    copies.append(
+                        pltpu.make_async_copy(
+                            src.at[pl.ds(row, ROWS), pl.ds(col, plan.spread)],
+                            out.at[pl.ds(j * ROWS, ROWS)],
+                            sems.at[j],
+                        )
+                    )
+                    copies[-1].start()
+                for copy in copies:
+                    copy.wait()
+
+
+def relay_kernel(plan, got, far, reply, out, held, meta, sems):
+    copies = [
+        pltpu.make_async_copy(got.at[:, pl.ds(plan.meta_at, LANES)], meta, sems.at[0]),
+        pltpu.make_async_copy(
+            got.at[:, pl.ds(plan.tok_cols, plan.spread)],
+            held.at[pl.ds(0, plan.packed)],
+            sems.at[1],
+        ),
+        pltpu.make_async_copy(far, held.at[pl.ds(plan.packed, plan.packed)], sems.at[2]),
+        pltpu.make_async_copy(reply, out.at[:, pl.ds(0, plan.back_cols)], sems.at[3]),
+    ]
+    for copy in copies:
+        copy.start()
+    for copy in copies[:3]:
+        copy.wait()
+    wanted = meta[...].astype(F32).astype(jnp.int32)[:, plan.sections : plan.sections + 1]
+    shape = (plan.packed, 2 * plan.packed)
+    inner = lax.broadcasted_iota(jnp.int32, shape, 0) % ROWS
+    pick = as_hot(lax.broadcasted_iota(jnp.int32, shape, 1) == wanted * ROWS + inner)
+    out[:, plan.back_cols :] = jnp.dot(
+        pick, held[...], preferred_element_type=F32
+    ).astype(BF16)
+    copies[3].wait()
+
+
+def near_final_kernel(plan, ids1, ids2, counts, back, base1, base2, out1, out2, down, up):
+    for j in range(plan.half):
+        row, first = plan.place(j)
+        rows = slice(row, row + ROWS)
+        for at in range(0, plan.spread, LANES):
+            col = first + at
+            start = plan.back_cols + at
+            tile = back[j * ROWS : (j + 1) * ROWS, start : start + LANES]
+            if col < plan.width:
+                down[0, rows, col : col + LANES] = tile
+            else:
+                up[0, rows, col - plan.width : col - plan.width + LANES] = tile
+    index = lax.broadcasted_iota(jnp.int32, (plan.tok, plan.packed), 1)
+    inner = index % ROWS
+    for b, (ids, base, out) in enumerate(((ids1, base1, out1), (ids2, base2, out2))):
+        _, _, peer, pos = route((ids[...] // plan.homed) % plan.half, 1)
+        cell = pos + b * plan.per
+        own = index // ROWS == peer
+        total = base[...]
+        for s in range(plan.sections):
+            if (b + 1) * plan.per <= s * ROWS or b * plan.per >= (s + 1) * ROWS:
+                continue
+            hot = as_hot(own & (inner + s * ROWS == cell))
+            at = s * plan.feature
+            total += jnp.dot(hot, back[:, at : at + plan.feature], preferred_element_type=F32)
+        valid = lax.broadcasted_iota(jnp.int32, total.shape, 0) < counts[b, 0]
+        out[...] = jnp.where(valid, total, 0.0).astype(BF16)
+
+
+def call(kernel, name, out_shape, operands, in_specs, out_specs, scratch=(), cost=0):
+    return pl.pallas_call(
+        kernel,
+        out_shape=out_shape,
+        in_specs=in_specs,
+        out_specs=out_specs,
+        scratch_shapes=list(scratch),
+        compiler_params=pltpu.CompilerParams(vmem_limit_bytes=60 * 1024 * 1024),
+        cost_estimate=pl.CostEstimate(flops=0, bytes_accessed=cost, transcendentals=0)
+        if cost
+        else None,
+        name=name,
+    )(*operands)
+
+
+def exchange(x, n, **kwargs):
+    x = x.reshape(n, x.shape[0] // n, x.shape[1])
+    x = lax.all_to_all(x, "replica", split_axis=0, concat_axis=0, tiled=True, **kwargs)
+    return x.reshape(n * x.shape[1], x.shape[2])
+
+
 def local(
     first_activations,
     second_activations,
@@ -362,98 +677,159 @@
     homed, _, rank = adapter_down_factors.shape
     feature = adapter_up_factors.shape[2]
     plan = Plan(lax.axis_size("replica"), tok, width, rank, feature, homed)
-    peers, half = plan.peers, plan.half
+    wide = Wide(plan, lax.axis_size("groups"))
     down = jnp.swapaxes(adapter_down_factors, 1, 2)
+    up = adapter_up_factors
     ids1 = first_adapter_ids.reshape(1, tok)
     ids2 = second_adapter_ids.reshape(1, tok)
     anywhere = pl.BlockSpec(memory_space=pl.ANY)
     vmem = pl.BlockSpec(memory_space=pltpu.VMEM)
     smem = pl.BlockSpec(memory_space=pltpu.SMEM)
-    params = pltpu.CompilerParams(vmem_limit_bytes=60 * 1024 * 1024)
-
-    def pack(part, *after):
-        sizes = {"all": [peers], "near": [half], "far": [1] * half}[part]
-        return pl.pallas_call(
-            functools.partial(pack_kernel, plan, part),
-            out_shape=[jax.ShapeDtypeStruct((n * ROWS, plan.cols), BF16) for n in sizes],
-            in_specs=[anywhere] * (8 + len(after)),
-            out_specs=[anywhere] * len(sizes),
-            scratch_shapes=[
-                pltpu.VMEM((2, 1, tok), jnp.int32),
-                pltpu.SMEM(popular_adapters.shape, jnp.int32),
-                pltpu.SMEM(replica_hosting.shape, jnp.int32),
-                pltpu.VMEM((2 * tok, width), BF16),
-                pltpu.VMEM((rank, width + feature), BF16),
-                pltpu.VMEM((sum(sizes) * ROWS, plan.cols), BF16),
-                pltpu.SemaphoreType.DMA((14,)),
-                pltpu.SemaphoreType.DMA((len(sizes) * (4 * plan.full + 2 * plan.rest + 1),)),
-            ],
-            compiler_params=params,
-            name="pack_" + part,
-        )(
-            ids1,
-            ids2,
-            popular_adapters,
-            replica_hosting,
-            first_activations,
-            second_activations,
-            down,
-            adapter_up_factors,
-            *after,
-        )
-
-    def exchange(x, n, **kwargs):
-        x = x.reshape(n, x.shape[0] // n, x.shape[1])
-        x = lax.all_to_all(x, "replica", split_axis=0, concat_axis=0, tiled=True, **kwargs)
-        return x.reshape(n * x.shape[1], x.shape[2])
-
-    if plan.split:
-        parts = ("far", "near")
-        gots = []
-        far = pack("far")
-        for m, block in enumerate(far):
-            pairs = [(i, i ^ (m + half)) for i in range(peers)]
-            gots.append(lax.ppermute(block, "replica", pairs))
-        halves = [list(range(half)), list(range(half, peers))]
-        near, _ = lax.optimization_barrier((pack("near", far[0])[0], gots[0]))
-        gots.append(exchange(near, half, axis_index_groups=halves))
-    else:
-        parts = ("all",)
-        gots = [exchange(pack("all")[0], peers)]
+    dma = pltpu.SemaphoreType.DMA
+    sources = (
+        ids1,
+        ids2,
+        popular_adapters,
+        replica_hosting,
+        first_activations,
+        second_activations,
+        down,
+        up,
+    )
+    first_scratch = [
+        pltpu.VMEM((2, 1, tok), jnp.int32),
+        pltpu.SMEM(popular_adapters.shape, jnp.int32),
+        pltpu.SMEM(replica_hosting.shape, jnp.int32),
+        pltpu.VMEM((2 * tok, width), BF16),
+    ]
     base1 = jnp.dot(first_activations, value_weight_base, preferred_element_type=F32)
     base2 = jnp.dot(second_activations, value_weight_base, preferred_element_type=F32)
-    pieces = (1 + 2 * plan.full + plan.rest) * len(gots)
-    reply = pl.pallas_call(
-        functools.partial(home_kernel, plan, parts),
-        out_shape=jax.ShapeDtypeStruct((plan.packed, plan.ret_cols), BF16),
-        in_specs=[vmem, vmem] + [anywhere] * len(gots),
-        out_specs=anywhere,
-        scratch_shapes=[
-            pltpu.VMEM((plan.packed, plan.cols), BF16),
-            pltpu.VMEM((plan.packed, plan.ret_cols), BF16),
-            pltpu.SemaphoreType.DMA((pieces,)),
-            pltpu.SemaphoreType.DMA((2,)),
-        ],
-        compiler_params=params,
-        name="home",
-    )(
-        down.reshape(plan.joined, width),
-        adapter_up_factors.reshape(plan.joined, feature),
-        *gots,
+    down_joined, up_joined = down.reshape(homed * rank, width), up.reshape(homed * rank, feature)
+
+    def shape(*dims):
+        return jax.ShapeDtypeStruct(dims, BF16)
+
+    if wide.fits:
+        half = wide.half
+        count = homed + 1
+        halves = [list(range(half)), list(range(half, wide.peers))]
+        across = [(0, 1), (1, 0)]
+        mirror = [(i, i ^ half) for i in range(wide.peers)]
+        other = lax.ppermute(popular_adapters, "groups", across)
+        both_hot = pltpu.SMEM((2,) + popular_adapters.shape, jnp.int32)
+        cuts = call(
+            functools.partial(cut_kernel, wide),
+            "cut",
+            [shape(wide.cut, wide.factor)] * count,
+            (popular_adapters, other, down, up),
+            [anywhere] * 4,
+            [vmem] * count,
+            [both_hot, dma((2,)), dma((2 * count,))],
+        )
+        crossed = [lax.ppermute(c, "replica", mirror) for c in cuts]
+        swapped = [lax.ppermute(c, "groups", across) for c in crossed[: homed - 1]]
+        sent = call(
+            functools.partial(near_pack_kernel, wide),
+            "pack",
+            shape(wide.packed, wide.cols),
+            sources,
+            [anywhere] * 8,
+            anywhere,
+            first_scratch
+            + [
+                pltpu.VMEM((wide.packed, wide.cols), BF16),
+                dma((12,)),
+                dma((4 * wide.sections + 1,)),
+                dma((2 * half,)),
+            ],
+            cost=4 * wide.packed * wide.cols,
+        )
+        got = exchange(sent, half, axis_index_groups=halves)
+        got, *arrived = lax.optimization_barrier((got, *crossed))
+        hot = call(
+            functools.partial(far_hot_kernel, wide),
+            "far_hot",
+            shape(wide.packed, wide.spread),
+            (popular_adapters, other, *arrived[:2], *swapped),
+            [anywhere] * (4 + homed - 1),
+            vmem,
+            [both_hot, dma((2,)), dma((half,))],
+        )
+        far = exchange(hot, half, axis_index_groups=halves)
+        rows = 2 * homed * rank
+        reply = call(
+            functools.partial(near_home_kernel, wide),
+            "home",
+            shape(wide.packed, wide.back_cols),
+            (got, popular_adapters, other, down_joined, up_joined, *crossed, *swapped),
+            [anywhere] * (5 + 2 * homed),
+            vmem,
+            [
+                pltpu.VMEM((wide.sections * wide.packed, width), BF16),
+                pltpu.VMEM((wide.packed, LANES), BF16),
+                pltpu.VMEM((rows, width), BF16),
+                pltpu.VMEM((rows, feature), BF16),
+                both_hot,
+                dma((2 + 2 * homed + 4 * (wide.sections + 1 + 2 * homed),)),
+                dma((2,)),
+            ],
+        )
+        answer = call(
+            functools.partial(relay_kernel, wide),
+            "relay",
+            shape(wide.packed, wide.ret_cols),
+            (got, far, reply),
+            [anywhere] * 3,
+            vmem,
+            [
+                pltpu.VMEM((2 * wide.packed, wide.spread), BF16),
+                pltpu.VMEM((wide.packed, LANES), BF16),
+                dma((4,)),
+            ],
+        )
+        back = exchange(answer, half, axis_index_groups=halves)
+        finish = functools.partial(near_final_kernel, wide)
+    else:
+        sent = call(
+            functools.partial(pack_kernel, plan),
+            "pack",
+            shape(plan.packed, plan.cols),
+            sources,
+            [anywhere] * 8,
+            anywhere,
+            first_scratch
+            + [
+                pltpu.VMEM((rank, width + feature), BF16),
+                pltpu.VMEM((plan.packed, plan.cols), BF16),
+                dma((14,)),
+                dma((4 * plan.full + 2 * plan.rest + 1,)),
+            ],
+        )
+        got = exchange(sent, plan.peers)
+        reply = call(
+            functools.partial(home_kernel, plan),
+            "home",
+            shape(plan.packed, plan.ret_cols),
+            (down_joined, up_joined, got),
+            [vmem, vmem, anywhere],
+            anywhere,
+            [
+                pltpu.VMEM((plan.packed, plan.cols), BF16),
+                pltpu.VMEM((plan.packed, plan.ret_cols), BF16),
+                dma((1 + 2 * plan.full + plan.rest,)),
+                dma((2,)),
+            ],
+        )
+        back = exchange(reply, plan.peers)
+        finish = functools.partial(final_kernel, plan)
+    out1, out2, resident_down, resident_up = call(
+        finish,
+        "finish",
+        [shape(tok, feature), shape(tok, feature), shape(1, rank, width), shape(1, rank, feature)],
+        (ids1, ids2, valid_row_counts, back, base1, base2),
+        [vmem, vmem, smem, vmem, vmem, vmem],
+        [vmem] * 4,
     )
-    out1, out2, resident_down, resident_up = pl.pallas_call(
-        functools.partial(final_kernel, plan),
-        out_shape=[
-            jax.ShapeDtypeStruct((tok, feature), BF16),
-            jax.ShapeDtypeStruct((tok, feature), BF16),
-            jax.ShapeDtypeStruct((1, rank, width), BF16),
-            jax.ShapeDtypeStruct((1, rank, feature), BF16),
-        ],
-        in_specs=[vmem, vmem, smem, vmem, vmem, vmem],
-        out_specs=[vmem] * 4,
-        compiler_params=params,
-        name="finish",
-    )(ids1, ids2, valid_row_counts, exchange(reply, peers), base1, base2)
     return out1, out2, jnp.swapaxes(resident_down, 1, 2), resident_up
 
 

time: 136 us -> 131 us (0.963)
  blocking collectives: 93.1 us -> 0 us
  waiting for transfers between devices: 15.9 us -> 64.3 us
  starting transfers between devices: 3.79 us -> 32.3 us
  Pallas kernels: 14 us -> 22.3 us
  local copies, waits for them, and re-layouts: 1.63 us -> 4.54 us
    all_to_all x1 -> x0, blocking collectives: 93.1 us -> none  [exchange(): lax.all_to_all(x, 'replica', split_axis=0, concat_axis=0, tiled=True, **k...]
    ppermute x0 -> x9, waiting for transfers between devices: none -> 51.5 us  [the longest x5 50 us: local(): crossed = [lax.ppermute(c, 'replica', mirror) for c in cuts]]
    ppermute x0 -> x9, starting transfers between devices: none -> 17.9 us  [the longest x5 9 us: local(): crossed = [lax.ppermute(c, 'replica', mirror) for c in cuts]]
    all_to_all x1 -> x3, starting transfers between devices: 3.79 us -> 14.3 us  [exchange(): lax.all_to_all(x, 'replica', split_axis=0, concat_axis=0, tiled=True, **k...]
    pallas_call x3 -> x6, Pallas kernels: 14 us -> 22.3 us  [call(): pl.pallas_call(kernel, out_shape=out_shape, in_specs=in_specs, out_specs=...]
    all_to_all x1 -> x3, waiting for transfers between devices: 15.9 us -> 12.8 us  [exchange(): lax.all_to_all(x, 'replica', split_axis=0, concat_axis=0, tiled=True, **k...]
    unnamed x11 -> x33, local copies, waits for them, and re-layouts: 1.63 us -> 4.54 us
  transfers between devices with their start and end apart: 1 -> 12, of which waited for: 1 -> 9; matrix products, arithmetic and copies ran while one was open for 4% -> 5% of each run, Pallas kernels for 0% -> 7%
where the time goes in v3:
time: 131 us; the launch traced here: 130 us
  waiting for transfers between devices  64.3 us (49%)
  starting transfers between devices  32.3 us (25%)
  Pallas kernels  22.3 us (17%)
  matrix products  5.25 us (4%)
  local copies, waits for them, and re-layouts  4.54 us (3%)
  between operations  1.44 us (1%)
    ppermute x5, waiting for transfers between devices, local(): crossed = [lax.ppermute(c, 'replica', mirror) for c in cuts]  50 us
    pallas_call x6, Pallas kernels, call(): pl.pallas_call(kernel, out_shape=out_shape, in_specs=in_specs, out_specs=...  22.3 us
    all_to_all x3, starting transfers between devices, exchange(): lax.all_to_all(x, 'replica', split_axis=0, concat_axis=0, tiled=True, **k...  14.3 us
    all_to_all x3, waiting for transfers between devices, exchange(): lax.all_to_all(x, 'replica', split_axis=0, concat_axis=0, tiled=True, **k...  12.8 us
    ppermute x5, starting transfers between devices, local(): crossed = [lax.ppermute(c, 'replica', mirror) for c in cuts]  9 us
    ppermute x3, starting transfers between devices, local(): swapped = [lax.ppermute(c, 'groups', across) for c in crossed[:homed - 1]]  6.6 us
    unnamed x33, local copies, waits for them, and re-layouts  4.54 us
    dot_general x1, matrix products, local(): jnp.dot(first_activations, value_weight_base, preferred_element_type=F32)  3.76 us
  transfers between devices with their start and end apart: 12, of which 9 were waited for; matrix products, arithmetic and copies ran while one was open for 5% of the time, Pallas kernels for 7%

profile of v3, /device:TPU:0, one launch (start us, length us, event | category | flops | bytes accessed | tf_op | source)
XLA Modules:
  0.0 130.1 jit_solution(5907796677060805692)
XLA Ops:
  1.3 4.3 %pack.1 = bf16[128,14720]{1,0:T(8,128)(2,1)} custom-call(s32[1,128]{1,0:T(1,128)} %bitcast.26, s32[1,128]{1,0:T(1,128)} %bitcast.28, s32[8]{0:T(128)} %popular.7, s32[1]{0:T(128)S(6)} %copy.15.hosting, bf16[128,4096]{1,0:T(8,128)(2,1)} %x1.1, bf16[128,4096]{1,0:T(8,128)(2,1)} %x2.1, bf16[4,64,4096]{2,1,0:T(8,128)(2,1)} %bitcast.17, bf16[4,64,512]{2,1,0:T(8,128)(2,1)} %up.3), custom_call_target="tpu_custom_call" | custom-call | bytes 7536640 | tf_op jit(solution)/shard_map/pack/pallas_call | solution.py:644
  5.6 0.0 copy-start.13
  5.6 5.2 %all-to-all-start = ((bf16[8,16,14720]{2,1,0:T(8,128)(2,1)}), bf16[8,16,14720]{2,1,0:T(8,128)(2,1)}, u32[]{:S(2)}, u32[]{:S(2)}) async-start(bf16[8,16,14720]{2,1,0:T(8,128)(2,1)} %bitcast.20), calls=%async_computation | async-start | bytes 7536640 | tf_op jit(solution)/shard_map/all_to_all | solution.py:660
  10.8 0.0 copy-done.13
  10.9 2.3 %collective-permute-start = (s32[8]{0:T(128)S(1)}, s32[8]{0:T(128)S(1)}, u32[]{:S(2)}, u32[]{:S(2)}) collective-permute-start(s32[8]{0:T(128)S(1)} %copy-done.13), channel_id=1, source_target_pairs={{0,16},{16,0},{1,17},{17,1},{2,18},{18,2},{3,19},{19,3},{4,20},{20... | collective-permute-start | bytes 104 | tf_op jit(solution)/shard_map/ppermute | solution.py:718
  13.2 1.5 %collective-permute-done.other = s32[8]{0:T(128)S(1)} collective-permute-done((s32[8]{0:T(128)S(1)}, s32[8]{0:T(128)S(1)}, u32[]{:S(2)}, u32[]{:S(2)}) %collective-permute-start) | collective-permute-done | bytes 64 | tf_op jit(solution)/shard_map/ppermute | solution.py:718
  14.7 0.5 copy-done.14
  15.2 3.3 %cut.1 = (bf16[32,4608]{1,0:T(8,128)(2,1)}, bf16[32,4608]{1,0:T(8,128)(2,1)}, bf16[32,4608]{1,0:T(8,128)(2,1)}, bf16[32,4608]{1,0:T(8,128)(2,1)}, bf16[32,4608]{1,0:T(8,128)(2,1)}) custom-call(s32[8]{0:T(128)} %popular.7, s32[8]{0:T(128)} %copy-done.14, bf16[4,64,4096]{2,1,0:T(8,128)(2,1)} %bitcast.18, bf16[4,64,512]{2,1,0:T(8,128)(2,1)} %up.3), custom_call_target="tpu_custom_call" | custom-call | tf_op jit(solution)/shard_map/cut/pallas_call | solution.py:644
  18.5 3.2 %collective-permute-start.1 = (bf16[32,4608]{1,0:T(8,128)(2,1)}, bf16[32,4608]{1,0:T(8,128)(2,1)S(1)}, u32[]{:S(2)}, u32[]{:S(2)}) collective-permute-start(bf16[32,4608]{1,0:T(8,128)(2,1)} %get-tuple-element.16), channel_id=1, source_target_pairs={{0,8},{1,9},{2,10},{3,11},{4,12},{5,13},{6,14},{7,15},{8,0},{9,1},... | collective-permute-start | bytes 884744 | tf_op jit(solution)/shard_map/ppermute | solution.py:729
  21.7 0.1 collective-permute-start.2
  21.8 2.8 %collective-permute-start.3 = (bf16[32,4608]{1,0:T(8,128)(2,1)}, bf16[32,4608]{1,0:T(8,128)(2,1)S(1)}, u32[]{:S(2)}, u32[]{:S(2)}) collective-permute-start(bf16[32,4608]{1,0:T(8,128)(2,1)} %get-tuple-element.18), channel_id=1, source_target_pairs={{0,8},{1,9},{2,10},{3,11},{4,12},{5,13},{6,14},{7,15},{8,0},{9,1},... | collective-permute-start | bytes 884744 | tf_op jit(solution)/shard_map/ppermute | solution.py:729
  24.6 0.1 collective-permute-start.4
  24.7 2.8 %collective-permute-start.5 = (bf16[32,4608]{1,0:T(8,128)(2,1)}, bf16[32,4608]{1,0:T(8,128)(2,1)S(1)}, u32[]{:S(2)}, u32[]{:S(2)}) collective-permute-start(bf16[32,4608]{1,0:T(8,128)(2,1)} %get-tuple-element.20), channel_id=1, source_target_pairs={{0,8},{1,9},{2,10},{3,11},{4,12},{5,13},{6,14},{7,15},{8,0},{9,1},... | collective-permute-start | bytes 884744 | tf_op jit(solution)/shard_map/ppermute | solution.py:729
  27.5 31.5 %collective-permute-done.1.refs_0_ = bf16[32,4608]{1,0:T(8,128)(2,1)S(1)} collective-permute-done((bf16[32,4608]{1,0:T(8,128)(2,1)}, bf16[32,4608]{1,0:T(8,128)(2,1)S(1)}, u32[]{:S(2)}, u32[]{:S(2)}) %collective-permute-start.1) | collective-permute-done | bytes 294944 | tf_op jit(solution)/shard_map/ppermute | solution.py:729
  59.0 2.2 %collective-permute-start.6 = (bf16[32,4608]{1,0:T(8,128)(2,1)S(1)}, bf16[32,4608]{1,0:T(8,128)(2,1)S(1)}, u32[]{:S(2)}, u32[]{:S(2)}) collective-permute-start(bf16[32,4608]{1,0:T(8,128)(2,1)S(1)} %collective-permute-done.1.refs_0_), channel_id=1, source_target_pairs={{0,16},{16,0},{1,17},{17,1},{2,18},{18,2},{3,19},{19,3},{4,20},{20... | collective-permute-start | bytes 884744 | tf_op jit(solution)/shard_map/ppermute | solution.py:730
  61.2 4.1 %collective-permute-done.2.refs_1_ = bf16[32,4608]{1,0:T(8,128)(2,1)S(1)} collective-permute-done((bf16[32,4608]{1,0:T(8,128)(2,1)}, bf16[32,4608]{1,0:T(8,128)(2,1)S(1)}, u32[]{:S(2)}, u32[]{:S(2)}) %collective-permute-start.2) | collective-permute-done | bytes 294944 | tf_op jit(solution)/shard_map/ppermute | solution.py:729
  65.3 2.2 %collective-permute-start.7 = (bf16[32,4608]{1,0:T(8,128)(2,1)S(1)}, bf16[32,4608]{1,0:T(8,128)(2,1)S(1)}, u32[]{:S(2)}, u32[]{:S(2)}) collective-permute-start(bf16[32,4608]{1,0:T(8,128)(2,1)S(1)} %collective-permute-done.2.refs_1_), channel_id=1, source_target_pairs={{0,16},{16,0},{1,17},{17,1},{2,18},{18,2},{3,19},{19,3},{4,20},{20... | collective-permute-start | bytes 884744 | tf_op jit(solution)/shard_map/ppermute | solution.py:730
  67.5 4.1 %collective-permute-done.3.refs_2_ = bf16[32,4608]{1,0:T(8,128)(2,1)S(1)} collective-permute-done((bf16[32,4608]{1,0:T(8,128)(2,1)}, bf16[32,4608]{1,0:T(8,128)(2,1)S(1)}, u32[]{:S(2)}, u32[]{:S(2)}) %collective-permute-start.3) | collective-permute-done | bytes 294944 | tf_op jit(solution)/shard_map/ppermute | solution.py:729
  71.7 2.2 %collective-permute-start.8 = (bf16[32,4608]{1,0:T(8,128)(2,1)S(1)}, bf16[32,4608]{1,0:T(8,128)(2,1)S(1)}, u32[]{:S(2)}, u32[]{:S(2)}) collective-permute-start(bf16[32,4608]{1,0:T(8,128)(2,1)S(1)} %collective-permute-done.3.refs_2_), channel_id=1, source_target_pairs={{0,16},{16,0},{1,17},{17,1},{2,18},{18,2},{3,19},{19,3},{4,20},{20... | collective-permute-start | bytes 884744 | tf_op jit(solution)/shard_map/ppermute | solution.py:730
  73.9 4.1 %collective-permute-done.4.refs_3_ = bf16[32,4608]{1,0:T(8,128)(2,1)S(1)} collective-permute-done((bf16[32,4608]{1,0:T(8,128)(2,1)}, bf16[32,4608]{1,0:T(8,128)(2,1)S(1)}, u32[]{:S(2)}, u32[]{:S(2)}) %collective-permute-start.4) | collective-permute-done | bytes 294944 | tf_op jit(solution)/shard_map/ppermute | solution.py:729
  78.0 6.1 %collective-permute-done.5.refs_4_ = bf16[32,4608]{1,0:T(8,128)(2,1)S(1)} collective-permute-done((bf16[32,4608]{1,0:T(8,128)(2,1)}, bf16[32,4608]{1,0:T(8,128)(2,1)S(1)}, u32[]{:S(2)}, u32[]{:S(2)}) %collective-permute-start.5) | collective-permute-done | bytes 294944 | tf_op jit(solution)/shard_map/ppermute | solution.py:729
  84.1 2.0 %all-to-all-done = bf16[8,16,14720]{2,1,0:T(8,128)(2,1)} async-done(((bf16[8,16,14720]{2,1,0:T(8,128)(2,1)}), bf16[8,16,14720]{2,1,0:T(8,128)(2,1)}, u32[]{:S(2)}, u32[]{:S(2)}) %all-to-all-start) | async-done | bytes 3768352 | tf_op jit(solution)/shard_map/all_to_all | solution.py:660
  86.2 0.0 collective-permute-done.6.refs_2_.refs_5_
  86.2 0.0 collective-permute-done.7.refs_3_.refs_6_
  86.2 0.0 copy-start.8
  86.2 0.0 collective-permute-done.8.refs_4_.refs_7_
  86.2 0.0 copy-done.5
  86.2 0.0 copy-done.6
  86.2 0.7 copy-done.7
  86.9 0.1 copy-done.8
  87.0 0.7 copy-done.9
  87.7 2.8 %far_hot.1 = bf16[128,2304]{1,0:T(8,128)(2,1)} custom-call(s32[8]{0:T(128)} %popular.7, s32[8]{0:T(128)} %copy-done.14, bf16[32,4608]{1,0:T(8,128)(2,1)} %copy-done.5, bf16[32,4608]{1,0:T(8,128)(2,1)} %copy-done.6, bf16[32,4608]{1,0:T(8,128)(2,1)} %copy-done.7, bf16[32,4608]{1,0:T(8,128)(2,1)} %copy-done.8, bf16[32,4608]{1,0:T(8,128)(2,1)} %copy-done.9), custom_call_target="tpu_custom_call" | custom-call | tf_op jit(solution)/shard_map/far_hot/pallas_call | solution.py:644
  90.6 5.4 %all-to-all-start.1 = ((bf16[8,16,2304]{2,1,0:T(8,128)(2,1)}), bf16[8,16,2304]{2,1,0:T(8,128)(2,1)S(1)}, u32[]{:S(2)}, u32[]{:S(2)}) async-start(bf16[8,16,2304]{2,1,0:T(8,128)(2,1)} %bitcast.24), calls=%async_computation.1 | async-start | bytes 1179648 | tf_op jit(solution)/shard_map/all_to_all | solution.py:660
  96.0 6.4 %home.1.reply = bf16[128,1536]{1,0:T(8,128)(2,1)} custom-call(bf16[128,14720]{1,0:T(8,128)(2,1)} %bitcast.4.got, s32[8]{0:T(128)} %popular.7, s32[8]{0:T(128)} %copy-done.14, bf16[256,4096]{1,0:T(8,128)(2,1)} %bitcast.19, bf16[256,512]{1,0:T(8,128)(2,1)} %bitcast.23, bf16[32,4608]{1,0:T(8,128)(2,1)} %copy-done.5, bf16[32,4608]{1,0:T(8,128)(2,1)} %copy-done.6, ...), custom_call_target="tpu_custom_call" | custom-call | tf_op jit(solution)/shard_map/home/pallas_call | solution.py:644
  102.4 0.0 copy-start.15
  102.4 0.0 copy-start.1
  102.5 3.0 %all-to-all-done.1 = bf16[8,16,2304]{2,1,0:T(8,128)(2,1)S(1)} async-done(((bf16[8,16,2304]{2,1,0:T(8,128)(2,1)}), bf16[8,16,2304]{2,1,0:T(8,128)(2,1)S(1)}, u32[]{:S(2)}, u32[]{:S(2)}) %all-to-all-start.1) | async-done | bytes 589856 | tf_op jit(solution)/shard_map/all_to_all | solution.py:660
  105.5 0.8 copy-done.4
  106.3 2.6 %relay.1 = bf16[128,3840]{1,0:T(8,128)(2,1)} custom-call(bf16[128,14720]{1,0:T(8,128)(2,1)} %bitcast.4.got, bf16[128,2304]{1,0:T(8,128)(2,1)} %bitcast.25, bf16[128,1536]{1,0:T(8,128)(2,1)} %home.1.reply), custom_call_target="tpu_custom_call" | custom-call | tf_op jit(solution)/shard_map/relay/pallas_call | solution.py:644
  109.0 0.0 copy-start.2
  109.0 3.7 %all-to-all-start.2 = ((bf16[8,16,3840]{2,1,0:T(8,128)(2,1)}), bf16[8,16,3840]{2,1,0:T(8,128)(2,1)S(1)}, u32[]{:S(2)}, u32[]{:S(2)}) async-start(bf16[8,16,3840]{2,1,0:T(8,128)(2,1)} %bitcast.22), calls=%async_computation.2 | async-start | bytes 1966080 | tf_op jit(solution)/shard_map/all_to_all | solution.py:660
  112.7 0.7 copy.14.counts
  113.4 3.8 %fusion.base1 = f32[128,512]{1,0:T(8,128)} fusion(bf16[128,4096]{1,0:T(8,128)(2,1)S(1)} %copy-done.1, bf16[4096,512]{1,0:T(8,128)(2,1)} %param.17), kind=kOutput, calls=%fused_computation | convolution fusion | flops 536870912 | bytes 5505024 | tf_op jit(solution)/shard_map/dot_general | solution.py:705
  117.1 0.0 copy-done.2
  117.1 1.5 %fusion.1.base2 = f32[128,512]{1,0:T(8,128)} fusion(bf16[128,4096]{1,0:T(8,128)(2,1)S(1)} %copy-done.2, bf16[4096,512]{1,0:T(8,128)(2,1)S(1)} %copy-done), kind=kOutput, calls=%fused_computation.1 | convolution fusion | flops 536870912 | bytes 5505024 | tf_op jit(solution)/shard_map/dot_general | solution.py:706
  118.6 7.7 %all-to-all-done.2 = bf16[8,16,3840]{2,1,0:T(8,128)(2,1)S(1)} async-done(((bf16[8,16,3840]{2,1,0:T(8,128)(2,1)}), bf16[8,16,3840]{2,1,0:T(8,128)(2,1)S(1)}, u32[]{:S(2)}, u32[]{:S(2)}) %all-to-all-start.2) | async-done | bytes 983072 | tf_op jit(solution)/shard_map/all_to_all | solution.py:660
  126.4 1.0 copy-done.3
  127.3 2.7 %finish.1 = (bf16[128,512]{1,0:T(8,128)(2,1)}, bf16[128,512]{1,0:T(8,128)(2,1)}, bf16[1,64,4096]{2,1,0:T(8,128)(2,1)}, bf16[1,64,512]{2,1,0:T(8,128)(2,1)}) custom-call(s32[1,128]{1,0:T(1,128)} %bitcast.27, s32[1,128]{1,0:T(1,128)} %bitcast.29, s32[2,1]{1,0:T(2,128)} %copy.14.counts, bf16[128,3840]{1,0:T(8,128)(2,1)} %bitcast.21, f32[128,512]{1,0:T(8,128)} %fusion.base1, ...), custom_call_target="tpu_custom_call" | custom-call | tf_op jit(solution)/shard_map/finish/pallas_call | solution.py:644
  (17 shorter events, 0.0 us)
Async XLA Ops:
  5.6 5.3 %copy-start.13 = (s32[8]{0:T(128)S(1)}, s32[8]{0:T(128)}, u32[]{:S(2)}) copy-start(s32[8]{0:T(128)} %popular.7) | copy-start | bytes 100
  5.6 80.5 %all-to-all-start = ((bf16[8,16,14720]{2,1,0:T(8,128)(2,1)}), bf16[8,16,14720]{2,1,0:T(8,128)(2,1)}, u32[]{:S(2)}, u32[]{:S(2)}) async-start(bf16[8,16,14720]{2,1,0:T(8,128)(2,1)} %bitcast.20), calls=%async_computation | async-start | bytes 7536640 | tf_op jit(solution)/shard_map/all_to_all | solution.py:660
  10.9 3.9 %collective-permute-start = (s32[8]{0:T(128)S(1)}, s32[8]{0:T(128)S(1)}, u32[]{:S(2)}, u32[]{:S(2)}) collective-permute-start(s32[8]{0:T(128)S(1)} %copy-done.13), channel_id=1, source_target_pairs={{0,16},{16,0},{1,17},{17,1},{2,18},{18,2},{3,19},{19,3},{4,20},{20... | collective-permute-start | bytes 104 | tf_op jit(solution)/shard_map/ppermute | solution.py:718
  14.7 0.5 copy-start.14
  18.5 40.5 %collective-permute-start.1 = (bf16[32,4608]{1,0:T(8,128)(2,1)}, bf16[32,4608]{1,0:T(8,128)(2,1)S(1)}, u32[]{:S(2)}, u32[]{:S(2)}) collective-permute-start(bf16[32,4608]{1,0:T(8,128)(2,1)} %get-tuple-element.16), channel_id=1, source_target_pairs={{0,8},{1,9},{2,10},{3,11},{4,12},{5,13},{6,14},{7,15},{8,0},{9,1},... | collective-permute-start | bytes 884744 | tf_op jit(solution)/shard_map/ppermute | solution.py:729
  21.7 43.7 %collective-permute-start.2 = (bf16[32,4608]{1,0:T(8,128)(2,1)}, bf16[32,4608]{1,0:T(8,128)(2,1)S(1)}, u32[]{:S(2)}, u32[]{:S(2)}) collective-permute-start(bf16[32,4608]{1,0:T(8,128)(2,1)} %get-tuple-element.17), channel_id=1, source_target_pairs={{0,8},{1,9},{2,10},{3,11},{4,12},{5,13},{6,14},{7,15},{8,0},{9,1},... | collective-permute-start | bytes 884744 | tf_op jit(solution)/shard_map/ppermute | solution.py:729
  21.8 49.9 %collective-permute-start.3 = (bf16[32,4608]{1,0:T(8,128)(2,1)}, bf16[32,4608]{1,0:T(8,128)(2,1)S(1)}, u32[]{:S(2)}, u32[]{:S(2)}) collective-permute-start(bf16[32,4608]{1,0:T(8,128)(2,1)} %get-tuple-element.18), channel_id=1, source_target_pairs={{0,8},{1,9},{2,10},{3,11},{4,12},{5,13},{6,14},{7,15},{8,0},{9,1},... | collective-permute-start | bytes 884744 | tf_op jit(solution)/shard_map/ppermute | solution.py:729
  24.6 53.4 %collective-permute-start.4 = (bf16[32,4608]{1,0:T(8,128)(2,1)}, bf16[32,4608]{1,0:T(8,128)(2,1)S(1)}, u32[]{:S(2)}, u32[]{:S(2)}) collective-permute-start(bf16[32,4608]{1,0:T(8,128)(2,1)} %get-tuple-element.19), channel_id=1, source_target_pairs={{0,8},{1,9},{2,10},{3,11},{4,12},{5,13},{6,14},{7,15},{8,0},{9,1},... | collective-permute-start | bytes 884744 | tf_op jit(solution)/shard_map/ppermute | solution.py:729
  24.7 59.4 %collective-permute-start.5 = (bf16[32,4608]{1,0:T(8,128)(2,1)}, bf16[32,4608]{1,0:T(8,128)(2,1)S(1)}, u32[]{:S(2)}, u32[]{:S(2)}) collective-permute-start(bf16[32,4608]{1,0:T(8,128)(2,1)} %get-tuple-element.20), channel_id=1, source_target_pairs={{0,8},{1,9},{2,10},{3,11},{4,12},{5,13},{6,14},{7,15},{8,0},{9,1},... | collective-permute-start | bytes 884744 | tf_op jit(solution)/shard_map/ppermute | solution.py:729
  59.0 27.2 %copy-start.5 = (bf16[32,4608]{1,0:T(8,128)(2,1)}, bf16[32,4608]{1,0:T(8,128)(2,1)S(1)}, u32[]{:S(2)}) copy-start(bf16[32,4608]{1,0:T(8,128)(2,1)S(1)} %collective-permute-done.1.refs_0_) | copy-start | bytes 884740
  59.0 27.1 %collective-permute-start.6 = (bf16[32,4608]{1,0:T(8,128)(2,1)S(1)}, bf16[32,4608]{1,0:T(8,128)(2,1)S(1)}, u32[]{:S(2)}, u32[]{:S(2)}) collective-permute-start(bf16[32,4608]{1,0:T(8,128)(2,1)S(1)} %collective-permute-done.1.refs_0_), channel_id=1, source_target_pairs={{0,16},{16,0},{1,17},{17,1},{2,18},{18,2},{3,19},{19,3},{4,20},{20... | collective-permute-start | bytes 884744 | tf_op jit(solution)/shard_map/ppermute | solution.py:730
  65.3 20.9 %copy-start.6 = (bf16[32,4608]{1,0:T(8,128)(2,1)}, bf16[32,4608]{1,0:T(8,128)(2,1)S(1)}, u32[]{:S(2)}) copy-start(bf16[32,4608]{1,0:T(8,128)(2,1)S(1)} %collective-permute-done.2.refs_1_) | copy-start | bytes 884740
  65.3 20.8 %collective-permute-start.7 = (bf16[32,4608]{1,0:T(8,128)(2,1)S(1)}, bf16[32,4608]{1,0:T(8,128)(2,1)S(1)}, u32[]{:S(2)}, u32[]{:S(2)}) collective-permute-start(bf16[32,4608]{1,0:T(8,128)(2,1)S(1)} %collective-permute-done.2.refs_1_), channel_id=1, source_target_pairs={{0,16},{16,0},{1,17},{17,1},{2,18},{18,2},{3,19},{19,3},{4,20},{20... | collective-permute-start | bytes 884744 | tf_op jit(solution)/shard_map/ppermute | solution.py:730
  71.7 24.3 %copy-start.10 = (bf16[32,4608]{1,0:T(8,128)(2,1)}, bf16[32,4608]{1,0:T(8,128)(2,1)S(1)}, u32[]{:S(2)}) copy-start(bf16[32,4608]{1,0:T(8,128)(2,1)S(1)} %collective-permute-done.3.refs_2_) | copy-start | bytes 884740
  71.7 14.5 %collective-permute-start.8 = (bf16[32,4608]{1,0:T(8,128)(2,1)S(1)}, bf16[32,4608]{1,0:T(8,128)(2,1)S(1)}, u32[]{:S(2)}, u32[]{:S(2)}) collective-permute-start(bf16[32,4608]{1,0:T(8,128)(2,1)S(1)} %collective-permute-done.3.refs_2_), channel_id=1, source_target_pairs={{0,16},{16,0},{1,17},{17,1},{2,18},{18,2},{3,19},{19,3},{4,20},{20... | collective-permute-start | bytes 884744 | tf_op jit(solution)/shard_map/ppermute | solution.py:730
  78.0 18.0 %copy-start.11 = (bf16[32,4608]{1,0:T(8,128)(2,1)}, bf16[32,4608]{1,0:T(8,128)(2,1)S(1)}, u32[]{:S(2)}) copy-start(bf16[32,4608]{1,0:T(8,128)(2,1)S(1)} %collective-permute-done.4.refs_3_) | copy-start | bytes 884740
  84.1 11.8 %copy-start.12 = (bf16[32,4608]{1,0:T(8,128)(2,1)}, bf16[32,4608]{1,0:T(8,128)(2,1)S(1)}, u32[]{:S(2)}) copy-start(bf16[32,4608]{1,0:T(8,128)(2,1)S(1)} %collective-permute-done.5.refs_4_) | copy-start | bytes 884740
  86.2 0.7 copy-start.7
  86.2 0.8 copy-start.8
  87.0 0.7 copy-start.9
  90.6 14.9 %all-to-all-start.1 = ((bf16[8,16,2304]{2,1,0:T(8,128)(2,1)}), bf16[8,16,2304]{2,1,0:T(8,128)(2,1)S(1)}, u32[]{:S(2)}, u32[]{:S(2)}) async-start(bf16[8,16,2304]{2,1,0:T(8,128)(2,1)} %bitcast.24), calls=%async_computation.1 | async-start | bytes 1179648 | tf_op jit(solution)/shard_map/all_to_all | solution.py:660
  102.4 10.3 %copy-start.15 = (s32[2,1]{0,1:T(1,128)S(1)}, s32[2,1]{0,1:T(1,128)}, u32[]{:S(2)}) copy-start(s32[2,1]{0,1:T(1,128)} %param.14) | copy-start | bytes 28
  102.4 10.9 %copy-start.1 = (bf16[128,4096]{1,0:T(8,128)(2,1)S(1)}, bf16[128,4096]{1,0:T(8,128)(2,1)}, u32[]{:S(2)}) copy-start(bf16[128,4096]{1,0:T(8,128)(2,1)} %x1.1) | copy-start | bytes 3145732
  105.5 0.8 copy-start.4
  109.0 8.2 %copy-start.2 = (bf16[128,4096]{1,0:T(8,128)(2,1)S(1)}, bf16[128,4096]{1,0:T(8,128)(2,1)}, u32[]{:S(2)}) copy-start(bf16[128,4096]{1,0:T(8,128)(2,1)} %x2.1) | copy-start | bytes 3145732
  109.0 17.4 %all-to-all-start.2 = ((bf16[8,16,3840]{2,1,0:T(8,128)(2,1)}), bf16[8,16,3840]{2,1,0:T(8,128)(2,1)S(1)}, u32[]{:S(2)}, u32[]{:S(2)}) async-start(bf16[8,16,3840]{2,1,0:T(8,128)(2,1)} %bitcast.22), calls=%async_computation.2 | async-start | bytes 1966080 | tf_op jit(solution)/shard_map/all_to_all | solution.py:660
  113.4 3.8 %copy-start = (bf16[4096,512]{1,0:T(8,128)(2,1)S(1)}, bf16[4096,512]{1,0:T(8,128)(2,1)}, u32[]{:S(2)}) copy-start(bf16[4096,512]{1,0:T(8,128)(2,1)} %param.17) | copy-start | bytes 12582916
  126.4 1.0 copy-start.3

commit v4 on v3

--- a/solution.py
+++ b/solution.py
@@ -327,7 +327,6 @@
             and tiles % self.half == 0
             and self.share > 0
             and col_tiles % self.share == 0
-            and self.homed > 2
             and self.cut % ROWS == 0
         )
 
@@ -339,12 +338,10 @@
         return group * ROWS, col * self.spread
 
 
-def cut_kernel(plan, popular, other, down, up, *refs):
-    outs, (hot_ids, hot_sems, sems) = refs[:-3], refs[-3:]
-    me, group = lax.axis_index("replica"), lax.axis_index("groups")
-    order = travel_order(plan, me, popular, other, hot_ids, hot_sems)
+def cut_kernel(plan, down, up, *refs):
+    outs, sems = refs[:-1], refs[-1]
     copies = []
-    for (place, part), out in zip(plan.chunks(group), outs):
+    for (adapter, part), out in zip(plan.chunks(lax.axis_index("groups")), outs):
         rows = pl.ds(pl.multiple_of(part * plan.cut, ROWS), plan.cut)
         for src, cols in (
             (down, pl.ds(0, plan.width)),
@@ -352,39 +349,13 @@
         ):
             copies.append(
                 pltpu.make_async_copy(
-                    src.at[order[place], rows], out.at[:, cols], sems.at[len(copies)]
+                    src.at[adapter, rows], out.at[:, cols], sems.at[len(copies)]
                 )
             )
     for copy in copies:
         copy.start()
     for copy in copies:
         copy.wait()
-
-
-def travel_order(plan, home, popular, other, hot_ids, sems):
-    loads = [
-        pltpu.make_async_copy(src, hot_ids.at[i], sems.at[i])
-        for i, src in enumerate((popular, other))
-    ]
-    for load in loads:
-        load.start()
-    for load in loads:
-        load.wait()
-    cold = [jnp.int32(1)] * plan.homed
-    for g in range(2):
-        for i in range(hot_ids.shape[1]):
-            for a in range(plan.homed):
-                cold[a] = jnp.where(hot_ids[g, i] == home * plan.homed + a, 0, cold[a])
-    order = [jnp.int32(0)] * plan.homed
-    for a in range(plan.homed):
-        rank = jnp.int32(0)
-        for b in range(plan.homed):
-            if b != a:
-                ahead = cold[b] <= cold[a] if b < a else cold[b] < cold[a]
-                rank = rank + jnp.where(ahead, 1, 0)
-        for c in range(plan.homed):
-            order[c] = jnp.where(rank == c, a, order[c])
-    return order
 
 
 def mirror_of(plan, me):
@@ -495,10 +466,10 @@
         store.wait()
 
 
-def near_home_kernel(plan, got, popular, other, down, up, *refs):
+def near_home_kernel(plan, got, down, up, *refs):
     count = plan.homed
     arrays, out = refs[: 2 * count], refs[2 * count]
-    x, meta, weights, ups, hot_ids, sems, hot_sems = refs[2 * count + 1 :]
+    x, meta, weights, ups, sems = refs[2 * count + 1 :]
     group = lax.axis_index("groups")
     pieces, joined = 4, plan.homed * plan.rank
     size = plan.width // pieces
@@ -509,14 +480,11 @@
         used[-1].start()
         return used[-1]
 
-    order = travel_order(
-        plan, mirror_of(plan, lax.axis_index("replica")), popular, other, hot_ids, hot_sems
-    )
     first = [load(got.at[:, pl.ds(plan.meta_at, LANES)], meta)]
     far = []
     halves = plan.chunks(group) + plan.chunks(1 - group)[: count - 1]
-    for (place, part), array in zip(halves, arrays):
-        at = joined + order[place] * plan.rank + part * plan.cut
+    for (adapter, part), array in zip(halves, arrays):
+        at = joined + adapter * plan.rank + part * plan.cut
         far.append((array, pl.ds(pl.multiple_of(at, ROWS), plan.cut)))
     steps = []
     for c in range(pieces):
@@ -556,24 +524,22 @@
         ]
 
 
-def far_hot_kernel(plan, popular, other, *refs):
-    out, hot_ids, hot_sems, sems = refs[-4:]
-    count = 2
-    crossed, swapped = refs[:count], refs[count : 2 * count]
-    mirror = mirror_of(plan, lax.axis_index("replica"))
+def far_hot_kernel(plan, popular, *refs):
+    count = plan.homed
+    arrays, (out, sems) = refs[: 2 * count], refs[2 * count :]
+    crossed, swapped = arrays[: count + 1], arrays[count + 1 :] + arrays[count : count + 1]
     group = lax.axis_index("groups")
-    order = travel_order(plan, mirror, popular, other, hot_ids, hot_sems)
-    second = hot_slot(hot_ids.at[0], plan.homed, mirror) == order[1]
-    for place in range(2):
+    slot = hot_slot(popular, plan.homed, mirror_of(plan, lax.axis_index("replica")))
+    for adapter in range(count):
         for g in range(2):
 
-            @pl.when((second if place else ~second) & (group == g))
+            @pl.when((slot == adapter) & (group == g))
             def _():
                 copies = []
                 for j in range(plan.half):
                     row, col = plan.place(j)
                     part, row = divmod(row, plan.cut)
-                    src = (crossed if part == g else swapped)[place]
+                    src = (crossed if part == g else swapped)[adapter]
                     copies.append(
                         pltpu.make_async_copy(
                             src.at[pl.ds(row, ROWS), pl.ds(col, plan.spread)],
@@ -586,29 +552,30 @@
                     copy.wait()
 
 
-def relay_kernel(plan, got, far, reply, out, held, meta, sems):
+def relay_kernel(plan, got, reply, far, out, held, meta, sems):
     copies = [
         pltpu.make_async_copy(got.at[:, pl.ds(plan.meta_at, LANES)], meta, sems.at[0]),
         pltpu.make_async_copy(
             got.at[:, pl.ds(plan.tok_cols, plan.spread)],
-            held.at[pl.ds(0, plan.packed)],
+            held,
             sems.at[1],
         ),
-        pltpu.make_async_copy(far, held.at[pl.ds(plan.packed, plan.packed)], sems.at[2]),
-        pltpu.make_async_copy(reply, out.at[:, pl.ds(0, plan.back_cols)], sems.at[3]),
+        pltpu.make_async_copy(reply, out.at[:, pl.ds(0, plan.back_cols)], sems.at[2]),
     ]
     for copy in copies:
         copy.start()
-    for copy in copies[:3]:
+    for copy in copies[:2]:
         copy.wait()
     wanted = meta[...].astype(F32).astype(jnp.int32)[:, plan.sections : plan.sections + 1]
-    shape = (plan.packed, 2 * plan.packed)
+    shape = (plan.packed, plan.packed)
     inner = lax.broadcasted_iota(jnp.int32, shape, 0) % ROWS
-    pick = as_hot(lax.broadcasted_iota(jnp.int32, shape, 1) == wanted * ROWS + inner)
-    out[:, plan.back_cols :] = jnp.dot(
-        pick, held[...], preferred_element_type=F32
-    ).astype(BF16)
-    copies[3].wait()
+    index = lax.broadcasted_iota(jnp.int32, shape, 1)
+    near = as_hot(index == wanted * ROWS + inner)
+    away = as_hot(index + plan.packed == wanted * ROWS + inner)
+    total = jnp.dot(near, held[...], preferred_element_type=F32)
+    total += jnp.dot(away, far[...], preferred_element_type=F32)
+    out[:, plan.back_cols :] = total.astype(BF16)
+    copies[2].wait()
 
 
 def near_final_kernel(plan, ids1, ids2, counts, back, base1, base2, out1, out2, down, up):
@@ -640,14 +607,14 @@
         out[...] = jnp.where(valid, total, 0.0).astype(BF16)
 
 
-def call(kernel, name, out_shape, operands, in_specs, out_specs, scratch=(), cost=0):
+def call(kernel, name, out_shape, operands, in_specs, out_specs, scratch=(), cost=0, mib=63):
     return pl.pallas_call(
         kernel,
         out_shape=out_shape,
         in_specs=in_specs,
         out_specs=out_specs,
         scratch_shapes=list(scratch),
-        compiler_params=pltpu.CompilerParams(vmem_limit_bytes=60 * 1024 * 1024),
+        compiler_params=pltpu.CompilerParams(vmem_limit_bytes=mib * 1024 * 1024),
         cost_estimate=pl.CostEstimate(flops=0, bytes_accessed=cost, transcendentals=0)
         if cost
         else None,
@@ -715,16 +682,14 @@
         halves = [list(range(half)), list(range(half, wide.peers))]
         across = [(0, 1), (1, 0)]
         mirror = [(i, i ^ half) for i in range(wide.peers)]
-        other = lax.ppermute(popular_adapters, "groups", across)
-        both_hot = pltpu.SMEM((2,) + popular_adapters.shape, jnp.int32)
         cuts = call(
             functools.partial(cut_kernel, wide),
             "cut",
             [shape(wide.cut, wide.factor)] * count,
-            (popular_adapters, other, down, up),
-            [anywhere] * 4,
+            (down, up),
+            [anywhere] * 2,
             [vmem] * count,
-            [both_hot, dma((2,)), dma((2 * count,))],
+            [dma((2 * count,))],
         )
         crossed = [lax.ppermute(c, "replica", mirror) for c in cuts]
         swapped = [lax.ppermute(c, "groups", across) for c in crossed[: homed - 1]]
@@ -750,10 +715,10 @@
             functools.partial(far_hot_kernel, wide),
             "far_hot",
             shape(wide.packed, wide.spread),
-            (popular_adapters, other, *arrived[:2], *swapped),
-            [anywhere] * (4 + homed - 1),
+            (popular_adapters, *arrived, *swapped),
+            [smem] + [anywhere] * (2 * homed),
             vmem,
-            [both_hot, dma((2,)), dma((half,))],
+            [dma((half,))],
         )
         far = exchange(hot, half, axis_index_groups=halves)
         rows = 2 * homed * rank
@@ -761,31 +726,30 @@
             functools.partial(near_home_kernel, wide),
             "home",
             shape(wide.packed, wide.back_cols),
-            (got, popular_adapters, other, down_joined, up_joined, *crossed, *swapped),
-            [anywhere] * (5 + 2 * homed),
+            (got, down_joined, up_joined, *crossed, *swapped),
+            [anywhere] * (3 + 2 * homed),
             vmem,
             [
                 pltpu.VMEM((wide.sections * wide.packed, width), BF16),
                 pltpu.VMEM((wide.packed, LANES), BF16),
                 pltpu.VMEM((rows, width), BF16),
                 pltpu.VMEM((rows, feature), BF16),
-                both_hot,
                 dma((2 + 2 * homed + 4 * (wide.sections + 1 + 2 * homed),)),
-                dma((2,)),
             ],
         )
         answer = call(
             functools.partial(relay_kernel, wide),
             "relay",
             shape(wide.packed, wide.ret_cols),
-            (got, far, reply),
-            [anywhere] * 3,
+            (got, reply, far),
+            [anywhere, anywhere, vmem],
             vmem,
             [
-                pltpu.VMEM((2 * wide.packed, wide.spread), BF16),
+                pltpu.VMEM((wide.packed, wide.spread), BF16),
                 pltpu.VMEM((wide.packed, LANES), BF16),
-                dma((4,)),
+                dma((3,)),
             ],
+            mib=24,
         )
         back = exchange(answer, half, axis_index_groups=halves)
         finish = functools.partial(near_final_kernel, wide)
@@ -829,6 +793,7 @@
         (ids1, ids2, valid_row_counts, back, base1, base2),
         [vmem, vmem, smem, vmem, vmem, vmem],
         [vmem] * 4,
+        mib=24,
     )
     return out1, out2, jnp.swapaxes(resident_down, 1, 2), resident_up
 

time: 131 us -> 129 us (0.985)
  waiting for transfers between devices: 64.3 us -> 69.9 us
  Pallas kernels: 22.3 us -> 20 us
  starting transfers between devices: 32.3 us -> 30.3 us
  local copies, waits for them, and re-layouts: 4.54 us -> 2.93 us
  matrix products: 5.25 us -> 3.82 us
    ppermute x5, waiting for transfers between devices: 50 us -> 54.8 us  [local(): crossed = [lax.ppermute(c, 'replica', mirror) for c in cuts]]
    ppermute x1 -> x0, starting transfers between devices: 2.34 us -> none  [local(): other = lax.ppermute(popular_adapters, 'groups', across)]
    all_to_all x3, waiting for transfers between devices: 12.8 us -> 15.1 us  [exchange(): lax.all_to_all(x, 'replica', split_axis=0, concat_axis=0, tiled=True, **k...]
    pallas_call x6, Pallas kernels: 22.3 us -> 20 us  [call(): pl.pallas_call(kernel, out_shape=out_shape, in_specs=in_specs, out_specs=...]
    unnamed x33 -> x25, local copies, waits for them, and re-layouts: 4.54 us -> 2.93 us
    ppermute x1 -> x0, waiting for transfers between devices: 1.52 us -> none  [local(): other = lax.ppermute(popular_adapters, 'groups', across)]
  transfers between devices with their start and end apart: 12 -> 11, of which waited for: 9 -> 8; matrix products, arithmetic and copies ran while one was open for 5% -> 3% of each run, Pallas kernels for 7% -> 7%
where the time goes in v4:
time: 129 us; the launch traced here: 128 us
  waiting for transfers between devices  69.9 us (54%)
  starting transfers between devices  30.3 us (23%)
  Pallas kernels  20 us (16%)
  matrix products  3.82 us (3%)
  local copies, waits for them, and re-layouts  2.93 us (2%)
  between operations  1.41 us (1%)
    ppermute x5, waiting for transfers between devices, local(): crossed = [lax.ppermute(c, 'replica', mirror) for c in cuts]  54.8 us
    pallas_call x6, Pallas kernels, call(): pl.pallas_call(kernel, out_shape=out_shape, in_specs=in_specs, out_specs=...  20 us
    all_to_all x3, waiting for transfers between devices, exchange(): lax.all_to_all(x, 'replica', split_axis=0, concat_axis=0, tiled=True, **k...  15.1 us
    all_to_all x3, starting transfers between devices, exchange(): lax.all_to_all(x, 'replica', split_axis=0, concat_axis=0, tiled=True, **k...  14.4 us
    ppermute x5, starting transfers between devices, local(): crossed = [lax.ppermute(c, 'replica', mirror) for c in cuts]  9.28 us
    ppermute x3, starting transfers between devices, local(): swapped = [lax.ppermute(c, 'groups', across) for c in crossed[:homed - 1]]  6.61 us
    dot_general x1, matrix products, local(): jnp.dot(first_activations, value_weight_base, preferred_element_type=F32)  3.05 us
    unnamed x25, local copies, waits for them, and re-layouts  2.93 us
  transfers between devices with their start and end apart: 11, of which 8 were waited for; matrix products, arithmetic and copies ran while one was open for 3% of the time, Pallas kernels for 7%

profile of v4, /device:TPU:0, one launch (start us, length us, event | category | flops | bytes accessed | tf_op | source)
XLA Modules:
  0.0 128.3 jit_solution(8494239610255723058)
XLA Ops:
  1.3 4.3 %pack.1 = bf16[128,14720]{1,0:T(8,128)(2,1)} custom-call(s32[1,128]{1,0:T(1,128)} %bitcast.19, s32[1,128]{1,0:T(1,128)} %bitcast.21, s32[8]{0:T(128)} %popular.3, s32[1]{0:T(128)S(6)} %copy.15.hosting, bf16[128,4096]{1,0:T(8,128)(2,1)} %x1.1, bf16[128,4096]{1,0:T(8,128)(2,1)} %x2.1, bf16[4,64,4096]{2,1,0:T(8,128)(2,1)} %bitcast.23, bf16[4,64,512]{2,1,0:T(8,128)(2,1)} %up.3), custom_call_target="tpu_custom_call" | custom-call | bytes 7536640 | tf_op jit(solution)/shard_map/pack/pallas_call | solution.py:611
  5.6 5.2 %all-to-all-start = ((bf16[8,16,14720]{2,1,0:T(8,128)(2,1)}), bf16[8,16,14720]{2,1,0:T(8,128)(2,1)}, u32[]{:S(2)}, u32[]{:S(2)}) async-start(bf16[8,16,14720]{2,1,0:T(8,128)(2,1)} %bitcast.26), calls=%async_computation | async-start | bytes 7536640 | tf_op jit(solution)/shard_map/all_to_all | solution.py:627
  10.8 2.5 %cut.1 = (bf16[32,4608]{1,0:T(8,128)(2,1)}, bf16[32,4608]{1,0:T(8,128)(2,1)}, bf16[32,4608]{1,0:T(8,128)(2,1)}, bf16[32,4608]{1,0:T(8,128)(2,1)}, bf16[32,4608]{1,0:T(8,128)(2,1)}) custom-call(bf16[4,64,4096]{2,1,0:T(8,128)(2,1)} %bitcast.24, bf16[4,64,512]{2,1,0:T(8,128)(2,1)} %up.3), custom_call_target="tpu_custom_call" | custom-call | tf_op jit(solution)/shard_map/cut/pallas_call | solution.py:611
  13.4 3.4 %collective-permute-start = (bf16[32,4608]{1,0:T(8,128)(2,1)}, bf16[32,4608]{1,0:T(8,128)(2,1)S(1)}, u32[]{:S(2)}, u32[]{:S(2)}) collective-permute-start(bf16[32,4608]{1,0:T(8,128)(2,1)} %get-tuple-element.19), channel_id=1, source_target_pairs={{0,8},{1,9},{2,10},{3,11},{4,12},{5,13},{6,14},{7,15},{8,0},{9,1},... | collective-permute-start | bytes 884744 | tf_op jit(solution)/shard_map/ppermute | solution.py:694
  16.8 0.1 collective-permute-start.1
  16.9 2.8 %collective-permute-start.2 = (bf16[32,4608]{1,0:T(8,128)(2,1)}, bf16[32,4608]{1,0:T(8,128)(2,1)S(1)}, u32[]{:S(2)}, u32[]{:S(2)}) collective-permute-start(bf16[32,4608]{1,0:T(8,128)(2,1)} %get-tuple-element.21), channel_id=1, source_target_pairs={{0,8},{1,9},{2,10},{3,11},{4,12},{5,13},{6,14},{7,15},{8,0},{9,1},... | collective-permute-start | bytes 884744 | tf_op jit(solution)/shard_map/ppermute | solution.py:694
  19.7 0.1 collective-permute-start.3
  19.8 2.8 %collective-permute-start.4 = (bf16[32,4608]{1,0:T(8,128)(2,1)}, bf16[32,4608]{1,0:T(8,128)(2,1)}, u32[]{:S(2)}, u32[]{:S(2)}) collective-permute-start(bf16[32,4608]{1,0:T(8,128)(2,1)} %get-tuple-element.23), channel_id=1, source_target_pairs={{0,8},{1,9},{2,10},{3,11},{4,12},{5,13},{6,14},{7,15},{8,0},{9,1},... | collective-permute-start | bytes 884744 | tf_op jit(solution)/shard_map/ppermute | solution.py:694
  22.6 36.3 %collective-permute-done.refs_0_ = bf16[32,4608]{1,0:T(8,128)(2,1)S(1)} collective-permute-done((bf16[32,4608]{1,0:T(8,128)(2,1)}, bf16[32,4608]{1,0:T(8,128)(2,1)S(1)}, u32[]{:S(2)}, u32[]{:S(2)}) %collective-permute-start) | collective-permute-done | bytes 294944 | tf_op jit(solution)/shard_map/ppermute | solution.py:694
  59.0 0.0 copy-start.6
  59.0 2.2 %collective-permute-start.5 = (bf16[32,4608]{1,0:T(8,128)(2,1)S(1)}, bf16[32,4608]{1,0:T(8,128)(2,1)S(1)}, u32[]{:S(2)}, u32[]{:S(2)}) collective-permute-start(bf16[32,4608]{1,0:T(8,128)(2,1)S(1)} %collective-permute-done.refs_0_), channel_id=1, source_target_pairs={{0,16},{16,0},{1,17},{17,1},{2,18},{18,2},{3,19},{19,3},{4,20},{20... | collective-permute-start | bytes 884744 | tf_op jit(solution)/shard_map/ppermute | solution.py:695
  61.2 4.1 %collective-permute-done.1.refs_1_ = bf16[32,4608]{1,0:T(8,128)(2,1)S(1)} collective-permute-done((bf16[32,4608]{1,0:T(8,128)(2,1)}, bf16[32,4608]{1,0:T(8,128)(2,1)S(1)}, u32[]{:S(2)}, u32[]{:S(2)}) %collective-permute-start.1) | collective-permute-done | bytes 294944 | tf_op jit(solution)/shard_map/ppermute | solution.py:694
  65.3 0.0 copy-start.7
  65.3 2.2 %collective-permute-start.6 = (bf16[32,4608]{1,0:T(8,128)(2,1)S(1)}, bf16[32,4608]{1,0:T(8,128)(2,1)S(1)}, u32[]{:S(2)}, u32[]{:S(2)}) collective-permute-start(bf16[32,4608]{1,0:T(8,128)(2,1)S(1)} %collective-permute-done.1.refs_1_), channel_id=1, source_target_pairs={{0,16},{16,0},{1,17},{17,1},{2,18},{18,2},{3,19},{19,3},{4,20},{20... | collective-permute-start | bytes 884744 | tf_op jit(solution)/shard_map/ppermute | solution.py:695
  67.5 4.1 %collective-permute-done.2.refs_2_ = bf16[32,4608]{1,0:T(8,128)(2,1)S(1)} collective-permute-done((bf16[32,4608]{1,0:T(8,128)(2,1)}, bf16[32,4608]{1,0:T(8,128)(2,1)S(1)}, u32[]{:S(2)}, u32[]{:S(2)}) %collective-permute-start.2) | collective-permute-done | bytes 294944 | tf_op jit(solution)/shard_map/ppermute | solution.py:694
  71.6 0.0 copy-start.8
  71.6 2.2 %collective-permute-start.7 = (bf16[32,4608]{1,0:T(8,128)(2,1)S(1)}, bf16[32,4608]{1,0:T(8,128)(2,1)}, u32[]{:S(2)}, u32[]{:S(2)}) collective-permute-start(bf16[32,4608]{1,0:T(8,128)(2,1)S(1)} %collective-permute-done.2.refs_2_), channel_id=1, source_target_pairs={{0,16},{16,0},{1,17},{17,1},{2,18},{18,2},{3,19},{19,3},{4,20},{20... | collective-permute-start | bytes 884744 | tf_op jit(solution)/shard_map/ppermute | solution.py:695
  73.8 4.1 %collective-permute-done.3.refs_3_ = bf16[32,4608]{1,0:T(8,128)(2,1)} collective-permute-done((bf16[32,4608]{1,0:T(8,128)(2,1)}, bf16[32,4608]{1,0:T(8,128)(2,1)}, u32[]{:S(2)}, u32[]{:S(2)}) %collective-permute-start.3) | collective-permute-done | bytes 294944 | tf_op jit(solution)/shard_map/ppermute | solution.py:694
  77.9 6.1 %collective-permute-done.4.refs_4_ = bf16[32,4608]{1,0:T(8,128)(2,1)} collective-permute-done((bf16[32,4608]{1,0:T(8,128)(2,1)}, bf16[32,4608]{1,0:T(8,128)(2,1)}, u32[]{:S(2)}, u32[]{:S(2)}) %collective-permute-start.4) | collective-permute-done | bytes 294944 | tf_op jit(solution)/shard_map/ppermute | solution.py:694
  84.1 2.1 %all-to-all-done = bf16[8,16,14720]{2,1,0:T(8,128)(2,1)} async-done(((bf16[8,16,14720]{2,1,0:T(8,128)(2,1)}), bf16[8,16,14720]{2,1,0:T(8,128)(2,1)}, u32[]{:S(2)}, u32[]{:S(2)}) %all-to-all-start) | async-done | bytes 3768352 | tf_op jit(solution)/shard_map/all_to_all | solution.py:627
  86.1 0.0 collective-permute-done.5.refs_5_
  86.1 0.0 collective-permute-done.6.refs_6_
  86.2 0.7 copy-done.9
  86.9 0.7 copy-done.10
  87.6 0.0 collective-permute-done.7.refs_7_
  87.6 0.0 copy-done.6
  87.6 0.0 copy-done.7
  87.6 0.0 copy-done.8
  87.6 2.8 %far_hot.1 = bf16[128,2304]{1,0:T(8,128)(2,1)} custom-call(s32[8]{0:T(128)} %popular.3, bf16[32,4608]{1,0:T(8,128)(2,1)} %copy-done.6, bf16[32,4608]{1,0:T(8,128)(2,1)} %copy-done.7, bf16[32,4608]{1,0:T(8,128)(2,1)} %copy-done.8, bf16[32,4608]{1,0:T(8,128)(2,1)} %collective-permute-done.3.refs_3_, bf16[32,4608]{1,0:T(8,128)(2,1)} %collective-permute-done.4.refs_4_, ...), custom_call_target="tpu_custom_call" | custom-call | tf_op jit(solution)/shard_map/far_hot/pallas_call | solution.py:611
  90.4 5.4 %all-to-all-start.1 = ((bf16[8,16,2304]{2,1,0:T(8,128)(2,1)}), bf16[8,16,2304]{2,1,0:T(8,128)(2,1)S(1)}, u32[]{:S(2)}, u32[]{:S(2)}) async-start(bf16[8,16,2304]{2,1,0:T(8,128)(2,1)} %bitcast.28), calls=%async_computation.1 | async-start | bytes 1179648 | tf_op jit(solution)/shard_map/all_to_all | solution.py:627
  95.8 5.8 %home.1.reply = bf16[128,1536]{1,0:T(8,128)(2,1)} custom-call(bf16[128,14720]{1,0:T(8,128)(2,1)} %bitcast.4.got, bf16[256,4096]{1,0:T(8,128)(2,1)} %bitcast.25, bf16[256,512]{1,0:T(8,128)(2,1)} %bitcast.27, bf16[32,4608]{1,0:T(8,128)(2,1)} %copy-done.6, bf16[32,4608]{1,0:T(8,128)(2,1)} %copy-done.7, bf16[32,4608]{1,0:T(8,128)(2,1)} %copy-done.8, ...), custom_call_target="tpu_custom_call" | custom-call | tf_op jit(solution)/shard_map/home/pallas_call | solution.py:611
  101.7 0.0 copy-start.11
  101.7 3.7 %all-to-all-done.1 = bf16[8,16,2304]{2,1,0:T(8,128)(2,1)S(1)} async-done(((bf16[8,16,2304]{2,1,0:T(8,128)(2,1)}), bf16[8,16,2304]{2,1,0:T(8,128)(2,1)S(1)}, u32[]{:S(2)}, u32[]{:S(2)}) %all-to-all-start.1) | async-done | bytes 589856 | tf_op jit(solution)/shard_map/all_to_all | solution.py:627
  105.4 1.0 copy-done
  106.4 2.7 %relay.1 = bf16[128,3840]{1,0:T(8,128)(2,1)} custom-call(bf16[128,14720]{1,0:T(8,128)(2,1)} %bitcast.4.got, bf16[128,1536]{1,0:T(8,128)(2,1)S(1)} %copy-done, bf16[128,2304]{1,0:T(8,128)(2,1)S(1)} %bitcast.18), custom_call_target="tpu_custom_call" | custom-call | tf_op jit(solution)/shard_map/relay/pallas_call | solution.py:611
  109.0 0.0 copy-start.5
  109.0 3.7 %all-to-all-start.2 = ((bf16[8,16,3840]{2,1,0:T(8,128)(2,1)}), bf16[8,16,3840]{2,1,0:T(8,128)(2,1)S(1)}, u32[]{:S(2)}, u32[]{:S(2)}) async-start(bf16[8,16,3840]{2,1,0:T(8,128)(2,1)} %bitcast.9), calls=%async_computation.2 | async-start | bytes 1966080 | tf_op jit(solution)/shard_map/all_to_all | solution.py:627
  112.7 0.0 copy-done.11
  112.8 0.1 copy.14.counts
  112.8 0.0 copy-done.4
  112.9 3.0 %fusion.base1 = f32[128,512]{1,0:T(8,128)S(1)} fusion(bf16[128,4096]{1,0:T(8,128)(2,1)S(1)} %copy-done.4, bf16[4096,512]{1,0:T(8,128)(2,1)} %param.17), kind=kOutput, calls=%fused_computation | convolution fusion | flops 536870912 | bytes 5505024 | tf_op jit(solution)/shard_map/dot_general | solution.py:672
  115.9 0.0 copy-done.5
  115.9 0.4 copy-done.3
  116.3 0.8 fusion.1.base2
  117.1 9.3 %all-to-all-done.2 = bf16[8,16,3840]{2,1,0:T(8,128)(2,1)S(1)} async-done(((bf16[8,16,3840]{2,1,0:T(8,128)(2,1)}), bf16[8,16,3840]{2,1,0:T(8,128)(2,1)S(1)}, u32[]{:S(2)}, u32[]{:S(2)}) %all-to-all-start.2) | async-done | bytes 983072 | tf_op jit(solution)/shard_map/all_to_all | solution.py:627
  126.4 0.0 copy-done.1
  126.4 0.0 copy-done.2
  126.4 1.9 %finish.1 = (bf16[128,512]{1,0:T(8,128)(2,1)}, bf16[128,512]{1,0:T(8,128)(2,1)}, bf16[1,64,4096]{2,1,0:T(8,128)(2,1)}, bf16[1,64,512]{2,1,0:T(8,128)(2,1)}) custom-call(s32[1,128]{1,0:T(1,128)S(1)} %bitcast.20, s32[1,128]{1,0:T(1,128)S(1)} %bitcast.22, s32[2,1]{1,0:T(2,128)S(1)} %copy.14.counts, bf16[128,3840]{1,0:T(8,128)(2,1)S(1)} %bitcast.17, ...), custom_call_target="tpu_custom_call" | custom-call | tf_op jit(solution)/shard_map/finish/pallas_call | solution.py:611
  (7 shorter events, 0.0 us)
Async XLA Ops:
  5.6 80.5 %all-to-all-start = ((bf16[8,16,14720]{2,1,0:T(8,128)(2,1)}), bf16[8,16,14720]{2,1,0:T(8,128)(2,1)}, u32[]{:S(2)}, u32[]{:S(2)}) async-start(bf16[8,16,14720]{2,1,0:T(8,128)(2,1)} %bitcast.26), calls=%async_computation | async-start | bytes 7536640 | tf_op jit(solution)/shard_map/all_to_all | solution.py:627
  13.4 45.6 %collective-permute-start = (bf16[32,4608]{1,0:T(8,128)(2,1)}, bf16[32,4608]{1,0:T(8,128)(2,1)S(1)}, u32[]{:S(2)}, u32[]{:S(2)}) collective-permute-start(bf16[32,4608]{1,0:T(8,128)(2,1)} %get-tuple-element.19), channel_id=1, source_target_pairs={{0,8},{1,9},{2,10},{3,11},{4,12},{5,13},{6,14},{7,15},{8,0},{9,1},... | collective-permute-start | bytes 884744 | tf_op jit(solution)/shard_map/ppermute | solution.py:694
  16.8 48.5 %collective-permute-start.1 = (bf16[32,4608]{1,0:T(8,128)(2,1)}, bf16[32,4608]{1,0:T(8,128)(2,1)S(1)}, u32[]{:S(2)}, u32[]{:S(2)}) collective-permute-start(bf16[32,4608]{1,0:T(8,128)(2,1)} %get-tuple-element.20), channel_id=1, source_target_pairs={{0,8},{1,9},{2,10},{3,11},{4,12},{5,13},{6,14},{7,15},{8,0},{9,1},... | collective-permute-start | bytes 884744 | tf_op jit(solution)/shard_map/ppermute | solution.py:694
  16.9 54.7 %collective-permute-start.2 = (bf16[32,4608]{1,0:T(8,128)(2,1)}, bf16[32,4608]{1,0:T(8,128)(2,1)S(1)}, u32[]{:S(2)}, u32[]{:S(2)}) collective-permute-start(bf16[32,4608]{1,0:T(8,128)(2,1)} %get-tuple-element.21), channel_id=1, source_target_pairs={{0,8},{1,9},{2,10},{3,11},{4,12},{5,13},{6,14},{7,15},{8,0},{9,1},... | collective-permute-start | bytes 884744 | tf_op jit(solution)/shard_map/ppermute | solution.py:694
  19.7 58.2 %collective-permute-start.3 = (bf16[32,4608]{1,0:T(8,128)(2,1)}, bf16[32,4608]{1,0:T(8,128)(2,1)}, u32[]{:S(2)}, u32[]{:S(2)}) collective-permute-start(bf16[32,4608]{1,0:T(8,128)(2,1)} %get-tuple-element.22), channel_id=1, source_target_pairs={{0,8},{1,9},{2,10},{3,11},{4,12},{5,13},{6,14},{7,15},{8,0},{9,1},... | collective-permute-start | bytes 884744 | tf_op jit(solution)/shard_map/ppermute | solution.py:694
  19.8 64.3 %collective-permute-start.4 = (bf16[32,4608]{1,0:T(8,128)(2,1)}, bf16[32,4608]{1,0:T(8,128)(2,1)}, u32[]{:S(2)}, u32[]{:S(2)}) collective-permute-start(bf16[32,4608]{1,0:T(8,128)(2,1)} %get-tuple-element.23), channel_id=1, source_target_pairs={{0,8},{1,9},{2,10},{3,11},{4,12},{5,13},{6,14},{7,15},{8,0},{9,1},... | collective-permute-start | bytes 884744 | tf_op jit(solution)/shard_map/ppermute | solution.py:694
  59.0 28.6 %copy-start.6 = (bf16[32,4608]{1,0:T(8,128)(2,1)}, bf16[32,4608]{1,0:T(8,128)(2,1)S(1)}, u32[]{:S(2)}) copy-start(bf16[32,4608]{1,0:T(8,128)(2,1)S(1)} %collective-permute-done.refs_0_) | copy-start | bytes 884740
  59.0 27.2 %collective-permute-start.5 = (bf16[32,4608]{1,0:T(8,128)(2,1)S(1)}, bf16[32,4608]{1,0:T(8,128)(2,1)S(1)}, u32[]{:S(2)}, u32[]{:S(2)}) collective-permute-start(bf16[32,4608]{1,0:T(8,128)(2,1)S(1)} %collective-permute-done.refs_0_), channel_id=1, source_target_pairs={{0,16},{16,0},{1,17},{17,1},{2,18},{18,2},{3,19},{19,3},{4,20},{20... | collective-permute-start | bytes 884744 | tf_op jit(solution)/shard_map/ppermute | solution.py:695
  65.3 22.3 %copy-start.7 = (bf16[32,4608]{1,0:T(8,128)(2,1)}, bf16[32,4608]{1,0:T(8,128)(2,1)S(1)}, u32[]{:S(2)}) copy-start(bf16[32,4608]{1,0:T(8,128)(2,1)S(1)} %collective-permute-done.1.refs_1_) | copy-start | bytes 884740
  65.3 20.9 %collective-permute-start.6 = (bf16[32,4608]{1,0:T(8,128)(2,1)S(1)}, bf16[32,4608]{1,0:T(8,128)(2,1)S(1)}, u32[]{:S(2)}, u32[]{:S(2)}) collective-permute-start(bf16[32,4608]{1,0:T(8,128)(2,1)S(1)} %collective-permute-done.1.refs_1_), channel_id=1, source_target_pairs={{0,16},{16,0},{1,17},{17,1},{2,18},{18,2},{3,19},{19,3},{4,20},{20... | collective-permute-start | bytes 884744 | tf_op jit(solution)/shard_map/ppermute | solution.py:695
  71.6 16.0 %copy-start.8 = (bf16[32,4608]{1,0:T(8,128)(2,1)}, bf16[32,4608]{1,0:T(8,128)(2,1)S(1)}, u32[]{:S(2)}) copy-start(bf16[32,4608]{1,0:T(8,128)(2,1)S(1)} %collective-permute-done.2.refs_2_) | copy-start | bytes 884740
  71.6 16.0 %collective-permute-start.7 = (bf16[32,4608]{1,0:T(8,128)(2,1)S(1)}, bf16[32,4608]{1,0:T(8,128)(2,1)}, u32[]{:S(2)}, u32[]{:S(2)}) collective-permute-start(bf16[32,4608]{1,0:T(8,128)(2,1)S(1)} %collective-permute-done.2.refs_2_), channel_id=1, source_target_pairs={{0,16},{16,0},{1,17},{17,1},{2,18},{18,2},{3,19},{19,3},{4,20},{20... | collective-permute-start | bytes 884744 | tf_op jit(solution)/shard_map/ppermute | solution.py:695
  86.1 0.7 copy-start.9
  86.9 0.7 copy-start.10
  90.4 15.0 %all-to-all-start.1 = ((bf16[8,16,2304]{2,1,0:T(8,128)(2,1)}), bf16[8,16,2304]{2,1,0:T(8,128)(2,1)S(1)}, u32[]{:S(2)}, u32[]{:S(2)}) async-start(bf16[8,16,2304]{2,1,0:T(8,128)(2,1)} %bitcast.28), calls=%async_computation.1 | async-start | bytes 1179648 | tf_op jit(solution)/shard_map/all_to_all | solution.py:627
  101.7 11.1 %copy-start.11 = (s32[2,1]{0,1:T(1,128)S(1)}, s32[2,1]{0,1:T(1,128)}, u32[]{:S(2)}) copy-start(s32[2,1]{0,1:T(1,128)} %param.14) | copy-start | bytes 28
  105.4 1.0 copy-start
  106.4 6.5 %copy-start.4 = (bf16[128,4096]{1,0:T(8,128)(2,1)S(1)}, bf16[128,4096]{1,0:T(8,128)(2,1)}, u32[]{:S(2)}) copy-start(bf16[128,4096]{1,0:T(8,128)(2,1)} %x1.1) | copy-start | bytes 3145732
  109.0 6.9 %copy-start.5 = (bf16[128,4096]{1,0:T(8,128)(2,1)S(1)}, bf16[128,4096]{1,0:T(8,128)(2,1)}, u32[]{:S(2)}) copy-start(bf16[128,4096]{1,0:T(8,128)(2,1)} %x2.1) | copy-start | bytes 3145732
  109.0 17.4 %all-to-all-start.2 = ((bf16[8,16,3840]{2,1,0:T(8,128)(2,1)}), bf16[8,16,3840]{2,1,0:T(8,128)(2,1)S(1)}, u32[]{:S(2)}, u32[]{:S(2)}) async-start(bf16[8,16,3840]{2,1,0:T(8,128)(2,1)} %bitcast.9), calls=%async_computation.2 | async-start | bytes 1966080 | tf_op jit(solution)/shard_map/all_to_all | solution.py:627
  112.8 3.5 %copy-start.3 = (bf16[4096,512]{1,0:T(8,128)(2,1)S(1)}, bf16[4096,512]{1,0:T(8,128)(2,1)}, u32[]{:S(2)}) copy-start(bf16[4096,512]{1,0:T(8,128)(2,1)} %param.17) | copy-start | bytes 12582916
  112.8 13.6 %copy-start.1 = (s32[128]{0:T(128)S(1)}, s32[128]{0:T(128)}, u32[]{:S(2)}) copy-start(s32[128]{0:T(128)} %param.12) | copy-start | bytes 1540
  112.9 13.6 %copy-start.2 = (s32[128]{0:T(128)S(1)}, s32[128]{0:T(128)}, u32[]{:S(2)}) copy-start(s32[128]{0:T(128)} %param.13) | copy-start | bytes 1540

commit v5 on v4

--- a/solution.py
+++ b/solution.py
@@ -427,16 +427,10 @@
     index = lax.broadcasted_iota(jnp.int32, (plan.packed, 2 * plan.tok), 0)
     own = index // ROWS == peer
     inner = index % ROWS
-    lane = lax.broadcasted_iota(jnp.int32, (plan.packed, LANES), 1)
-    meta = jnp.where(lane == plan.sections, wanted.astype(F32), 0.0)
     masks = []
     for s in range(plan.sections):
-        mark = own & (inner + s * ROWS == cell)
-        masks.append(as_hot(mark))
-        value = jnp.sum(jnp.where(mark, slots, 0.0), axis=1, keepdims=True)
-        meta = jnp.where(lane == s, value, meta)
-    mask = jnp.concatenate(masks, axis=0)
-    packed[:, plan.meta_at :] = meta.astype(BF16)
+        masks.append(own & (inner + s * ROWS == cell))
+    mask = jnp.concatenate([as_hot(m) for m in masks], axis=0)
 
     def send(at, size):
         stores.append(
@@ -458,7 +452,13 @@
             at = s * plan.width + c * quarter
             packed[:, at : at + quarter] = value[s * plan.packed : (s + 1) * plan.packed]
             send(at, quarter)
-        if c == 0:
+        if c == 2:
+            lane = lax.broadcasted_iota(jnp.int32, (plan.packed, LANES), 1)
+            meta = jnp.where(lane == plan.sections, wanted.astype(F32), 0.0)
+            for s, mark in enumerate(masks):
+                column = jnp.sum(jnp.where(mark, slots, 0.0), axis=1, keepdims=True)
+                meta = jnp.where(lane == s, column, meta)
+            packed[:, plan.meta_at :] = meta.astype(BF16)
             for load in hots:
                 load.wait()
             send(plan.tok_cols, plan.spread + LANES)
@@ -469,7 +469,7 @@
 def near_home_kernel(plan, got, down, up, *refs):
     count = plan.homed
     arrays, out = refs[: 2 * count], refs[2 * count]
-    x, meta, weights, ups, sems = refs[2 * count + 1 :]
+    x, meta, weights, ups, reply, sems = refs[2 * count + 1 :]
     group = lax.axis_index("groups")
     pieces, joined = 4, plan.homed * plan.rank
     size = plan.width // pieces
@@ -519,9 +519,10 @@
     kept = jnp.where(column == slots, total, 0.0).astype(BF16)
     delta = jnp.dot(kept, ups[...], preferred_element_type=F32).astype(BF16)
     for s in range(plan.sections):
-        out[:, s * plan.feature : (s + 1) * plan.feature] = delta[
+        reply[:, s * plan.feature : (s + 1) * plan.feature] = delta[
             s * plan.packed : (s + 1) * plan.packed
         ]
+    load(reply, out.at[:, pl.ds(0, plan.back_cols)]).wait()
 
 
 def far_hot_kernel(plan, popular, *refs):
@@ -552,7 +553,7 @@
                     copy.wait()
 
 
-def relay_kernel(plan, got, reply, far, out, held, meta, sems):
+def relay_kernel(plan, got, reply, far, out, held, meta, sent, sems):
     copies = [
         pltpu.make_async_copy(got.at[:, pl.ds(plan.meta_at, LANES)], meta, sems.at[0]),
         pltpu.make_async_copy(
@@ -560,11 +561,10 @@
             held,
             sems.at[1],
         ),
-        pltpu.make_async_copy(reply, out.at[:, pl.ds(0, plan.back_cols)], sems.at[2]),
     ]
     for copy in copies:
         copy.start()
-    for copy in copies[:2]:
+    for copy in copies:
         copy.wait()
     wanted = meta[...].astype(F32).astype(jnp.int32)[:, plan.sections : plan.sections + 1]
     shape = (plan.packed, plan.packed)
@@ -574,8 +574,10 @@
     away = as_hot(index + plan.packed == wanted * ROWS + inner)
     total = jnp.dot(near, held[...], preferred_element_type=F32)
     total += jnp.dot(away, far[...], preferred_element_type=F32)
-    out[:, plan.back_cols :] = total.astype(BF16)
-    copies[2].wait()
+    sent[...] = total.astype(BF16)
+    last = pltpu.make_async_copy(sent, out.at[:, pl.ds(plan.back_cols, plan.spread)], sems.at[2])
+    last.start()
+    last.wait()
 
 
 def near_final_kernel(plan, ids1, ids2, counts, back, base1, base2, out1, out2, down, up):
@@ -607,13 +609,14 @@
         out[...] = jnp.where(valid, total, 0.0).astype(BF16)
 
 
-def call(kernel, name, out_shape, operands, in_specs, out_specs, scratch=(), cost=0, mib=63):
+def call(kernel, name, out_shape, operands, in_specs, out_specs, scratch=(), cost=0, mib=63, aliases=None):
     return pl.pallas_call(
         kernel,
         out_shape=out_shape,
         in_specs=in_specs,
         out_specs=out_specs,
         scratch_shapes=list(scratch),
+        input_output_aliases=aliases or {},
         compiler_params=pltpu.CompilerParams(vmem_limit_bytes=mib * 1024 * 1024),
         cost_estimate=pl.CostEstimate(flops=0, bytes_accessed=cost, transcendentals=0)
         if cost
@@ -719,22 +722,24 @@
             [smem] + [anywhere] * (2 * homed),
             vmem,
             [dma((half,))],
+            mib=16,
         )
         far = exchange(hot, half, axis_index_groups=halves)
         rows = 2 * homed * rank
         reply = call(
             functools.partial(near_home_kernel, wide),
             "home",
-            shape(wide.packed, wide.back_cols),
+            shape(wide.packed, wide.ret_cols),
             (got, down_joined, up_joined, *crossed, *swapped),
             [anywhere] * (3 + 2 * homed),
-            vmem,
+            anywhere,
             [
                 pltpu.VMEM((wide.sections * wide.packed, width), BF16),
                 pltpu.VMEM((wide.packed, LANES), BF16),
                 pltpu.VMEM((rows, width), BF16),
                 pltpu.VMEM((rows, feature), BF16),
-                dma((2 + 2 * homed + 4 * (wide.sections + 1 + 2 * homed),)),
+                pltpu.VMEM((wide.packed, wide.back_cols), BF16),
+                dma((3 + 2 * homed + 4 * (wide.sections + 1 + 2 * homed),)),
             ],
         )
         answer = call(
@@ -743,13 +748,15 @@
             shape(wide.packed, wide.ret_cols),
             (got, reply, far),
             [anywhere, anywhere, vmem],
-            vmem,
+            anywhere,
             [
                 pltpu.VMEM((wide.packed, wide.spread), BF16),
                 pltpu.VMEM((wide.packed, LANES), BF16),
+                pltpu.VMEM((wide.packed, wide.spread), BF16),
                 dma((3,)),
             ],
             mib=24,
+            aliases={1: 0},
         )
         back = exchange(answer, half, axis_index_groups=halves)
         finish = functools.partial(near_final_kernel, wide)

time: 129 us -> 126 us (0.977)
  Pallas kernels: 20 us -> 17.9 us
    pallas_call x6, Pallas kernels: 20 us -> 17.9 us  [call(): pl.pallas_call(kernel, out_shape=out_shape, in_specs=in_specs, out_specs=...]
    unnamed x25 -> x35, local copies, waits for them, and re-layouts: 2.93 us -> 2.69 us
where the time goes in v5:
time: 126 us
  waiting for transfers between devices  69.9 us (55%)
  starting transfers between devices  30.1 us (24%)
  Pallas kernels  17.9 us (14%)
  matrix products  3.82 us (3%)
  local copies, waits for them, and re-layouts  2.69 us (2%)
  between operations  1.5 us (1%)
    ppermute x5, waiting for transfers between devices, local(): crossed = [lax.ppermute(c, 'replica', mirror) for c in cuts]  54.8 us
    pallas_call x6, Pallas kernels, call(): pl.pallas_call(kernel, out_shape=out_shape, in_specs=in_specs, out_specs=...  17.9 us
    all_to_all x3, waiting for transfers between devices, exchange(): lax.all_to_all(x, 'replica', split_axis=0, concat_axis=0, tiled=True, **k...  15.1 us
    all_to_all x3, starting transfers between devices, exchange(): lax.all_to_all(x, 'replica', split_axis=0, concat_axis=0, tiled=True, **k...  14.3 us
    ppermute x5, starting transfers between devices, local(): crossed = [lax.ppermute(c, 'replica', mirror) for c in cuts]  9.27 us
    ppermute x3, starting transfers between devices, local(): swapped = [lax.ppermute(c, 'groups', across) for c in crossed[:homed - 1]]  6.6 us
    dot_general x1, matrix products, local(): jnp.dot(first_activations, value_weight_base, preferred_element_type=F32)  3.05 us
    unnamed x35, local copies, waits for them, and re-layouts  2.69 us
  transfers between devices with their start and end apart: 11, of which 8 were waited for; matrix products, arithmetic and copies ran while one was open for 3% of the time, Pallas kernels for 7%

profile of v5, /device:TPU:0, one launch (start us, length us, event | category | flops | bytes accessed | tf_op | source)
XLA Modules:
  0.0 125.9 jit_solution(6001564932836012705)
XLA Ops:
  1.3 3.9 %pack.1 = bf16[128,14720]{1,0:T(8,128)(2,1)} custom-call(s32[1,128]{1,0:T(1,128)} %bitcast.20, s32[1,128]{1,0:T(1,128)} %bitcast.22, s32[8]{0:T(128)} %popular.3, s32[1]{0:T(128)S(6)} %copy.17.hosting, bf16[128,4096]{1,0:T(8,128)(2,1)} %x1.1, bf16[128,4096]{1,0:T(8,128)(2,1)} %x2.1, bf16[4,64,4096]{2,1,0:T(8,128)(2,1)} %bitcast.24, bf16[4,64,512]{2,1,0:T(8,128)(2,1)} %up.3), custom_call_target="tpu_custom_call" | custom-call | bytes 7536640 | tf_op jit(solution)/shard_map/pack/pallas_call | solution.py:613
  5.2 0.0 copy-start.10
  5.2 5.2 %all-to-all-start = ((bf16[8,16,14720]{2,1,0:T(8,128)(2,1)}), bf16[8,16,14720]{2,1,0:T(8,128)(2,1)}, u32[]{:S(2)}, u32[]{:S(2)}) async-start(bf16[8,16,14720]{2,1,0:T(8,128)(2,1)} %bitcast.27), calls=%async_computation | async-start | bytes 7536640 | tf_op jit(solution)/shard_map/all_to_all | solution.py:630
  10.5 2.6 %cut.1 = (bf16[32,4608]{1,0:T(8,128)(2,1)}, bf16[32,4608]{1,0:T(8,128)(2,1)}, bf16[32,4608]{1,0:T(8,128)(2,1)}, bf16[32,4608]{1,0:T(8,128)(2,1)}, bf16[32,4608]{1,0:T(8,128)(2,1)}) custom-call(bf16[4,64,4096]{2,1,0:T(8,128)(2,1)} %bitcast.25, bf16[4,64,512]{2,1,0:T(8,128)(2,1)} %up.3), custom_call_target="tpu_custom_call" | custom-call | tf_op jit(solution)/shard_map/cut/pallas_call | solution.py:613
  13.0 3.4 %collective-permute-start = (bf16[32,4608]{1,0:T(8,128)(2,1)}, bf16[32,4608]{1,0:T(8,128)(2,1)S(1)}, u32[]{:S(2)}, u32[]{:S(2)}) collective-permute-start(bf16[32,4608]{1,0:T(8,128)(2,1)} %get-tuple-element.19), channel_id=1, source_target_pairs={{0,8},{1,9},{2,10},{3,11},{4,12},{5,13},{6,14},{7,15},{8,0},{9,1},... | collective-permute-start | bytes 884744 | tf_op jit(solution)/shard_map/ppermute | solution.py:697
  16.5 0.1 collective-permute-start.1
  16.5 2.8 %collective-permute-start.2 = (bf16[32,4608]{1,0:T(8,128)(2,1)}, bf16[32,4608]{1,0:T(8,128)(2,1)S(1)}, u32[]{:S(2)}, u32[]{:S(2)}) collective-permute-start(bf16[32,4608]{1,0:T(8,128)(2,1)} %get-tuple-element.21), channel_id=1, source_target_pairs={{0,8},{1,9},{2,10},{3,11},{4,12},{5,13},{6,14},{7,15},{8,0},{9,1},... | collective-permute-start | bytes 884744 | tf_op jit(solution)/shard_map/ppermute | solution.py:697
  19.4 0.1 collective-permute-start.3
  19.5 2.8 %collective-permute-start.4 = (bf16[32,4608]{1,0:T(8,128)(2,1)}, bf16[32,4608]{1,0:T(8,128)(2,1)S(1)}, u32[]{:S(2)}, u32[]{:S(2)}) collective-permute-start(bf16[32,4608]{1,0:T(8,128)(2,1)} %get-tuple-element.23), channel_id=1, source_target_pairs={{0,8},{1,9},{2,10},{3,11},{4,12},{5,13},{6,14},{7,15},{8,0},{9,1},... | collective-permute-start | bytes 884744 | tf_op jit(solution)/shard_map/ppermute | solution.py:697
  22.3 36.3 %collective-permute-done.refs_0_ = bf16[32,4608]{1,0:T(8,128)(2,1)S(1)} collective-permute-done((bf16[32,4608]{1,0:T(8,128)(2,1)}, bf16[32,4608]{1,0:T(8,128)(2,1)S(1)}, u32[]{:S(2)}, u32[]{:S(2)}) %collective-permute-start) | collective-permute-done | bytes 294944 | tf_op jit(solution)/shard_map/ppermute | solution.py:697
  58.6 2.2 %collective-permute-start.5 = (bf16[32,4608]{1,0:T(8,128)(2,1)S(1)}, bf16[32,4608]{1,0:T(8,128)(2,1)S(1)}, u32[]{:S(2)}, u32[]{:S(2)}) collective-permute-start(bf16[32,4608]{1,0:T(8,128)(2,1)S(1)} %collective-permute-done.refs_0_), channel_id=1, source_target_pairs={{0,16},{16,0},{1,17},{17,1},{2,18},{18,2},{3,19},{19,3},{4,20},{20... | collective-permute-start | bytes 884744 | tf_op jit(solution)/shard_map/ppermute | solution.py:698
  60.8 4.1 %collective-permute-done.1.refs_1_ = bf16[32,4608]{1,0:T(8,128)(2,1)S(1)} collective-permute-done((bf16[32,4608]{1,0:T(8,128)(2,1)}, bf16[32,4608]{1,0:T(8,128)(2,1)S(1)}, u32[]{:S(2)}, u32[]{:S(2)}) %collective-permute-start.1) | collective-permute-done | bytes 294944 | tf_op jit(solution)/shard_map/ppermute | solution.py:697
  64.9 2.2 %collective-permute-start.6 = (bf16[32,4608]{1,0:T(8,128)(2,1)S(1)}, bf16[32,4608]{1,0:T(8,128)(2,1)S(1)}, u32[]{:S(2)}, u32[]{:S(2)}) collective-permute-start(bf16[32,4608]{1,0:T(8,128)(2,1)S(1)} %collective-permute-done.1.refs_1_), channel_id=1, source_target_pairs={{0,16},{16,0},{1,17},{17,1},{2,18},{18,2},{3,19},{19,3},{4,20},{20... | collective-permute-start | bytes 884744 | tf_op jit(solution)/shard_map/ppermute | solution.py:698
  67.1 4.1 %collective-permute-done.2.refs_2_ = bf16[32,4608]{1,0:T(8,128)(2,1)S(1)} collective-permute-done((bf16[32,4608]{1,0:T(8,128)(2,1)}, bf16[32,4608]{1,0:T(8,128)(2,1)S(1)}, u32[]{:S(2)}, u32[]{:S(2)}) %collective-permute-start.2) | collective-permute-done | bytes 294944 | tf_op jit(solution)/shard_map/ppermute | solution.py:697
  71.2 2.2 %collective-permute-start.7 = (bf16[32,4608]{1,0:T(8,128)(2,1)S(1)}, bf16[32,4608]{1,0:T(8,128)(2,1)S(1)}, u32[]{:S(2)}, u32[]{:S(2)}) collective-permute-start(bf16[32,4608]{1,0:T(8,128)(2,1)S(1)} %collective-permute-done.2.refs_2_), channel_id=1, source_target_pairs={{0,16},{16,0},{1,17},{17,1},{2,18},{18,2},{3,19},{19,3},{4,20},{20... | collective-permute-start | bytes 884744 | tf_op jit(solution)/shard_map/ppermute | solution.py:698
  73.4 4.1 %collective-permute-done.3.refs_3_ = bf16[32,4608]{1,0:T(8,128)(2,1)S(1)} collective-permute-done((bf16[32,4608]{1,0:T(8,128)(2,1)}, bf16[32,4608]{1,0:T(8,128)(2,1)S(1)}, u32[]{:S(2)}, u32[]{:S(2)}) %collective-permute-start.3) | collective-permute-done | bytes 294944 | tf_op jit(solution)/shard_map/ppermute | solution.py:697
  77.6 6.1 %collective-permute-done.4.refs_4_ = bf16[32,4608]{1,0:T(8,128)(2,1)S(1)} collective-permute-done((bf16[32,4608]{1,0:T(8,128)(2,1)}, bf16[32,4608]{1,0:T(8,128)(2,1)S(1)}, u32[]{:S(2)}, u32[]{:S(2)}) %collective-permute-start.4) | collective-permute-done | bytes 294944 | tf_op jit(solution)/shard_map/ppermute | solution.py:697
  83.7 2.1 %all-to-all-done = bf16[8,16,14720]{2,1,0:T(8,128)(2,1)} async-done(((bf16[8,16,14720]{2,1,0:T(8,128)(2,1)}), bf16[8,16,14720]{2,1,0:T(8,128)(2,1)}, u32[]{:S(2)}, u32[]{:S(2)}) %all-to-all-start) | async-done | bytes 3768352 | tf_op jit(solution)/shard_map/all_to_all | solution.py:630
  85.8 0.0 collective-permute-done.5.refs_5_
  85.8 0.0 collective-permute-done.6.refs_6_
  85.8 0.0 copy-start.8
  85.8 0.0 collective-permute-done.7.refs_7_
  85.8 0.0 copy-done.10
  85.8 0.0 copy-start.9
  85.8 1.9 %far_hot.1 = bf16[128,2304]{1,0:T(8,128)(2,1)} custom-call(s32[8]{0:T(128)S(1)} %copy-done.10, bf16[32,4608]{1,0:T(8,128)(2,1)S(1)} %collective-permute-done.refs_0_, bf16[32,4608]{1,0:T(8,128)(2,1)S(1)} %collective-permute-done.1.refs_1_, bf16[32,4608]{1,0:T(8,128)(2,1)S(1)} %collective-permute-done.2.refs_2_, ...), custom_call_target="tpu_custom_call" | custom-call | tf_op jit(solution)/shard_map/far_hot/pallas_call | solution.py:613
  87.8 0.0 copy-done.3
  87.8 0.0 copy-done.4
  87.8 5.3 %all-to-all-start.1 = ((bf16[8,16,2304]{2,1,0:T(8,128)(2,1)}), bf16[8,16,2304]{2,1,0:T(8,128)(2,1)S(1)}, u32[]{:S(2)}, u32[]{:S(2)}) async-start(bf16[8,16,2304]{2,1,0:T(8,128)(2,1)} %bitcast.7), calls=%async_computation.1 | async-start | bytes 1179648 | tf_op jit(solution)/shard_map/all_to_all | solution.py:630
  93.1 0.0 copy-done.6
  93.2 0.0 copy-done.7
  93.2 0.0 copy-done.8
  93.2 0.0 copy-done.9
  93.2 0.0 copy-done.2
  93.2 5.8 %home.1.reply = bf16[128,3840]{1,0:T(8,128)(2,1)} custom-call(bf16[128,14720]{1,0:T(8,128)(2,1)} %bitcast.4.got, bf16[256,4096]{1,0:T(8,128)(2,1)} %bitcast.26, bf16[256,512]{1,0:T(8,128)(2,1)} %bitcast.28, bf16[32,4608]{1,0:T(8,128)(2,1)} %copy-done.2, bf16[32,4608]{1,0:T(8,128)(2,1)} %copy-done.3, bf16[32,4608]{1,0:T(8,128)(2,1)} %copy-done.4, ...), custom_call_target="tpu_custom_call" | custom-call | tf_op jit(solution)/shard_map/home/pallas_call | solution.py:613
  99.0 0.0 copy-start.16
  99.0 3.7 %all-to-all-done.1 = bf16[8,16,2304]{2,1,0:T(8,128)(2,1)S(1)} async-done(((bf16[8,16,2304]{2,1,0:T(8,128)(2,1)}), bf16[8,16,2304]{2,1,0:T(8,128)(2,1)S(1)}, u32[]{:S(2)}, u32[]{:S(2)}) %all-to-all-start.1) | async-done | bytes 589856 | tf_op jit(solution)/shard_map/all_to_all | solution.py:630
  102.7 1.2 copy-done
  103.9 1.8 %relay.1 = bf16[128,3840]{1,0:T(8,128)(2,1)S(1)} custom-call(bf16[128,14720]{1,0:T(8,128)(2,1)} %bitcast.4.got, bf16[128,3840]{1,0:T(8,128)(2,1)S(1)} %copy-done, bf16[128,2304]{1,0:T(8,128)(2,1)S(1)} %bitcast.19), custom_call_target="tpu_custom_call", output_to_operand_aliasing={{}: (1, {})} | custom-call | tf_op jit(solution)/shard_map/relay/pallas_call | solution.py:613
  105.7 1.0 copy-done.1
  106.6 3.7 %all-to-all-start.2 = ((bf16[8,16,3840]{2,1,0:T(8,128)(2,1)}), bf16[8,16,3840]{2,1,0:T(8,128)(2,1)S(1)}, u32[]{:S(2)}, u32[]{:S(2)}) async-start(bf16[8,16,3840]{2,1,0:T(8,128)(2,1)} %bitcast.17), calls=%async_computation.2 | async-start | bytes 1966080 | tf_op jit(solution)/shard_map/all_to_all | solution.py:630
  110.3 0.0 copy-done.16
  110.3 0.1 copy.15.counts
  110.4 3.1 %fusion.base1 = f32[128,512]{1,0:T(8,128)S(1)} fusion(bf16[128,4096]{1,0:T(8,128)(2,1)S(1)} %copy-done.14, bf16[4096,512]{1,0:T(8,128)(2,1)} %param.17), kind=kOutput, calls=%fused_computation | convolution fusion | flops 536870912 | bytes 5505024 | tf_op jit(solution)/shard_map/dot_general | solution.py:675
  113.5 0.4 copy-done.13
  113.9 0.8 fusion.1.base2
  114.7 9.3 %all-to-all-done.2 = bf16[8,16,3840]{2,1,0:T(8,128)(2,1)S(1)} async-done(((bf16[8,16,3840]{2,1,0:T(8,128)(2,1)}), bf16[8,16,3840]{2,1,0:T(8,128)(2,1)S(1)}, u32[]{:S(2)}, u32[]{:S(2)}) %all-to-all-start.2) | async-done | bytes 983072 | tf_op jit(solution)/shard_map/all_to_all | solution.py:630
  124.0 0.0 copy-done.11
  124.0 1.9 %finish.1 = (bf16[128,512]{1,0:T(8,128)(2,1)}, bf16[128,512]{1,0:T(8,128)(2,1)}, bf16[1,64,4096]{2,1,0:T(8,128)(2,1)}, bf16[1,64,512]{2,1,0:T(8,128)(2,1)}) custom-call(s32[1,128]{1,0:T(1,128)S(1)} %bitcast.21, s32[1,128]{1,0:T(1,128)S(1)} %bitcast.23, s32[2,1]{1,0:T(2,128)S(1)} %copy.15.counts, bf16[128,3840]{1,0:T(8,128)(2,1)S(1)} %bitcast.18, ...), custom_call_target="tpu_custom_call" | custom-call | tf_op jit(solution)/shard_map/finish/pallas_call | solution.py:613
  (17 shorter events, 0.0 us)
Async XLA Ops:
  5.2 80.6 %copy-start.10 = (s32[8]{0:T(128)S(1)}, s32[8]{0:T(128)}, u32[]{:S(2)}) copy-start(s32[8]{0:T(128)} %popular.3) | copy-start | bytes 100
  5.2 80.5 %all-to-all-start = ((bf16[8,16,14720]{2,1,0:T(8,128)(2,1)}), bf16[8,16,14720]{2,1,0:T(8,128)(2,1)}, u32[]{:S(2)}, u32[]{:S(2)}) async-start(bf16[8,16,14720]{2,1,0:T(8,128)(2,1)} %bitcast.27), calls=%async_computation | async-start | bytes 7536640 | tf_op jit(solution)/shard_map/all_to_all | solution.py:630
  13.0 45.6 %collective-permute-start = (bf16[32,4608]{1,0:T(8,128)(2,1)}, bf16[32,4608]{1,0:T(8,128)(2,1)S(1)}, u32[]{:S(2)}, u32[]{:S(2)}) collective-permute-start(bf16[32,4608]{1,0:T(8,128)(2,1)} %get-tuple-element.19), channel_id=1, source_target_pairs={{0,8},{1,9},{2,10},{3,11},{4,12},{5,13},{6,14},{7,15},{8,0},{9,1},... | collective-permute-start | bytes 884744 | tf_op jit(solution)/shard_map/ppermute | solution.py:697
  16.5 48.5 %collective-permute-start.1 = (bf16[32,4608]{1,0:T(8,128)(2,1)}, bf16[32,4608]{1,0:T(8,128)(2,1)S(1)}, u32[]{:S(2)}, u32[]{:S(2)}) collective-permute-start(bf16[32,4608]{1,0:T(8,128)(2,1)} %get-tuple-element.20), channel_id=1, source_target_pairs={{0,8},{1,9},{2,10},{3,11},{4,12},{5,13},{6,14},{7,15},{8,0},{9,1},... | collective-permute-start | bytes 884744 | tf_op jit(solution)/shard_map/ppermute | solution.py:697
  16.5 54.7 %collective-permute-start.2 = (bf16[32,4608]{1,0:T(8,128)(2,1)}, bf16[32,4608]{1,0:T(8,128)(2,1)S(1)}, u32[]{:S(2)}, u32[]{:S(2)}) collective-permute-start(bf16[32,4608]{1,0:T(8,128)(2,1)} %get-tuple-element.21), channel_id=1, source_target_pairs={{0,8},{1,9},{2,10},{3,11},{4,12},{5,13},{6,14},{7,15},{8,0},{9,1},... | collective-permute-start | bytes 884744 | tf_op jit(solution)/shard_map/ppermute | solution.py:697
  19.4 58.2 %collective-permute-start.3 = (bf16[32,4608]{1,0:T(8,128)(2,1)}, bf16[32,4608]{1,0:T(8,128)(2,1)S(1)}, u32[]{:S(2)}, u32[]{:S(2)}) collective-permute-start(bf16[32,4608]{1,0:T(8,128)(2,1)} %get-tuple-element.22), channel_id=1, source_target_pairs={{0,8},{1,9},{2,10},{3,11},{4,12},{5,13},{6,14},{7,15},{8,0},{9,1},... | collective-permute-start | bytes 884744 | tf_op jit(solution)/shard_map/ppermute | solution.py:697
  19.5 64.2 %collective-permute-start.4 = (bf16[32,4608]{1,0:T(8,128)(2,1)}, bf16[32,4608]{1,0:T(8,128)(2,1)S(1)}, u32[]{:S(2)}, u32[]{:S(2)}) collective-permute-start(bf16[32,4608]{1,0:T(8,128)(2,1)} %get-tuple-element.23), channel_id=1, source_target_pairs={{0,8},{1,9},{2,10},{3,11},{4,12},{5,13},{6,14},{7,15},{8,0},{9,1},... | collective-permute-start | bytes 884744 | tf_op jit(solution)/shard_map/ppermute | solution.py:697
  58.6 34.6 %copy-start.2 = (bf16[32,4608]{1,0:T(8,128)(2,1)}, bf16[32,4608]{1,0:T(8,128)(2,1)S(1)}, u32[]{:S(2)}) copy-start(bf16[32,4608]{1,0:T(8,128)(2,1)S(1)} %collective-permute-done.refs_0_) | copy-start | bytes 884740
  58.6 27.2 %collective-permute-start.5 = (bf16[32,4608]{1,0:T(8,128)(2,1)S(1)}, bf16[32,4608]{1,0:T(8,128)(2,1)S(1)}, u32[]{:S(2)}, u32[]{:S(2)}) collective-permute-start(bf16[32,4608]{1,0:T(8,128)(2,1)S(1)} %collective-permute-done.refs_0_), channel_id=1, source_target_pairs={{0,16},{16,0},{1,17},{17,1},{2,18},{18,2},{3,19},{19,3},{4,20},{20... | collective-permute-start | bytes 884744 | tf_op jit(solution)/shard_map/ppermute | solution.py:698
  64.9 22.9 %copy-start.3 = (bf16[32,4608]{1,0:T(8,128)(2,1)}, bf16[32,4608]{1,0:T(8,128)(2,1)S(1)}, u32[]{:S(2)}) copy-start(bf16[32,4608]{1,0:T(8,128)(2,1)S(1)} %collective-permute-done.1.refs_1_) | copy-start | bytes 884740
  64.9 20.9 %collective-permute-start.6 = (bf16[32,4608]{1,0:T(8,128)(2,1)S(1)}, bf16[32,4608]{1,0:T(8,128)(2,1)S(1)}, u32[]{:S(2)}, u32[]{:S(2)}) collective-permute-start(bf16[32,4608]{1,0:T(8,128)(2,1)S(1)} %collective-permute-done.1.refs_1_), channel_id=1, source_target_pairs={{0,16},{16,0},{1,17},{17,1},{2,18},{18,2},{3,19},{19,3},{4,20},{20... | collective-permute-start | bytes 884744 | tf_op jit(solution)/shard_map/ppermute | solution.py:698
  71.2 16.5 %copy-start.4 = (bf16[32,4608]{1,0:T(8,128)(2,1)}, bf16[32,4608]{1,0:T(8,128)(2,1)S(1)}, u32[]{:S(2)}) copy-start(bf16[32,4608]{1,0:T(8,128)(2,1)S(1)} %collective-permute-done.2.refs_2_) | copy-start | bytes 884740
  71.2 14.6 %collective-permute-start.7 = (bf16[32,4608]{1,0:T(8,128)(2,1)S(1)}, bf16[32,4608]{1,0:T(8,128)(2,1)S(1)}, u32[]{:S(2)}, u32[]{:S(2)}) collective-permute-start(bf16[32,4608]{1,0:T(8,128)(2,1)S(1)} %collective-permute-done.2.refs_2_), channel_id=1, source_target_pairs={{0,16},{16,0},{1,17},{17,1},{2,18},{18,2},{3,19},{19,3},{4,20},{20... | collective-permute-start | bytes 884744 | tf_op jit(solution)/shard_map/ppermute | solution.py:698
  77.6 15.6 %copy-start.5 = (bf16[32,4608]{1,0:T(8,128)(2,1)}, bf16[32,4608]{1,0:T(8,128)(2,1)S(1)}, u32[]{:S(2)}) copy-start(bf16[32,4608]{1,0:T(8,128)(2,1)S(1)} %collective-permute-done.3.refs_3_) | copy-start | bytes 884740
  83.7 9.5 %copy-start.6 = (bf16[32,4608]{1,0:T(8,128)(2,1)}, bf16[32,4608]{1,0:T(8,128)(2,1)S(1)}, u32[]{:S(2)}) copy-start(bf16[32,4608]{1,0:T(8,128)(2,1)S(1)} %collective-permute-done.4.refs_4_) | copy-start | bytes 884740
  85.8 7.4 %copy-start.7 = (bf16[32,4608]{1,0:T(8,128)(2,1)}, bf16[32,4608]{1,0:T(8,128)(2,1)S(1)}, u32[]{:S(2)}) copy-start(bf16[32,4608]{1,0:T(8,128)(2,1)S(1)} %collective-permute-done.5.refs_5_) | copy-start | bytes 884740
  85.8 7.4 %copy-start.8 = (bf16[32,4608]{1,0:T(8,128)(2,1)}, bf16[32,4608]{1,0:T(8,128)(2,1)S(1)}, u32[]{:S(2)}) copy-start(bf16[32,4608]{1,0:T(8,128)(2,1)S(1)} %collective-permute-done.6.refs_6_) | copy-start | bytes 884740
  85.8 7.4 %copy-start.9 = (bf16[32,4608]{1,0:T(8,128)(2,1)}, bf16[32,4608]{1,0:T(8,128)(2,1)S(1)}, u32[]{:S(2)}) copy-start(bf16[32,4608]{1,0:T(8,128)(2,1)S(1)} %collective-permute-done.7.refs_7_) | copy-start | bytes 884740
  87.8 14.9 %all-to-all-start.1 = ((bf16[8,16,2304]{2,1,0:T(8,128)(2,1)}), bf16[8,16,2304]{2,1,0:T(8,128)(2,1)S(1)}, u32[]{:S(2)}, u32[]{:S(2)}) async-start(bf16[8,16,2304]{2,1,0:T(8,128)(2,1)} %bitcast.7), calls=%async_computation.1 | async-start | bytes 1179648 | tf_op jit(solution)/shard_map/all_to_all | solution.py:630
  99.0 11.3 %copy-start.16 = (s32[2,1]{0,1:T(1,128)S(1)}, s32[2,1]{0,1:T(1,128)}, u32[]{:S(2)}) copy-start(s32[2,1]{0,1:T(1,128)} %param.14) | copy-start | bytes 28
  102.7 1.2 copy-start
  103.9 6.5 %copy-start.14 = (bf16[128,4096]{1,0:T(8,128)(2,1)S(1)}, bf16[128,4096]{1,0:T(8,128)(2,1)}, u32[]{:S(2)}) copy-start(bf16[128,4096]{1,0:T(8,128)(2,1)} %x1.1) | copy-start | bytes 3145732
  105.7 1.0 copy-start.1
  106.6 6.9 %copy-start.15 = (bf16[128,4096]{1,0:T(8,128)(2,1)S(1)}, bf16[128,4096]{1,0:T(8,128)(2,1)}, u32[]{:S(2)}) copy-start(bf16[128,4096]{1,0:T(8,128)(2,1)} %x2.1) | copy-start | bytes 3145732
  106.6 17.4 %all-to-all-start.2 = ((bf16[8,16,3840]{2,1,0:T(8,128)(2,1)}), bf16[8,16,3840]{2,1,0:T(8,128)(2,1)S(1)}, u32[]{:S(2)}, u32[]{:S(2)}) async-start(bf16[8,16,3840]{2,1,0:T(8,128)(2,1)} %bitcast.17), calls=%async_computation.2 | async-start | bytes 1966080 | tf_op jit(solution)/shard_map/all_to_all | solution.py:630
  110.4 3.5 %copy-start.13 = (bf16[4096,512]{1,0:T(8,128)(2,1)S(1)}, bf16[4096,512]{1,0:T(8,128)(2,1)}, u32[]{:S(2)}) copy-start(bf16[4096,512]{1,0:T(8,128)(2,1)} %param.17) | copy-start | bytes 12582916
  110.4 13.6 %copy-start.11 = (s32[128]{0:T(128)S(1)}, s32[128]{0:T(128)}, u32[]{:S(2)}) copy-start(s32[128]{0:T(128)} %param.12) | copy-start | bytes 1540
  110.4 13.6 %copy-start.12 = (s32[128]{0:T(128)S(1)}, s32[128]{0:T(128)}, u32[]{:S(2)}) copy-start(s32[128]{0:T(128)} %param.13) | copy-start | bytes 1540
